TPU v7x, 32 devices: a whole 2x2x4 slice. The times are simulated.
32 devices in a mesh: pipe: 4 (over y, x), dp: 8 (over z, core).
Axes of the slice: x: 2, y: 2, z: 4, core: 2. Of those that a mesh axis runs over, the one named last changes fastest.
Arguments:
- activations: bfloat16 [4, 8, 134, 384], P('pipe', 'dp'), may hold values from -8 to 8
- cotangent: bfloat16 [4, 8, 134, 384], P('pipe', 'dp'), may hold values from -6 to 6
- att_qkv: bfloat16 [2, 384, 1152], replicated, may hold values from -0.3125 to 0.3125
- att_dw: bfloat16 [2, 25, 1152], replicated, may hold values from -1.25 to 1.25
- att_group: bfloat16 [2, 36, 32, 32], replicated, may hold values from -1 to 1
- att_proj: bfloat16 [2, 768, 384], replicated, may hold values from -0.21875 to 0.21875
- mb_inv: bfloat16 [2, 384, 1536], replicated, may hold values from -0.3125 to 0.3125
- mb_inv_bias: bfloat16 [2, 1536], replicated, may hold values from -2 to 2
- mb_dw: bfloat16 [2, 9, 1536], replicated, may hold values from -2 to 2
- mb_dw_bias: bfloat16 [2, 1536], replicated, may hold values from -2 to 2
- mb_point: bfloat16 [2, 1536, 384], replicated, may hold values from -0.15625 to 0.15625
- bn_gain: bfloat16 [4, 384], replicated, may hold values from 0.5 to 1.5
- bn_bias: bfloat16 [4, 384], replicated, may hold values from -2 to 2
Outputs:
- outputs: bfloat16 [4, 8, 134, 384], P('pipe', 'dp')
- input_grad: bfloat16 [4, 8, 134, 384], P('pipe', 'dp')
- grad_att_qkv: float32 [2, 384, 1152], P(None, 'pipe', 'dp')
- grad_att_dw: float32 [2, 25, 1152], replicated
- grad_att_group: float32 [2, 36, 32, 32], replicated
- grad_att_proj: float32 [2, 768, 384], P(None, 'dp', 'pipe')
- grad_mb_inv: float32 [2, 384, 1536], P(None, 'pipe', 'dp')
- grad_mb_inv_bias: float32 [2, 1536], replicated
- grad_mb_dw: float32 [2, 9, 1536], replicated
- grad_mb_dw_bias: float32 [2, 1536], replicated
- grad_mb_point: float32 [2, 1536, 384], P(None, 'dp', 'pipe')
- grad_bn_gain: float32 [4, 384], replicated
- grad_bn_bias: float32 [4, 384], replicated
All inputs are finite; a program needn't handle non-finite values.
Results may differ from a plain program's by a relative error of at most 0.02.
Values may be sent and summed in bfloat16 or wider, within the bound.
A program may use at most 320 MiB of HBM per device.

v0:
```python
import jax
import jax.numpy as jnp
from jax import lax
from jax.sharding import PartitionSpec as P

HIGH = lax.Precision.HIGHEST
EPS = 1e-05


def passed_along(value, axis, steps):
    count = lax.axis_size(axis)
    first, last = (max(0, -steps), min(count, count - steps))
    return lax.ppermute(value, axis, [(source, source + steps) for source in range(first, last)])


def depthwise(tokens, kernel, reach):
    images = tokens.shape[0]
    channels = tokens.shape[-1]
    kernel_grid = kernel.reshape(reach, reach, 1, channels)
    results = []
    for crop_count, crop_side, offset in ((2, 7, 0), (4, 3, 98)):
        crop_tokens = crop_count * crop_side * crop_side
        crop_cells = tokens[:, offset : offset + crop_tokens].reshape(
            images * crop_count, crop_side, crop_side, channels
        )
        summed = lax.conv_general_dilated(
            crop_cells,
            kernel_grid,
            (1, 1),
            "SAME",
            dimension_numbers=("NHWC", "HWIO", "NHWC"),
            feature_group_count=channels,
            precision=HIGH,
        )
        results.append(summed.reshape(images, crop_tokens, channels))
    return jnp.concatenate(results, axis=1)


def crop_attention(queries, keys, values):
    kv_state = jnp.einsum("...lhi,...lhj->...hij", keys, values, precision=HIGH)
    key_total = jnp.sum(keys, axis=-3)
    numerator = jnp.einsum("...lhi,...hij->...lhj", queries, kv_state, precision=HIGH)
    denominator = jnp.einsum("...lhi,...hi->...lh", queries, key_total, precision=HIGH)
    return numerator / denominator[..., None]


def attention_mix(joined, conv_kernel, group_weight):
    images = joined.shape[0]
    tokens_img = joined.shape[1]
    triple = joined.shape[2]
    head_size = group_weight.shape[-1]
    groups = group_weight.shape[0]
    spread = depthwise(joined, conv_kernel, 5)
    spread = jnp.einsum(
        "abgi,gio->abgo",
        spread.reshape(images, tokens_img, groups, head_size),
        group_weight,
        precision=HIGH,
    )
    heads = triple // (3 * head_size)
    scales = jnp.concatenate(
        [
            joined.reshape(images, tokens_img, heads, 3 * head_size),
            spread.reshape(images, tokens_img, heads, 3 * head_size),
        ],
        axis=2,
    )
    queries = jax.nn.softplus(scales[..., :head_size])
    keys = jax.nn.softplus(scales[..., head_size : 2 * head_size])
    values = scales[..., 2 * head_size :]
    outputs_crop = []
    for crop_count, crop_side, offset in ((2, 7, 0), (4, 3, 98)):
        crop_tokens = crop_count * crop_side * crop_side

        def by_crop(array_in):
            return array_in[:, offset : offset + crop_tokens].reshape(
                images, crop_count, crop_side * crop_side, 2 * heads, head_size
            )

        attended = crop_attention(by_crop(queries), by_crop(keys), by_crop(values))
        outputs_crop.append(attended.reshape(images, crop_tokens, 2 * heads * head_size))
    return jnp.concatenate(outputs_crop, axis=1)


def mb_mix(pre_act, conv_kernel, conv_bias):
    spread = depthwise(jax.nn.silu(pre_act), conv_kernel, 3) + conv_bias
    return jax.nn.silu(spread)


def put_slot(buffer, new_value, slot_id):
    return lax.dynamic_update_index_in_dim(buffer, new_value, slot_id, 0)


def take_slot(buffer, slot_id):
    return lax.dynamic_index_in_dim(buffer, slot_id, 0, keepdims=False)


def widen(matrix, wanted):
    return jnp.pad(matrix, ((0, 0), (0, wanted - matrix.shape[1])))


def body(
    activations,
    cotangent,
    att_qkv,
    att_dw,
    att_group,
    att_proj,
    mb_inv,
    mb_inv_bias,
    mb_dw,
    mb_dw_bias,
    mb_point,
    bn_gain,
    bn_bias,
):
    segment_index = lax.axis_index("pipe")
    segments = lax.axis_size("pipe")
    layer_index = segment_index // 2
    is_attention = segment_index % 2 == 0
    inputs_all, grads_all = (
        lax.all_gather(activations, "pipe", axis=0, tiled=True),
        lax.all_gather(cotangent, "pipe", axis=0, tiled=True),
    )
    micro_count = inputs_all.shape[0]
    images = activations.shape[1]
    tokens_img = activations.shape[2]
    features = activations.shape[3]
    row_count = images * tokens_img
    total_rows = row_count * lax.axis_size("dp")
    inputs_all = inputs_all.reshape(micro_count, row_count, features)
    grads_all = grads_all.reshape(micro_count, row_count, features)
    w_qkv = take_slot(att_qkv, layer_index)
    conv_att = take_slot(att_dw, layer_index).astype(jnp.float32)
    group_w = take_slot(att_group, layer_index).astype(jnp.float32)
    w_proj = take_slot(att_proj, layer_index)
    w_inv = take_slot(mb_inv, layer_index)
    bias_inv = take_slot(mb_inv_bias, layer_index).astype(jnp.float32)
    conv_mb = take_slot(mb_dw, layer_index).astype(jnp.float32)
    bias_mb = take_slot(mb_dw_bias, layer_index).astype(jnp.float32)
    w_point = take_slot(mb_point, layer_index)
    segment_gain = take_slot(bn_gain, segment_index).astype(jnp.float32)
    segment_bias = take_slot(bn_bias, segment_index).astype(jnp.float32)
    expanded = w_inv.shape[1]
    wide = max(3 * features, expanded)

    def mix_rows(joined_in, kernel_in, group_in):
        return attention_mix(
            joined_in.reshape(images, tokens_img, -1), kernel_in, group_in
        ).reshape(row_count, -1)

    def expand_rows(pre_in, kernel_in, bias_in):
        return mb_mix(pre_in.reshape(images, tokens_img, -1), kernel_in, bias_in).reshape(
            row_count, -1
        )

    def attention_branch(hidden):
        joined = jnp.dot(hidden, w_qkv, preferred_element_type=jnp.float32).astype(jnp.bfloat16)
        mixed = mix_rows(joined.astype(jnp.float32), conv_att, group_w)
        return jnp.dot(mixed.astype(jnp.bfloat16), w_proj, preferred_element_type=jnp.float32)

    def expand_branch(hidden):
        pre_act = jnp.dot(hidden, w_inv, preferred_element_type=jnp.float32) + bias_inv
        mixed = expand_rows(pre_act, conv_mb, bias_mb)
        return jnp.dot(mixed.astype(jnp.bfloat16), w_point, preferred_element_type=jnp.float32)

    att_small_zero = (jnp.zeros(conv_att.shape, jnp.float32), jnp.zeros(group_w.shape, jnp.float32))
    mb_small_zero = (jnp.zeros(conv_mb.shape, jnp.float32), jnp.zeros(bias_mb.shape, jnp.float32))

    def attention_back(hidden, grad_branch):
        joined = jnp.dot(hidden, w_qkv, preferred_element_type=jnp.float32).astype(jnp.bfloat16)
        mixed, pullback = jax.vjp(mix_rows, joined.astype(jnp.float32), conv_att, group_w)
        mixed_low = mixed.astype(jnp.bfloat16)
        grad_mixed = jnp.dot(grad_branch, w_proj.T, preferred_element_type=jnp.float32).astype(
            jnp.bfloat16
        )
        grad_joined, grad_kernel, grad_group = pullback(grad_mixed.astype(jnp.float32))
        grad_joined = grad_joined.astype(jnp.bfloat16)
        grad_hidden = jnp.dot(grad_joined, w_qkv.T, preferred_element_type=jnp.float32)
        return (
            grad_hidden,
            widen(grad_joined, wide),
            widen(mixed_low, wide),
            (grad_kernel, grad_group),
            mb_small_zero,
        )

    def expand_back(hidden, grad_branch):
        pre_act = jnp.dot(hidden, w_inv, preferred_element_type=jnp.float32) + bias_inv
        mixed, pullback = jax.vjp(expand_rows, pre_act, conv_mb, bias_mb)
        mixed_low = mixed.astype(jnp.bfloat16)
        grad_mixed = jnp.dot(grad_branch, w_point.T, preferred_element_type=jnp.float32).astype(
            jnp.bfloat16
        )
        grad_pre, grad_kernel, grad_kbias = pullback(grad_mixed.astype(jnp.float32))
        grad_pre = grad_pre.astype(jnp.bfloat16)
        grad_hidden = jnp.dot(grad_pre, w_inv.T, preferred_element_type=jnp.float32)
        return (
            grad_hidden,
            widen(grad_pre, wide),
            widen(mixed_low, wide),
            att_small_zero,
            (grad_kernel, grad_kbias),
        )

    zero_rows = jnp.zeros((row_count, features), jnp.bfloat16)
    slots = micro_count + 1
    kept_in = jnp.zeros((slots, row_count, features), jnp.bfloat16)
    kept_branch = jnp.zeros((slots, row_count, features), jnp.float32)
    kept_mean = jnp.zeros((slots, features), jnp.float32)
    kept_scale = jnp.zeros((slots, features), jnp.float32)
    results = jnp.zeros((slots, row_count, features), jnp.float32)
    steps_all = micro_count + segments - 1
    received = zero_rows
    for clock_step in range(steps_all):
        batch_id = clock_step - segment_index
        is_valid = (batch_id >= 0) & (batch_id < micro_count)
        slot_id = jnp.clip(batch_id, 0, micro_count - 1)
        store_id = jnp.where(is_valid, slot_id, micro_count)
        fresh_rows = take_slot(inputs_all, slot_id)
        hidden = jnp.where(segment_index == 0, jnp.where(is_valid, fresh_rows, zero_rows), received)
        branch = lax.cond(is_attention, attention_branch, expand_branch, hidden)
        col_sums, squares = lax.psum(
            (jnp.sum(branch, axis=0), jnp.sum(branch * branch, axis=0)), "dp"
        )
        col_mean = col_sums / total_rows
        inv_std = lax.rsqrt(squares / total_rows - col_mean * col_mean + EPS)
        normed = (branch - col_mean) * inv_std
        output_low = (hidden.astype(jnp.float32) + segment_gain * normed + segment_bias).astype(
            jnp.bfloat16
        )
        kept_in = put_slot(kept_in, hidden, store_id)
        kept_branch = put_slot(kept_branch, branch, store_id)
        kept_mean = put_slot(kept_mean, col_mean, store_id)
        kept_scale = put_slot(kept_scale, inv_std, store_id)
        results = put_slot(
            results,
            output_low.astype(jnp.float32),
            jnp.where(segment_index == segments - 1, store_id, micro_count),
        )
        if clock_step + 1 < steps_all:
            received = passed_along(output_low, "pipe", 1)
    att_small = att_small_zero
    mb_small = mb_small_zero
    kept_mid = jnp.zeros((slots, row_count, wide), jnp.bfloat16)
    kept_act = jnp.zeros((slots, row_count, wide), jnp.bfloat16)
    kept_grad = jnp.zeros((slots, row_count, features), jnp.bfloat16)
    gain_acc = jnp.zeros((features,), jnp.float32)
    shift_acc = jnp.zeros((features,), jnp.float32)
    inputs_grad = jnp.zeros((slots, row_count, features), jnp.float32)
    received_grad = zero_rows
    for clock_step in range(steps_all):
        batch_id = clock_step - (segments - 1 - segment_index)
        is_valid = (batch_id >= 0) & (batch_id < micro_count)
        slot_id = jnp.clip(batch_id, 0, micro_count - 1)
        store_id = jnp.where(is_valid, slot_id, micro_count)
        fresh_grad = take_slot(grads_all, slot_id)
        upstream = jnp.where(
            segment_index == segments - 1, jnp.where(is_valid, fresh_grad, zero_rows), received_grad
        ).astype(jnp.float32)
        hidden = take_slot(kept_in, slot_id)
        branch = take_slot(kept_branch, slot_id)
        inv_std = take_slot(kept_scale, slot_id)
        normed = (branch - take_slot(kept_mean, slot_id)) * inv_std
        grad_normed = upstream * segment_gain
        sum_grad, sum_cross = lax.psum(
            (jnp.sum(grad_normed, axis=0), jnp.sum(grad_normed * normed, axis=0)), "dp"
        )
        grad_branch = (
            inv_std * (grad_normed - sum_grad / total_rows - normed * (sum_cross / total_rows))
        ).astype(jnp.bfloat16)
        valid_scale = is_valid.astype(jnp.float32)
        gain_acc = gain_acc + valid_scale * jnp.sum(upstream * normed, axis=0)
        shift_acc = shift_acc + valid_scale * jnp.sum(upstream, axis=0)
        grad_hidden, mid_low, act_low, att_part, mb_part = lax.cond(
            is_attention, attention_back, expand_back, hidden, grad_branch
        )
        att_small = jax.tree.map(
            lambda total, term: total + valid_scale * term, att_small, att_part
        )
        mb_small = jax.tree.map(lambda total, term: total + valid_scale * term, mb_small, mb_part)
        kept_mid = put_slot(kept_mid, mid_low, store_id)
        kept_act = put_slot(kept_act, act_low, store_id)
        kept_grad = put_slot(kept_grad, grad_branch, store_id)
        grad_out = (upstream + grad_hidden).astype(jnp.bfloat16)
        inputs_grad = put_slot(
            inputs_grad,
            grad_out.astype(jnp.float32),
            jnp.where(segment_index == 0, store_id, micro_count),
        )
        if clock_step + 1 < steps_all:
            received_grad = passed_along(grad_out, "pipe", -1)
    rows_all = micro_count * row_count
    hidden_all = kept_in[:micro_count].reshape(rows_all, features)
    mid_all = kept_mid[:micro_count].reshape(rows_all, wide)
    act_all = kept_act[:micro_count].reshape(rows_all, wide)
    grad_all = kept_grad[:micro_count].reshape(rows_all, features)

    def attention_weights(unused):
        grad_qkv_local = jnp.dot(
            hidden_all.T, mid_all[:, : 3 * features], preferred_element_type=jnp.float32
        )
        grad_proj_local = jnp.dot(
            act_all[:, : 2 * features].T, grad_all, preferred_element_type=jnp.float32
        )
        return (
            grad_qkv_local,
            grad_proj_local,
            jnp.zeros(w_inv.shape, jnp.float32),
            jnp.zeros(bias_inv.shape, jnp.float32),
            jnp.zeros(w_point.shape, jnp.float32),
        )

    def expand_weights(unused):
        grad_inv_local = jnp.dot(hidden_all.T, mid_all, preferred_element_type=jnp.float32)
        grad_ibias_local = jnp.sum(mid_all.astype(jnp.float32), axis=0)
        grad_point_local = jnp.dot(act_all.T, grad_all, preferred_element_type=jnp.float32)
        return (
            jnp.zeros(w_qkv.shape, jnp.float32),
            jnp.zeros(w_proj.shape, jnp.float32),
            grad_inv_local,
            grad_ibias_local,
            grad_point_local,
        )

    qkv_sum, proj_sum, inv_sum, ibias_sum, point_sum = lax.cond(
        is_attention, attention_weights, expand_weights, 0
    )
    att_acc = (qkv_sum, proj_sum, att_small[0], att_small[1])
    mb_acc = (inv_sum, ibias_sum, mb_small[0], mb_small[1], point_sum)
    results = results[:micro_count]
    inputs_grad = inputs_grad[:micro_count]

    def by_layer(grad_in):
        return jnp.stack([grad_in * (layer_index == 0), grad_in * (layer_index == 1)])

    segment_rows = (lax.iota(jnp.int32, 4) == segment_index)[:, None]
    big_grads = (
        by_layer(att_acc[0]),
        by_layer(att_acc[1]),
        by_layer(mb_acc[0]),
        by_layer(mb_acc[4]),
    )
    partial_grads = (
        lax.psum_scatter(big_grads[0], "dp", scatter_dimension=2, tiled=True),
        lax.psum_scatter(big_grads[1], "dp", scatter_dimension=1, tiled=True),
        lax.psum_scatter(big_grads[2], "dp", scatter_dimension=2, tiled=True),
        lax.psum_scatter(big_grads[3], "dp", scatter_dimension=1, tiled=True),
    )
    grad_qkv, grad_proj, grad_inv, grad_point = (
        lax.psum_scatter(
            partial_grads[0].astype(jnp.bfloat16), "pipe", scatter_dimension=1, tiled=True
        ).astype(jnp.float32),
        lax.psum_scatter(
            partial_grads[1].astype(jnp.bfloat16), "pipe", scatter_dimension=2, tiled=True
        ).astype(jnp.float32),
        lax.psum_scatter(
            partial_grads[2].astype(jnp.bfloat16), "pipe", scatter_dimension=1, tiled=True
        ).astype(jnp.float32),
        lax.psum_scatter(
            partial_grads[3].astype(jnp.bfloat16), "pipe", scatter_dimension=2, tiled=True
        ).astype(jnp.float32),
    )
    grad_dw, grad_group, grad_ibias, grad_mbdw, grad_kbias, grad_gain, grad_shift = lax.psum(
        (
            by_layer(att_acc[2]),
            by_layer(att_acc[3]),
            by_layer(mb_acc[1]),
            by_layer(mb_acc[2]),
            by_layer(mb_acc[3]),
            segment_rows * gain_acc,
            segment_rows * shift_acc,
        ),
        ("pipe", "dp"),
    )
    result_sum, input_sum = (
        lax.psum_scatter(
            results.astype(jnp.bfloat16), "pipe", scatter_dimension=0, tiled=True
        ).astype(jnp.float32),
        lax.psum_scatter(
            inputs_grad.astype(jnp.bfloat16), "pipe", scatter_dimension=0, tiled=True
        ).astype(jnp.float32),
    )
    result_low = result_sum.astype(jnp.bfloat16)
    input_low = input_sum.astype(jnp.bfloat16)
    return (
        result_low.reshape(activations.shape),
        input_low.reshape(activations.shape),
        grad_qkv,
        grad_dw,
        grad_group,
        grad_proj,
        grad_inv,
        grad_ibias,
        grad_mbdw,
        grad_kbias,
        grad_point,
        grad_gain,
        grad_shift,
    )


def solution(mesh):
    placed = (
        P("pipe", "dp", None, None),
        P("pipe", "dp", None, None),
        P(),
        P(),
        P(),
        P(),
        P(),
        P(),
        P(),
        P(),
        P(),
        P(),
        P(),
    )
    return jax.shard_map(
        body,
        mesh=mesh,
        in_specs=placed,
        out_specs=(
            P("pipe", "dp", None, None),
            P("pipe", "dp", None, None),
            P(None, "pipe", "dp"),
            P(),
            P(),
            P(None, "dp", "pipe"),
            P(None, "pipe", "dp"),
            P(),
            P(),
            P(),
            P(None, "dp", "pipe"),
            P(),
            P(),
        ),
        check_vma=False,
    )
```

profile of v0, /device:TPU:0, one launch (start us, length us, event | category | flops | bytes accessed | tf_op | source)
XLA Modules:
  0.0 2719.2 jit_solution(6163495918217364256)
XLA Ops:
  14.1 11.8 all_gather.6
  32.8 80.1 %conditional.15 = (f32[134,384]{1,0:T(8,128)}) conditional(s32[]{:T(128)} %convert_element_type.640, (bf16[134,384]{1,0:T(8,128)(2,1)}, bf16[384,1536]{1,0:T(8,128)(2,1)S(1)}, f32[1536]{0:T(1024)S(1)}, f32[9,1536]{1,0:T(8,128)S(1)}, f32[1536]{0:T(1024)S(1)}, /*index=5*/bf16[1536,384]{1,0:T(8,128)(2,1)}) %tuple.552, (bf16[134,384]{1,0:T(8,128)(2,1)}, ...), branch_computations={%region_0.1_spmd, %region_1.4_spmd} | conditional | flops 367438848 | bytes 32861012 | solution.py:222
  113.9 14.9 all-reduce.122
  136.9 80.4 %conditional.16 = (f32[134,384]{1,0:T(8,128)}) conditional(s32[]{:T(128)} %convert_element_type.640, (bf16[134,384]{1,0:T(8,128)(2,1)}, bf16[384,1536]{1,0:T(8,128)(2,1)S(1)}, f32[1536]{0:T(1024)S(1)}, f32[9,1536]{1,0:T(8,128)S(1)}, f32[1536]{0:T(1024)S(1)}, /*index=5*/bf16[1536,384]{1,0:T(8,128)(2,1)}) %tuple.553, (bf16[134,384]{1,0:T(8,128)(2,1)}, ...), branch_computations={%region_8.9_spmd, %region_9.12_spmd} | conditional | flops 367438848 | bytes 32861012 | solution.py:222
  218.3 13.6 all-reduce.121
  239.5 80.4 %conditional.17 = (f32[134,384]{1,0:T(8,128)}) conditional(s32[]{:T(128)} %convert_element_type.640, (bf16[134,384]{1,0:T(8,128)(2,1)}, bf16[384,1536]{1,0:T(8,128)(2,1)S(1)}, f32[1536]{0:T(1024)S(1)}, f32[9,1536]{1,0:T(8,128)S(1)}, f32[1536]{0:T(1024)S(1)}, /*index=5*/bf16[1536,384]{1,0:T(8,128)(2,1)}) %tuple.554, (bf16[134,384]{1,0:T(8,128)(2,1)}, ...), branch_computations={%region_16.17_spmd, %region_17.20_spmd} | conditional | flops 367438848 | bytes 32861012 | solution.py:222
  320.8 13.6 all-reduce.120
  342.0 80.3 %conditional.18 = (f32[134,384]{1,0:T(8,128)}) conditional(s32[]{:T(128)} %convert_element_type.640, (bf16[134,384]{1,0:T(8,128)(2,1)}, bf16[384,1536]{1,0:T(8,128)(2,1)S(1)}, f32[1536]{0:T(1024)S(1)}, f32[9,1536]{1,0:T(8,128)S(1)}, f32[1536]{0:T(1024)S(1)}, /*index=5*/bf16[1536,384]{1,0:T(8,128)(2,1)}) %tuple.555, (bf16[134,384]{1,0:T(8,128)(2,1)}, ...), branch_computations={%region_24.25_spmd, %region_25.28_spmd} | conditional | flops 367438848 | bytes 32861012 | solution.py:222
  423.2 13.6 all-reduce.119
  444.4 80.2 %conditional.19 = (f32[134,384]{1,0:T(8,128)}) conditional(s32[]{:T(128)} %convert_element_type.640, (bf16[134,384]{1,0:T(8,128)(2,1)}, bf16[384,1536]{1,0:T(8,128)(2,1)S(1)}, f32[1536]{0:T(1024)S(1)}, f32[9,1536]{1,0:T(8,128)S(1)}, f32[1536]{0:T(1024)S(1)}, /*index=5*/bf16[1536,384]{1,0:T(8,128)(2,1)}) %tuple.556, (bf16[134,384]{1,0:T(8,128)(2,1)}, ...), branch_computations={%region_32.33_spmd, %region_33.36_spmd} | conditional | flops 367438848 | bytes 32861012 | solution.py:222
  525.6 13.6 all-reduce.118
  546.8 80.2 %conditional.20 = (f32[134,384]{1,0:T(8,128)}) conditional(s32[]{:T(128)} %convert_element_type.640, (bf16[134,384]{1,0:T(8,128)(2,1)}, bf16[384,1536]{1,0:T(8,128)(2,1)S(1)}, f32[1536]{0:T(1024)S(1)}, f32[9,1536]{1,0:T(8,128)S(1)}, f32[1536]{0:T(1024)S(1)}, /*index=5*/bf16[1536,384]{1,0:T(8,128)(2,1)}) %tuple.557, (bf16[134,384]{1,0:T(8,128)(2,1)}, ...), branch_computations={%region_40.41_spmd, %region_41.44_spmd} | conditional | flops 367438848 | bytes 32861012 | solution.py:222
  628.0 13.6 all-reduce.117
  648.0 31.3 %all_gather.7 = bf16[4,1,134,384]{3,2,1,0:T(8,128)(2,1)} all-gather(bf16[1,1,134,384]{3,2,1,0:T(8,128)(2,1)} %param.45), channel_id=1, replica_groups=mesh['pipe'=4,'dp'=8] {'pipe'}, dimensions={0}, use_global_device_ids=true | all-gather | bytes 514560 | tf_op jit(solution)/shard_map/all_gather | solution.py:123
  686.8 80.1 %conditional.21 = (f32[134,384]{1,0:T(8,128)}) conditional(s32[]{:T(128)} %convert_element_type.640, (bf16[134,384]{1,0:T(8,128)(2,1)}, bf16[384,1536]{1,0:T(8,128)(2,1)S(1)}, f32[1536]{0:T(1024)S(1)}, f32[9,1536]{1,0:T(8,128)S(1)}, f32[1536]{0:T(1024)S(1)}, /*index=5*/bf16[1536,384]{1,0:T(8,128)(2,1)}) %tuple.558, (bf16[134,384]{1,0:T(8,128)(2,1)}, ...), branch_computations={%region_48.49_spmd, %region_49.52_spmd} | conditional | flops 367438848 | bytes 32861012 | solution.py:222
  767.9 13.6 all-reduce.116
  788.5 13.6 all-reduce.115
  805.9 212.9 %conditional.22 = (f32[134,384]{1,0:T(8,128)S(1)}, f32[25,1152]{1,0:T(8,128)}, f32[9,1536]{1,0:T(8,128)}, f32[1536]{0:T(1024)S(1)}, bf16[1,134,1536]{2,1,0:T(8,1...) conditional(s32[]{:T(128)} %convert_element_type.640, (bf16[134,384]{1,0:T(8,128)(2,1)}, ...), branch_computations={%region_61.63_spmd, %region_63.69_spmd} | conditional | flops 823366592 | bytes 108069320 | solution.py:275
  871.2 5.9 compare_select_fusion.19
  929.3 4.1 fusion.429
  946.4 4.3 fusion.419
  996.8 7.2 fusion.433
  1031.7 13.6 all-reduce.114
  1047.0 200.8 %conditional.23 = (f32[134,384]{1,0:T(8,128)S(1)}, f32[25,1152]{1,0:T(8,128)}, f32[9,1536]{1,0:T(8,128)}, f32[1536]{0:T(1024)S(1)}, bf16[1,134,1536]{2,1,0:T(8,1...) conditional(s32[]{:T(128)} %convert_element_type.640, (bf16[134,384]{1,0:T(8,128)(2,1)}, ...), branch_computations={%region_72.75_spmd, %region_74.80_spmd} | conditional | flops 823366592 | bytes 109715936 | solution.py:275
  1100.2 5.7 compare_select_fusion.25
  1175.5 4.3 fusion.477
  1225.6 7.2 fusion.491
  1258.4 13.6 all-reduce.113
  1273.7 200.5 %conditional.24 = (f32[134,384]{1,0:T(8,128)S(1)}, f32[25,1152]{1,0:T(8,128)}, f32[9,1536]{1,0:T(8,128)}, f32[1536]{0:T(1024)S(1)}, bf16[1,134,1536]{2,1,0:T(8,1...) conditional(s32[]{:T(128)} %convert_element_type.640, (bf16[134,384]{1,0:T(8,128)(2,1)}, ...), branch_computations={%region_83.86_spmd, %region_85.91_spmd} | conditional | flops 823366592 | bytes 109715936 | solution.py:275
  1326.7 5.8 compare_select_fusion.31
  1401.9 4.3 fusion.535
  1452.3 7.2 fusion.549
  1484.9 13.6 all-reduce.112
  1500.2 200.8 %conditional.25 = (f32[134,384]{1,0:T(8,128)S(1)}, f32[25,1152]{1,0:T(8,128)}, f32[9,1536]{1,0:T(8,128)}, f32[1536]{0:T(1024)S(1)}, bf16[1,134,1536]{2,1,0:T(8,1...) conditional(s32[]{:T(128)} %convert_element_type.640, (bf16[134,384]{1,0:T(8,128)(2,1)}, ...), branch_computations={%region_94.97_spmd, %region_96.102_spmd} | conditional | flops 823366592 | bytes 109715936 | solution.py:275
  1553.5 5.7 compare_select_fusion.37
  1611.2 4.1 fusion.603
  1628.6 4.3 fusion.593
  1678.7 7.2 fusion.607
  1711.6 13.6 all-reduce.111
  1726.9 200.4 %conditional.26 = (f32[134,384]{1,0:T(8,128)S(1)}, f32[25,1152]{1,0:T(8,128)}, f32[9,1536]{1,0:T(8,128)}, f32[1536]{0:T(1024)S(1)}, bf16[1,134,1536]{2,1,0:T(8,1...) conditional(s32[]{:T(128)} %convert_element_type.640, (bf16[134,384]{1,0:T(8,128)(2,1)}, ...), branch_computations={%region_105.108_spmd, %region_107.113_spmd} | conditional | flops 823366592 | bytes 109715936 | solution.py:275
  1779.9 5.8 compare_select_fusion.43
  1855.1 4.3 fusion.651
  1905.3 7.2 fusion.665
  1937.9 13.6 all-reduce.110
  1953.3 200.6 %conditional.27 = (f32[134,384]{1,0:T(8,128)S(1)}, f32[25,1152]{1,0:T(8,128)}, f32[9,1536]{1,0:T(8,128)}, f32[1536]{0:T(1024)S(1)}, bf16[1,134,1536]{2,1,0:T(8,1...) conditional(s32[]{:T(128)} %convert_element_type.640, (bf16[134,384]{1,0:T(8,128)(2,1)}, ...), branch_computations={%region_116.119_spmd, %region_118.124_spmd} | conditional | flops 823366592 | bytes 109715936 | solution.py:275
  2006.5 5.7 compare_select_fusion.49
  2081.6 4.3 fusion.709
  2131.7 7.2 fusion.723
  2163.8 13.6 all-reduce.109
  2182.8 139.3 %conditional.28 = (f32[134,384]{1,0:T(8,128)}, f32[25,1152]{1,0:T(8,128)}, f32[9,1536]{1,0:T(8,128)}, f32[1536]{0:T(1024)S(1)}, bf16[1,134,1536]{2,1,0:T(8,128)(...) conditional(s32[]{:T(128)} %convert_element_type.640, (bf16[134,384]{1,0:T(8,128)(2,1)}, ...), branch_computations={%region_127.130_spmd, %region_129.135_spmd} | conditional | flops 823366592 | bytes 111098320 | solution.py:275
  2214.2 5.1 compare_select_fusion.55
  2279.0 4.3 fusion.767
  2311.7 5.3 fusion.781
  2333.3 5.8 conditional.29
  2358.9 8.2 copy.3558
  2367.1 4.8 copy.3694
  2382.1 49.4 %reduce-scatter.23.cloned.1.call-done = f32[2,384,144]{1,2,0:T(8,128)} async-done(((f32[2,384,1152]{1,2,0:T(8,128)}), f32[2,384,144]{1,2,0:T(8,128)}) %reduce-scatter.23.cloned.1.call-update) | async-done | bytes 442384 | tf_op jit(solution)/shard_map/reduce_scatter | solution.py:345
  2434.3 53.5 %reduce-scatter.29.cloned.1.call-done = f32[2,192,384]{2,1,0:T(8,128)} async-done(((f32[2,1536,384]{2,1,0:T(8,128)}), f32[2,192,384]{2,1,0:T(8,128)}) %reduce-scatter.29.cloned.1.call-update) | async-done | bytes 589840 | tf_op jit(solution)/shard_map/reduce_scatter | solution.py:348
  2490.7 56.7 %reduce-scatter.35.cloned.1.call-done = f32[192,768]{1,0:T(8,128)} async-done(((f32[1536,768]{1,0:T(8,128)}), f32[192,768]{1,0:T(8,128)}) %reduce-scatter.35.cloned.1.call-update) | async-done | bytes 589840
  2555.1 38.9 %all-reduce.107 = (f32[2,1536]{1,0:T(2,128)}, f32[2,1536]{1,0:T(2,128)}, f32[4,384]{1,0:T(4,128)}, f32[4,384]{1,0:T(4,128)}) all-reduce(f32[2,1536]{1,0:T(2,128)S(1)} %pad_maximum_fusion.21, f32[2,1536]{1,0:T(2,128)S(1)} %pad_maximum_fusion.22, ...), channel_id=1, replica_groups=mesh['pipe'=4,'dp'=8] {'pipe','dp'}, use_global_device_ids=true, to_apply=%region_146.148 | all-reduce | flops 9216 | bytes 73728 | tf_op jit(solution)/shard_map/psum | solution.py:364
  2604.0 23.8 reduce-scatter.37.cloned.1.call-done
  2632.7 22.6 reduce-scatter.27.cloned.1.call-done
  2656.8 26.3 reduce-scatter.39.cloned.1.call-done
  2683.1 27.5 %reduce-scatter.41.cloned.1.call-done = bf16[1,134,384]{2,1,0:T(8,128)(2,1)} async-done(((bf16[4,134,384]{2,1,0:T(8,128)(2,1)}), bf16[1,134,384]{2,1,0:T(8,128)(2,1)}) %reduce-scatter.41.cloned.1.call-update) | async-done | bytes 102928
  (2039 shorter events, 2006.7 us)
Async XLA Ops:
  8.0 19.9 copy-start
  8.0 2372.0 %reduce-scatter.25.cloned.1.call-start = ((), (), s32[]{:S(2)}) async-start(), calls=%async_computation.11 | async-start | bytes 2654208 | tf_op jit(solution)/shard_map/reduce_scatter | solution.py:346
  13.2 14.7 copy-start.294
  131.6 3.9 collective-permute-start
  233.7 4.1 collective-permute-start.1
  336.3 4.0 collective-permute-start.2
  438.7 4.1 collective-permute-start.3
  541.1 4.0 collective-permute-start.4
  627.0 52.3 %copy-start.399 = (f32[384]{0:T(512)S(1)}, f32[384]{0:T(512)}, u32[]{:S(2)}) copy-start(f32[384]{0:T(512)} %copy-done.398) | copy-start | bytes 4612
  627.0 53.6 %copy-start.403 = (f32[384]{0:T(512)S(1)}, f32[384]{0:T(512)}, u32[]{:S(2)}) copy-start(f32[384]{0:T(512)} %copy-done.402) | copy-start | bytes 4612
  627.0 53.6 %copy-start.401 = (f32[384]{0:T(512)S(1)}, f32[384]{0:T(512)}, u32[]{:S(2)}) copy-start(f32[384]{0:T(512)} %copy-done.400) | copy-start | bytes 4612
  643.4 41.7 %collective-permute-start.5 = (bf16[134,384]{1,0:T(8,128)(2,1)}, bf16[134,384]{1,0:T(8,128)(2,1)}, u32[]{:S(2)}, u32[]{:S(2)}) collective-permute-start(bf16[134,384]{1,0:T(8,128)(2,1)} %get-tuple-element.1291), channel_id=1, source_target_pairs={{0,8},{8,16},{16,24},{1,9},{9,17},{17,25},{2,10},{10,18},{18,26},{... | collective-permute-start | bytes 308744 | tf_op jit(solution)/shard_map/ppermute | solution.py:13
  994.9 9.1 copy-start.281
  994.9 9.1 copy-start.334
  996.8 9.5 copy-start.309
  1020.6 8.7 collective-permute-start.6
  1223.6 9.1 copy-start.282
  1223.6 9.1 copy-start.335
  1225.6 9.5 copy-start.310
  1247.8 25.9 copy-start.423
  1249.4 6.6 collective-permute-start.7
  1450.3 9.1 copy-start.283
  1450.3 9.1 copy-start.336
  1452.3 9.5 copy-start.311
  1474.3 25.9 copy-start.425
  1474.3 8.2 copy-start.390
  1475.9 6.6 collective-permute-start.8
  1676.7 9.1 copy-start.284
  1676.7 9.1 copy-start.337
  1678.7 9.5 copy-start.312
  1701.0 25.9 copy-start.427
  1701.0 8.2 copy-start.388
  1701.0 8.2 copy-start.389
  1702.6 6.6 collective-permute-start.9
  1903.4 9.1 copy-start.285
  1903.4 9.1 copy-start.338
  1905.3 9.5 copy-start.313
  1927.3 25.9 copy-start.429
  1927.4 8.2 copy-start.386
  1929.0 6.6 collective-permute-start.10
  2129.7 9.1 copy-start.286
  2129.7 9.1 copy-start.339
  2131.7 9.4 copy-start.314
  2153.9 8.2 copy-start.384
  2155.5 6.6 collective-permute-start.11
  2345.8 85.8 %reduce-scatter.23.cloned.1.call-start = ((), (), s32[]{:S(2)}) async-start(), calls=%async_computation.10 | async-start | bytes 3981312 | tf_op jit(solution)/shard_map/reduce_scatter | solution.py:345
  2349.6 138.2 %reduce-scatter.29.cloned.1.call-start = ((), (), s32[]{:S(2)}) async-start(), calls=%async_computation.13 | async-start | bytes 5308416 | tf_op jit(solution)/shard_map/reduce_scatter | solution.py:348
  2354.1 193.4 %reduce-scatter.35.cloned.1.call-start = ((), (), s32[]{:S(2)}) async-start(), calls=%async_computation.16 | async-start | bytes 5308416
  2371.9 222.1 %all-reduce.125.cloned.1.call-start = ((), (), s32[]{:S(2)}) async-start(), calls=%async_computation.20 | async-start | bytes 3080192 | tf_op jit(solution)/shard_map/psum | solution.py:364
  2378.9 218.7 %reduce-scatter.33.cloned.1.call-start = ((), (), s32[]{:S(2)}) async-start(), calls=%async_computation.15 | async-start | bytes 245760
  2382.1 218.5 %reduce-scatter.31.cloned.1.call-start = ((), (), s32[]{:S(2)}) async-start(), calls=%async_computation.14 | async-start | bytes 368640
  2434.2 193.6 %reduce-scatter.37.cloned.1.call-start = ((), (), s32[]{:S(2)}) async-start(), calls=%async_computation.17 | async-start | bytes 368640
  2490.6 62.3 %copy-start.422 = (f32[1536]{0:T(1024)S(1)}, f32[1536]{0:T(1024)}, u32[]{:S(2)}) copy-start(f32[1536]{0:T(1024)} %copy-done.421) | copy-start | bytes 18436
  2490.6 62.3 %copy-start.424 = (f32[1536]{0:T(1024)S(1)}, f32[1536]{0:T(1024)}, u32[]{:S(2)}) copy-start(f32[1536]{0:T(1024)} %copy-done.423) | copy-start | bytes 18436
  2490.6 62.3 %copy-start.426 = (f32[1536]{0:T(1024)S(1)}, f32[1536]{0:T(1024)}, u32[]{:S(2)}) copy-start(f32[1536]{0:T(1024)} %copy-done.425) | copy-start | bytes 18436
  2490.6 62.3 %copy-start.428 = (f32[1536]{0:T(1024)S(1)}, f32[1536]{0:T(1024)}, u32[]{:S(2)}) copy-start(f32[1536]{0:T(1024)} %copy-done.427) | copy-start | bytes 18436
  2490.7 62.3 %copy-start.430 = (f32[1536]{0:T(1024)S(1)}, f32[1536]{0:T(1024)}, u32[]{:S(2)}) copy-start(f32[1536]{0:T(1024)} %copy-done.429) | copy-start | bytes 18436
  2490.7 62.3 %copy-start.243 = (f32[5,134,384]{2,1,0:T(8,128)S(1)}, f32[5,134,384]{2,1,0:T(8,128)}, u32[]{:S(2)}) copy-start(f32[5,134,384]{2,1,0:T(8,128)} %get-tuple-element.1261) | copy-start | bytes 3087364
  2490.7 62.3 %copy-start.262 = (bf16[134,384]{1,0:T(8,128)(2,1)S(1)}, bf16[134,384]{1,0:T(8,128)(2,1)}, u32[]{:S(2)}) copy-start(bf16[134,384]{1,0:T(8,128)(2,1)} %get-tuple-element.1260) | copy-start | bytes 308740
  2490.7 164.6 %reduce-scatter.27.cloned.1.call-start = ((), (), s32[]{:S(2)}) async-start(), calls=%async_computation.12 | async-start | bytes 491520 | tf_op jit(solution)/shard_map/reduce_scatter | solution.py:357
  2549.7 133.4 %reduce-scatter.39.cloned.1.call-start = ((), (), s32[]{:S(2)}) async-start(), calls=%async_computation.18 | async-start | bytes 522240
  2552.8 157.8 %reduce-scatter.41.cloned.1.call-start = ((), (), s32[]{:S(2)}) async-start(), calls=%async_computation.19 | async-start | bytes 522240
  2594.0 116.6 %copy-start.260 = (f32[2,36,32,32]{1,3,2,0:T(8,128)S(1)}, f32[2,36,32,32]{1,3,2,0:T(8,128)}, u32[]{:S(2)}) copy-start(f32[2,36,32,32]{1,3,2,0:T(8,128)} %get-tuple-element.1596) | copy-start | bytes 884740
  2602.2 109.4 %copy-start.1 = (bf16[2,384,1536]{2,1,0:T(8,128)(2,1)S(1)}, bf16[2,384,1536]{2,1,0:T(8,128)(2,1)}, u32[]{:S(2)}) copy-start(bf16[2,384,1536]{2,1,0:T(8,128)(2,1)} %param.50) | copy-start | bytes 7077892
  (366 other events, 1123.4 us)
Sparse Core Ops, SparseCore 0:
  2345.9 34.1 reduce-scatter.24
  2382.4 49.1 reduce-scatter.22
  2434.0 53.8 reduce-scatter.28
  2490.1 57.3 reduce-scatter.34
  2550.9 22.5 reduce-scatter.32
  2576.3 24.1 reduce-scatter.30
  2603.5 24.2 reduce-scatter.36
  2630.8 24.4 reduce-scatter.26
  2658.9 24.1 reduce-scatter.38
  2686.4 24.1 reduce-scatter.40
Sparse Core Ops, SparseCore 1:
  2380.2 181.1 all-reduce.124
where the time goes:
time: 2750 us; the launch traced here: 2720 us
  local copies, waits for them, and re-layouts  1080 us (39%)
  matrix products  680 us (25%)
  other arithmetic  332 us (12%)
  waiting for transfers between devices  290 us (11%)
  blocking collectives  274 us (10%)
    dot_general x56, matrix products, crop_attention(): jnp.einsum('...lhi,...hij->...lhj', queries, kv_state, precision=HIGH)  160 us
    dot_general x56, matrix products, crop_attention(): kv_state = jnp.einsum('...lhi,...lhj->...hij', keys, values, precision=HIGH)  159 us
    concatenate x56, local copies, waits for them, and re-layouts, depthwise(): return jnp.concatenate(results, axis=1)  143 us
    unnamed x17, waiting for transfers between devices  136 us
    conv_general_dilated x56, matrix products, depthwise(): lax.conv_general_dilated(crop_cells, kernel_grid, (1, 1), 'SAME', dimensi...  135 us
    reshape x63, local copies, waits for them, and re-layouts, attention_mix(): attended.reshape(images, crop_tokens, 2 * heads * head_size)  117 us
    psum x7, blocking collectives, body(): lax.psum((jnp.sum(branch, axis=0), jnp.sum(branch * branch, axis=0)), 'dp')  96.6 us
    dot_general x28, matrix products, attention_mix(): jnp.einsum('abgi,gio->abgo', spread.reshape(images, tokens_img, groups, h...  95.7 us
  transfers between devices with their start and end apart: 23, of which 19 were waited for; matrix products, arithmetic and copies ran while one was open for 3% of the time, Pallas kernels for 0%

commit v1 on v0

v1 whole, which is shorter than its diff:
```python
import functools

import jax
import jax.numpy as jnp
from jax import lax
from jax.experimental import pallas as pl
from jax.experimental.pallas import tpu as pltpu
from jax.sharding import PartitionSpec as P

F32 = jnp.float32
BF = jnp.bfloat16
EPS = 1e-05
LANE = 128
SUB = 8
ROWS = 160
SMALL = 112
BLOCKS = ((0, 56), (56, 56), (112, 48))
HEADS = 4
UNITS = 6
NN = (((1,), (0,)), ((), ()))
NT = (((1,), (1,)), ((), ()))
TN = (((0,), (0,)), ((), ()))


def mm(a, b, dims=NN):
    return lax.dot_general(a, b, dims, preferred_element_type=F32)


def iota(shape, dim):
    return lax.broadcasted_iota(jnp.int32, shape, dim)


def lanes(j):
    if isinstance(j, int):
        return slice(j * LANE, (j + 1) * LANE)
    return pl.ds(pl.multiple_of(j * LANE, LANE), LANE)


def spread_matrix(tokens):
    row, col = iota((ROWS, tokens), 0), iota((ROWS, tokens), 1)
    crop = (row >= 56).astype(jnp.int32)
    inner = row - 56 * crop
    big = crop * 49 + (inner >> 3) * 7 + (inner & 7)
    small_row = row - SMALL
    pair = (small_row >= 24).astype(jnp.int32)
    inner = small_row - 24 * pair
    small = 98 + (pair * 2 + ((inner & 7) >> 2)) * 9 + (inner >> 3) * 3 + (inner & 3)
    is_big = row < SMALL
    valid = jnp.where(is_big, row & 7, (row & 3) + 4) < 7
    hit = (jnp.where(is_big, big, small) == col) & valid
    return jnp.where(hit, 1.0, 0.0).astype(BF)


def split_matrix(width):
    row, col = iota((width, width), 0), iota((width, width), 1)
    head = (row >= 96).astype(jnp.int32) + (row >= 192).astype(jnp.int32) + (row >= 288).astype(jnp.int32)
    rest = row - 96 * head
    part = (rest >= 32).astype(jnp.int32) + (rest >= 64).astype(jnp.int32)
    target = part * 128 + head * 32 + (rest - 32 * part)
    return jnp.where(target == col, 1.0, 0.0).astype(BF)


def row_mask(width=LANE):
    row = iota((ROWS, width), 0)
    valid = jnp.where(row < SMALL, row & 7, (row & 3) + 4) < 7
    return jnp.where(valid, 1.0, 0.0)


def crop_mask(rows, columns):
    row, col = iota((rows, columns), 0), iota((rows, columns), 1)
    for step in (3, 2, 1):
        col = jnp.where(col >= rows * step, col - rows * step, col)
    row_crop = (row >= 24).astype(jnp.int32) * 2 + ((row & 7) >> 2)
    col_crop = (col >= 24).astype(jnp.int32) * 2 + ((col & 7) >> 2)
    return jnp.where(row_crop == col_crop, 1.0, 0.0)


def head_masks():
    lane = iota((1, LANE), 1)
    return [jnp.where((lane >= 32 * h) & (lane < 32 * h + 32), 1.0, 0.0) for h in range(HEADS)]


def stacked(value, masks):
    return jnp.concatenate([value * mask for mask in masks], axis=0).astype(BF)


def shifted(tokens, step):
    if step == 0:
        return tokens
    moved = pltpu.roll(tokens, (-step) % SUB, 1)
    if abs(step) == 1:
        return moved
    at = iota((1, SUB, LANE), 1)
    if tokens.shape[0] > 6:
        wrong = (at == 0) if step < 0 else (at == 6)
    else:
        wrong = ((at & 3) == 0) if step < 0 else ((at & 3) == 2)
    return jnp.where(wrong, 0.0, moved)


def tap_pairs(side, step):
    return range(max(0, -step), min(side, side - step))


def crops(tokens):
    return ((tokens[:14], 7), (tokens[14:], 3))


def depthwise(tokens, taps, reach, flip=False):
    margin = reach // 2
    parts = []
    for cells, side in crops(tokens):
        sums = [None] * side
        for dj in range(-margin, margin + 1):
            moved = shifted(cells, dj).reshape(2, side, SUB, LANE)
            for di in range(-margin, margin + 1):
                tap = (margin - di) * reach + margin - dj if flip else (margin + di) * reach + margin + dj
                weight = taps[tap : tap + 1, :].reshape(1, 1, LANE)
                for a in tap_pairs(side, di):
                    term = moved[:, a + di] * weight
                    sums[a] = term if sums[a] is None else sums[a] + term
        parts.append(jnp.stack(sums, axis=1).reshape(2 * side, SUB, LANE))
    return jnp.concatenate(parts, axis=0)


def depthwise_taps(tokens, grads, reach):
    margin = reach // 2
    totals = {}
    for (cells, side), (grad_cells, _) in zip(crops(tokens), crops(grads)):
        grad_cells = grad_cells.reshape(2, side, SUB, LANE)
        for dj in range(-margin, margin + 1):
            moved = shifted(cells, dj).reshape(2, side, SUB, LANE)
            for di in range(-margin, margin + 1):
                tap = (margin + di) * reach + margin + dj
                total = totals.get(tap)
                for a in tap_pairs(side, di):
                    term = moved[:, a + di] * grad_cells[:, a]
                    total = term if total is None else total + term
                if total is not None:
                    totals[tap] = total
    return [jnp.sum(jnp.sum(totals[tap], axis=0), axis=0, keepdims=True) for tap in range(reach * reach)]


def softplus(x):
    small = jnp.exp(-jnp.abs(x))
    return jnp.maximum(x, 0.0) + jnp.where(small < 1e-3, small * (1.0 - 0.5 * small), jnp.log(1.0 + small))


def silu_parts(x):
    gate = 0.5 * jnp.tanh(0.5 * x) + 0.5
    value = x * gate
    return value, gate + value * (1.0 - gate)


def column_sum(value):
    return jnp.sum(value, axis=0, keepdims=True)


def kernel(
    n_dp,
    x_ref, ct_ref, qkv_ref, dw_ref, group_ref, proj_ref, inv_ref, ibias_ref, mdw_ref, mbias_ref, point_ref,
    gain_ref, shift_ref,
    out_ref, xgrad_ref, gqkv_ref, gproj_ref, ginv_ref, gpoint_ref, sga_ref, sgm_ref,
    perm, wp, blocks_bd, dwp, rmask, smask, hid, hidf, normed, mixo, rden, tvals, joined, s0, dvals, gmix,
    pre_u, pre_d, act, act_d, mid, gact, branch, gnow, stats, exbuf, send_sem, recv_sem,
):
    me = lax.axis_index("dp")
    layers = qkv_ref.shape[0]
    width = x_ref.shape[1]
    expanded = inv_ref.shape[2]
    total_rows = float(x_ref.shape[0] * n_dp)
    wide = width // LANE
    stages = 2 * layers

    barrier = pltpu.get_barrier_semaphore()

    def greet(k, carry):
        pl.semaphore_signal(barrier, inc=1, device_id={"dp": lax.rem(me + k, n_dp)})
        return carry

    lax.fori_loop(1, n_dp, greet, 0)

    masks = head_masks()
    perm[...] = split_matrix(width)
    rmask[...] = row_mask()
    smask[...] = crop_mask(48, 192)

    block_lane, block_row = iota((LANE, LANE), 1), iota((LANE, LANE), 0)
    on_diag = (block_lane >> 5) == (block_row >> 5)
    tile = jnp.where((iota((32, LANE), 1) & 31) == iota((32, LANE), 0), 1.0, 0.0).astype(BF)
    for l in range(layers):
        for c in range(wide):
            cut = slice(c * width, (c + 1) * width)
            w_split = mm(qkv_ref[l, :, cut], perm[...]).astype(BF)
            k_split = mm(dw_ref[l, :, cut], perm[...])
            for part in range(3):
                target = lanes(part * wide + c)
                wp[l, :, target] = w_split[:, lanes(part)]
                dwp[l, 0:25, target] = k_split[:, lanes(part)]
                rows = jnp.concatenate([group_ref[l, 3 * (4 * c + i) + part] for i in range(HEADS)], axis=0)
                full = jnp.where(on_diag, mm(rows, tile), 0.0)
                blocks_bd[l, part * wide + c] = full.astype(BF)

    spread = spread_matrix(x_ref.shape[0])
    hid[0] = mm(spread, x_ref[...]).astype(BF)
    gnow[...] = mm(spread, ct_ref[...])
    pl.semaphore_wait(barrier, n_dp - 1)

    def exchange(e, vectors):
        count = len(vectors) * wide
        rows = -(-count // SUB) * SUB
        for i, vector in enumerate(vectors):
            for j in range(wide):
                at = i * wide + j
                exbuf[e, me, at : at + 1, :] = vector[:, lanes(j)]

        def send(k, carry):
            pltpu.make_async_remote_copy(
                src_ref=exbuf.at[e, me, 0:rows],
                dst_ref=exbuf.at[e, me, 0:rows],
                send_sem=send_sem.at[e],
                recv_sem=recv_sem.at[e],
                device_id={"dp": lax.rem(me + k, n_dp)},
            ).start()
            return carry

        lax.fori_loop(1, n_dp, send, 0)
        whole = exbuf.at[e, 0 : n_dp - 1, 0:rows]
        pltpu.make_async_copy(whole, whole, recv_sem.at[e]).wait()
        total = exbuf[e, 0, 0:rows]
        for d in range(1, n_dp):
            total = total + exbuf[e, d, 0:rows]
        pltpu.make_async_copy(whole, whole, send_sem.at[e]).wait()
        return [
            jnp.concatenate([total[i * wide + j : i * wide + j + 1] for j in range(wide)], axis=1)
            for i in range(len(vectors))
        ]

    def attention_forward(l, s):
        joined[l] = mm(hid[s], wp[l]).astype(BF).astype(F32)

        def chunk(j, carry):
            at = lanes(j)
            cells = joined[l, :, at]
            conv = depthwise(cells.reshape(20, SUB, LANE), dwp[l, :, at], 5).reshape(ROWS, LANE)
            conv = (conv * rmask[...]).astype(BF)
            s0[l, :, at] = conv
            linear = mm(conv, blocks_bd[l, j])
            part = j // wide
            keep = rmask[...]
            for source, value in ((0, cells), (1, linear)):
                soft = softplus(value)
                soft = jnp.where(part == 1, soft * keep, soft)
                tvals[l, :, lanes(part * UNITS + source * wide + j % wide)] = jnp.where(part == 2, value, soft)
            return carry

        lax.fori_loop(0, 3 * wide, chunk, 0)

        def unit(u, carry):
            for start, size in BLOCKS:
                rows = slice(start, start + size)
                query = tvals[l, rows, lanes(u)]
                key = tvals[l, rows, lanes(u + UNITS)]
                value = tvals[l, rows, lanes(u + 2 * UNITS)]
                scores = mm(query.astype(BF), stacked(key, masks), NT)
                if start == SMALL:
                    scores = scores * smask[...]
                both = jnp.concatenate(
                    [stacked(value, masks), stacked(jnp.ones_like(value), masks)], axis=1
                )
                sums = mm(scores.astype(BF), both)
                inverse = 1.0 / sums[:, LANE:]
                rden[l, rows, lanes(u)] = inverse
                mixo[l, rows, lanes(u)] = sums[:, :LANE] * inverse
            return carry

        lax.fori_loop(0, UNITS, unit, 0)
        branch[...] = mm(mixo[l].astype(BF), proj_ref[l])

    def expand_forward(l, s):
        pre_u[l] = mm(hid[s], inv_ref[l])

        def chunk(j, carry):
            at = lanes(j)
            pre = pre_u[l, :, at] + ibias_ref[l, :, at].astype(F32)
            value, slope = silu_parts(pre)
            value = value * rmask[...]
            pre_u[l, :, at] = value
            pre_d[l, :, at] = slope * rmask[...]
            taps = mdw_ref[l, :, at].astype(F32)
            conv = depthwise(value.reshape(20, SUB, LANE), taps, 3).reshape(ROWS, LANE)
            out, out_slope = silu_parts(conv + mbias_ref[l, :, at].astype(F32))
            act[l, :, at] = (out * rmask[...]).astype(BF)
            act_d[l, :, at] = out_slope
            return carry

        lax.fori_loop(0, expanded // LANE, chunk, 0)
        branch[...] = mm(act[l], point_ref[l])

    for s in range(stages):
        l = s // 2
        if s % 2 == 0:
            attention_forward(l, s)
        else:
            expand_forward(l, s)
        keep = rmask[...]
        for j in range(wide):
            branch[:, lanes(j)] = branch[:, lanes(j)] * keep
        value = branch[...]
        vectors = [column_sum(value), column_sum(value * value)]
        mean, square = exchange(s, vectors)
        mean = mean * (1.0 / total_rows)
        square = square * (1.0 / total_rows)
        scale = lax.rsqrt(square - mean * mean + EPS)
        stats[s : s + 1, :] = scale
        norm = (branch[...] - mean) * scale
        gain = gain_ref[s].astype(F32)
        shift = shift_ref[s].astype(F32)
        after = hid[s].astype(F32) + gain * norm + shift
        for j in range(wide):
            normed[s, :, lanes(j)] = norm[:, lanes(j)] * keep
            hid[s + 1, :, lanes(j)] = (after[:, lanes(j)] * keep).astype(BF)

    out_ref[...] = mm(spread, hid[stages], TN).astype(BF)

    def attention_backward(l, s, grad_branch):
        gmix[...] = mm(grad_branch, proj_ref[l], NT).astype(BF).astype(F32)

        def unit(u, carry):
            for start, size in BLOCKS:
                rows = slice(start, start + size)
                query = tvals[l, rows, lanes(u)]
                key = tvals[l, rows, lanes(u + UNITS)]
                value = tvals[l, rows, lanes(u + 2 * UNITS)]
                down = gmix[rows, lanes(u)] * rden[l, rows, lanes(u)]
                level = -down * mixo[l, rows, lanes(u)]
                ones = jnp.ones_like(value)
                key_stack, query_stack, down_stack = (
                    stacked(key, masks),
                    stacked(query, masks),
                    stacked(down, masks),
                )
                grad_scores = mm(
                    jnp.concatenate([down, level], axis=1).astype(BF),
                    jnp.concatenate([stacked(value, masks), stacked(ones, masks)], axis=1),
                    NT,
                )
                grad_scores_t = mm(
                    jnp.concatenate([value, ones], axis=1).astype(BF),
                    jnp.concatenate([down_stack, stacked(level, masks)], axis=1),
                    NT,
                )
                scores_t = mm(key.astype(BF), query_stack, NT)
                if start == SMALL:
                    inside = smask[...]
                    grad_scores = grad_scores * inside
                    grad_scores_t = grad_scores_t * inside
                    scores_t = scores_t * inside
                grad_query = mm(grad_scores.astype(BF), key_stack)
                grad_key = mm(grad_scores_t.astype(BF), query_stack)
                grad_value = mm(scores_t.astype(BF), down_stack)
                dvals[rows, lanes(u)] = grad_query * (1.0 - jnp.exp(-query))
                dvals[rows, lanes(u + UNITS)] = grad_key * (1.0 - jnp.exp(-key))
                dvals[rows, lanes(u + 2 * UNITS)] = grad_value
            return carry

        lax.fori_loop(0, UNITS, unit, 0)

        def chunk(j, carry):
            at = lanes(j)
            part = j // wide
            slot = part * UNITS + j % wide
            grad_spread = dvals[:, lanes(slot + wide)].astype(BF)
            block = jnp.where(on_diag, mm(s0[l, :, at], grad_spread, TN), 0.0)
            sga_ref[l, 32:64, at] = block[0:32] + block[32:64] + block[64:96] + block[96:128]
            grad_conv = mm(grad_spread, blocks_bd[l, j], NT).reshape(20, SUB, LANE)
            cells = joined[l, :, at].reshape(20, SUB, LANE)
            for tap, row in enumerate(depthwise_taps(cells, grad_conv, 5)):
                sga_ref[l, tap : tap + 1, at] = row
            back = depthwise(grad_conv, dwp[l, :, at], 5, flip=True).reshape(ROWS, LANE)
            mid[:, at] = (dvals[:, lanes(slot)] + back * rmask[...]).astype(BF)
            return carry

        lax.fori_loop(0, 3 * wide, chunk, 0)
        grad_hidden = mm(mid[:, : 3 * width], wp[l], NT)
        for c in range(wide):
            piece = jnp.concatenate([mid[:, lanes(part * wide + c)] for part in range(3)], axis=1)
            natural = mm(piece, perm[...], NT).astype(BF)
            gqkv_ref[l, :, c * width : (c + 1) * width] = mm(hid[s], natural, TN).astype(BF)
        gproj_ref[l] = mm(grad_branch, mixo[l].astype(BF), TN).astype(BF)
        return grad_hidden

    def expand_backward(l, s, grad_branch):
        gact[...] = mm(grad_branch, point_ref[l], NT).astype(BF).astype(F32)

        def chunk(j, carry):
            at = lanes(j)
            grad_conv = gact[:, at] * act_d[l, :, at]
            sgm_ref[l, 9:10, at] = column_sum(grad_conv)
            cells = pre_u[l, :, at].reshape(20, SUB, LANE)
            grad_conv = grad_conv.reshape(20, SUB, LANE)
            for tap, row in enumerate(depthwise_taps(cells, grad_conv, 3)):
                sgm_ref[l, tap : tap + 1, at] = row
            taps = mdw_ref[l, :, at].astype(F32)
            back = depthwise(grad_conv, taps, 3, flip=True).reshape(ROWS, LANE)
            grad_pre = (back * pre_d[l, :, at]).astype(BF)
            mid[:, at] = grad_pre
            sgm_ref[l, 10:11, at] = column_sum(grad_pre.astype(F32))
            return carry

        lax.fori_loop(0, expanded // LANE, chunk, 0)
        grad_hidden = mm(mid[...], inv_ref[l], NT)
        ginv_ref[l] = mm(hid[s], mid[...], TN).astype(BF)
        gpoint_ref[l] = mm(grad_branch, act[l], TN).astype(BF)
        return grad_hidden

    for s in range(stages - 1, -1, -1):
        l = s // 2
        keep = rmask[...]
        upstream = gnow[...]
        norm = normed[s]
        local_cross, local_sum = column_sum(upstream * norm), column_sum(upstream)
        if s % 2 == 0:
            sga_ref[l, 25:26, 0:width] = local_cross
            sga_ref[l, 25:26, width : 2 * width] = local_sum
        else:
            sgm_ref[l, 11:12, 0:width] = local_cross
            sgm_ref[l, 11:12, width : 2 * width] = local_sum
        cross, total = exchange(stages + s, [local_cross, local_sum])
        gain = gain_ref[s].astype(F32)
        scale = stats[s : s + 1, :]
        cross = cross * (1.0 / total_rows)
        total = total * (1.0 / total_rows)
        grad_branch = (scale * gain) * (gnow[...] - total - normed[s] * cross)
        grad_branch = jnp.concatenate(
            [grad_branch[:, lanes(j)] * keep for j in range(wide)], axis=1
        ).astype(BF)
        back = attention_backward if s % 2 == 0 else expand_backward
        grad_hidden = back(l, s, grad_branch)
        gnow[...] = (gnow[...] + grad_hidden).astype(BF).astype(F32)

    xgrad_ref[...] = mm(spread, gnow[...].astype(BF), TN).astype(BF)


def body(
    activations, cotangent, att_qkv, att_dw, att_group, att_proj, mb_inv, mb_inv_bias, mb_dw, mb_dw_bias, mb_point,
    bn_gain, bn_bias,
):
    n_dp = lax.axis_size("dp")
    layers, width, joined_width = att_qkv.shape
    mixed_width = att_proj.shape[1]
    expanded = mb_inv.shape[2]
    tokens = activations.shape[2]
    stages = 2 * layers
    vmem = pl.BlockSpec(memory_space=pltpu.VMEM)
    results = pl.pallas_call(
        functools.partial(kernel, n_dp),
        out_shape=(
            jax.ShapeDtypeStruct((tokens, width), BF),
            jax.ShapeDtypeStruct((tokens, width), BF),
            jax.ShapeDtypeStruct((layers, width, joined_width), BF),
            jax.ShapeDtypeStruct((layers, width, mixed_width), BF),
            jax.ShapeDtypeStruct((layers, width, expanded), BF),
            jax.ShapeDtypeStruct((layers, width, expanded), BF),
            jax.ShapeDtypeStruct((layers, 64, joined_width), F32),
            jax.ShapeDtypeStruct((layers, 16, expanded), F32),
        ),
        in_specs=[vmem] * 13,
        out_specs=(vmem,) * 8,
        scratch_shapes=[
            pltpu.VMEM((width, width), BF),
            pltpu.VMEM((layers, width, joined_width), BF),
            pltpu.VMEM((layers, joined_width // LANE, LANE, LANE), BF),
            pltpu.VMEM((layers, 32, joined_width), F32),
            pltpu.VMEM((ROWS, LANE), F32),
            pltpu.VMEM((48, 192), F32),
            pltpu.VMEM((stages + 1, ROWS, width), BF),
            pltpu.VMEM((8, LANE), F32),
            pltpu.VMEM((stages, ROWS, width), F32),
            pltpu.VMEM((layers, ROWS, mixed_width), F32),
            pltpu.VMEM((layers, ROWS, mixed_width), F32),
            pltpu.VMEM((layers, ROWS, 3 * mixed_width), F32),
            pltpu.VMEM((layers, ROWS, joined_width), F32),
            pltpu.VMEM((layers, ROWS, joined_width), BF),
            pltpu.VMEM((ROWS, 3 * mixed_width), F32),
            pltpu.VMEM((ROWS, mixed_width), F32),
            pltpu.VMEM((layers, ROWS, expanded), F32),
            pltpu.VMEM((layers, ROWS, expanded), F32),
            pltpu.VMEM((layers, ROWS, expanded), BF),
            pltpu.VMEM((layers, ROWS, expanded), F32),
            pltpu.VMEM((ROWS, expanded), BF),
            pltpu.VMEM((ROWS, expanded), F32),
            pltpu.VMEM((ROWS, width), F32),
            pltpu.VMEM((ROWS, width), F32),
            pltpu.VMEM((8, width), F32),
            pltpu.VMEM((2 * stages, n_dp, SUB, LANE), F32),
            pltpu.SemaphoreType.DMA((2 * stages,)),
            pltpu.SemaphoreType.DMA((2 * stages,)),
        ],
        compiler_params=pltpu.CompilerParams(
            collective_id=0, has_side_effects=True, vmem_limit_bytes=60 * 1024 * 1024
        ),
    )(
        activations.reshape(tokens, width),
        cotangent.reshape(tokens, width),
        att_qkv,
        att_dw,
        att_group,
        att_proj,
        mb_inv,
        mb_inv_bias.reshape(layers, 1, expanded),
        mb_dw,
        mb_dw_bias.reshape(layers, 1, expanded),
        mb_point,
        bn_gain.reshape(stages, 1, width),
        bn_bias.reshape(stages, 1, width),
    )
    out, xgrad, gqkv, gproj, ginv, gpoint, sga, sgm = results

    def owned(grad):
        summed = lax.psum_scatter(grad.astype(F32), "dp", scatter_dimension=2, tiled=True)
        return lax.psum_scatter(summed.astype(BF), "pipe", scatter_dimension=1, tiled=True).astype(F32)

    sga, sgm = lax.psum((sga, sgm), ("pipe", "dp"))
    heads = width // 32
    natural = sga.reshape(layers, 64, 3, heads, 32).transpose(0, 1, 3, 2, 4)
    grad_dw = natural[:, :25].reshape(layers, 25, joined_width)
    grad_group = natural[:, 32:].transpose(0, 2, 3, 1, 4).reshape(layers, 3 * heads, 32, 32)
    gains = jnp.stack([sga[:, 25, : 2 * width], sgm[:, 11, : 2 * width]], axis=1).reshape(stages, 2 * width)
    return (
        out.reshape(activations.shape),
        xgrad.reshape(activations.shape),
        owned(gqkv),
        grad_dw,
        grad_group,
        owned(gproj).transpose(0, 2, 1),
        owned(ginv),
        sgm[:, 10],
        sgm[:, :9],
        sgm[:, 9],
        owned(gpoint).transpose(0, 2, 1),
        gains[:, :width],
        gains[:, width:],
    )


def solution(mesh):
    placed = (P("pipe", "dp", None, None), P("pipe", "dp", None, None)) + (P(),) * 11
    return jax.shard_map(
        body,
        mesh=mesh,
        in_specs=placed,
        out_specs=(
            P("pipe", "dp", None, None),
            P("pipe", "dp", None, None),
            P(None, "pipe", "dp"),
            P(),
            P(),
            P(None, "dp", "pipe"),
            P(None, "pipe", "dp"),
            P(),
            P(),
            P(),
            P(None, "dp", "pipe"),
            P(),
            P(),
        ),
        check_vma=False,
    )
```

time: 2750 us -> 674 us (0.25)
  local copies, waits for them, and re-layouts: 1080 us -> 248 us
  matrix products: 680 us -> 0 us
  other arithmetic: 332 us -> 0.12 us
  waiting for transfers between devices: 290 us -> 9.54 us
  Pallas kernels: 0 us -> 87.4 us
    dot_general x218 -> x0, matrix products: 543 us -> none  [the longest x56 160 us: crop_attention(): jnp.einsum('...lhi,...hij->...lhj', queries, kv_state, precision=HIGH)]
    reshape x214 -> x6, local copies, waits for them, and re-layouts: 407 us -> 6.62 us  [the longest x1 1.44 us: body(): grad_dw = natural[:, :25].reshape(layers, 25, joined_width)]
    unnamed x0 -> x1, blocking collectives: none -> 301 us
    psum x15 -> x0, blocking collectives: 230 us -> none  [the longest x7 96.6 us: body(): lax.psum((jnp.sum(branch, axis=0), jnp.sum(branch * branch, axis=0)), 'dp')]
    unnamed x188 -> x41, local copies, waits for them, and re-layouts: 39.6 us -> 208 us
    concatenate x56 -> x0, local copies, waits for them, and re-layouts: 143 us -> none  [depthwise(): return jnp.concatenate(results, axis=1)]
    unnamed x17 -> x9, waiting for transfers between devices: 136 us -> 0.61 us
    conv_general_dilated x56 -> x0, matrix products: 135 us -> none  [depthwise(): lax.conv_general_dilated(crop_cells, kernel_grid, (1, 1), 'SAME', dimensi...]
  transfers between devices with their start and end apart: 23 -> 5, of which waited for: 19 -> 1; matrix products, arithmetic and copies ran while one was open for 3% -> 24% of each run, Pallas kernels for 0% -> 0%
where the time goes in v1:
time: 674 us; the launch traced here: 663 us
  blocking collectives  301 us (45%)
  local copies, waits for them, and re-layouts  248 us (37%)
  Pallas kernels  87.4 us (13%)
  between operations  17.8 us (3%)
  waiting for transfers between devices  9.54 us (1%)
    unnamed x1, blocking collectives  301 us
    unnamed x41, local copies, waits for them, and re-layouts  208 us
    pallas_call x1, Pallas kernels, body(): pl.pallas_call(functools.partial(kernel, n_dp), out_shape=(jax.ShapeDtype...  87.4 us
    convert_element_type x4, local copies, waits for them, and re-layouts, owned(): grad.astype(F32)  22.9 us
  transfers between devices with their start and end apart: 5, of which 1 were waited for; matrix products, arithmetic and copies ran while one was open for 24% of the time, Pallas kernels for 0%

profile of v1, /device:TPU:0, one launch (start us, length us, event | category | flops | bytes accessed | tf_op | source)
XLA Modules:
  0.0 663.3 jit_solution(7086586610689969835)
XLA Ops:
  8.0 0.0 reduce-scatter.15.cloned.1.call-start
  8.1 2.9 copy.71.group_ref
  11.0 1.6 copy.70.dw_ref
  12.5 1.5 copy.73.mdw_ref
  14.0 1.3 copy.72.ibias_ref
  15.3 1.3 copy.74.mbias_ref
  16.6 1.3 copy.75.gain_ref
  17.9 1.3 copy.76.shift_ref
  19.2 87.4 %shard_map.228 = (bf16[134,384]{1,0:T(8,128)(2,1)}, bf16[134,384]{1,0:T(8,128)(2,1)}, bf16[2,384,1152]{2,1,0:T(8,128)(2,1)}, bf16[2,384,768]{2,1,0:T(8,128)(2,1)...) custom-call(bf16[134,384]{1,0:T(8,128)(2,1)} %bitcast.51, ...), custom_call_target="tpu_custom_call" | custom-call | tf_op jit(solution)/shard_map/pallas_call | solution.py:456
  106.6 7.3 %copy.82 = f32[2,384,1536]{1,0,2:T(2,128)} copy(bf16[2,384,1536]{2,1,0:T(8,128)(2,1)} %get-tuple-element.26) | data formatting | bytes 7077888 | tf_op jit(solution)/shard_map/convert_element_type | solution.py:521
  113.9 5.0 copy.83
  118.9 5.6 copy.77
  124.5 5.0 copy.81
  129.5 0.6 dynamic-slice
  130.7 300.5 %all-reduce.10 = (bf16[2,384,1152]{1,0,2:T(2,128)(2,1)}, bf16[2,384,1536]{1,0,2:T(2,128)(2,1)}, bf16[2,384,768]{1,0,2:T(2,128)(2,1)}, bf16[2,384,1536]{1,0,2:T(2,128)(2,1)}) all-reduce(f32[2,384,1152]{1,0,2:T(2,128)S(1)} %copy.77, f32[2,384,1536]{1,0,2:T(2,128)} %copy.82, ...), channel_id=2, replica_groups=mesh['pipe'=4,'dp'=8] {'dp'}, use_global_device_ids=true, to_apply=%region_0.0.clone | all-reduce | flops 3833856 | bytes 23003136
  431.2 1.0 dynamic-slice_convert_fusion.3
  432.2 15.3 %copy.92 = bf16[2,384,96]{0,2,1:T(8,128)(2,1)} copy(bf16[2,384,96]{1,0,2:T(2,128)(2,1)S(1)} %dynamic-slice_convert_fusion.3) | data formatting | bytes 294912
  447.6 15.5 %reshape.76 = bf16[384,192]{1,0:T(8,128)(2,1)} reshape(bf16[384,96,2]{2,1,0:T(8,128)(2,1)} %bitcast.42) | data formatting | bytes 294912
  463.1 0.0 reduce-scatter.15.cloned.1.call-update
  463.1 0.0 all-reduce.9.cloned.1.call-start
  463.1 0.5 all-reduce.9.cloned.1.call-update
  463.7 0.0 reduce-scatter.13.cloned.1.call-start
  464.4 1.1 dynamic-slice_convert_fusion.2
  465.5 11.2 %copy.90 = bf16[2,384,144]{0,2,1:T(8,128)(2,1)} copy(bf16[2,384,144]{1,0,2:T(2,128)(2,1)S(1)} %dynamic-slice_convert_fusion.2) | data formatting | bytes 442368
  476.7 15.1 %reshape.74 = bf16[384,288]{1,0:T(8,128)(2,1)} reshape(bf16[384,144,2]{2,1,0:T(8,128)(2,1)} %bitcast.41) | data formatting | bytes 442368
  491.8 0.0 reduce-scatter.13.cloned.1.call-update
  491.8 0.0 reduce-scatter.19.cloned.1.call-start
  492.5 1.5 dynamic-slice_convert_fusion
  494.0 14.3 %copy.96 = bf16[2,384,192]{0,2,1:T(8,128)(2,1)} copy(bf16[2,384,192]{1,0,2:T(2,128)(2,1)S(1)} %get-tuple-element.91) | data formatting | bytes 589824
  508.3 28.3 %reshape.80 = bf16[384,384]{1,0:T(8,128)(2,1)} reshape(bf16[384,192,2]{2,1,0:T(8,128)(2,1)} %bitcast.39) | data formatting | bytes 589824
  536.6 0.0 reduce-scatter.19.cloned.1.call-update
  536.6 0.0 reduce-scatter.17.cloned.1.call-start
  536.7 14.5 %copy.94 = bf16[2,384,192]{0,2,1:T(8,128)(2,1)} copy(bf16[2,384,192]{1,0,2:T(2,128)(2,1)S(1)} %get-tuple-element.92) | data formatting | bytes 589824
  551.2 28.3 %reshape.78 = bf16[384,384]{1,0:T(8,128)(2,1)} reshape(bf16[384,192,2]{2,1,0:T(8,128)(2,1)} %bitcast.40) | data formatting | bytes 589824
  579.5 0.0 reduce-scatter.17.cloned.1.call-update
  579.5 0.0 reduce-scatter.15.cloned.1.call-done
  579.5 5.7 reshape.77
  585.2 1.9 copy.93
  587.2 0.6 copy.86
  587.8 8.9 %all-reduce.9.cloned.1.call-done = (f32[2,64,1152]{2,1,0:T(8,128)}, f32[2,16,1536]{2,1,0:T(8,128)}) async-done(((f32[2,64,1152]{2,1,0:T(8,128)}, f32[2,16,1536]{2,1,0:T(8,128)}), (f32[2,64,1152]{2,1,0:T(8,128)}, f32[2,16,1536]{2,1,0:T(8,128)})) %all-reduce.9.cloned.1.call-update) | async-done | bytes 786448 | tf_op jit(solution)/shard_map/psum | solution.py:524
  596.7 1.6 fusion
  598.3 0.8 slice.42
  599.1 0.8 slice.41
  599.9 1.4 copy.78
  601.4 0.6 fusion.1
  602.0 0.4 slice_bitcast_fusion
  602.4 0.4 copy.80
  602.7 1.8 copy.85
  604.5 1.1 copy.79
  605.6 1.4 reshape.71
  607.0 0.7 copy.88
  607.8 0.6 copy_bitcast_fusion
  608.4 4.6 reshape.75
  613.0 3.5 copy.91
  616.4 1.6 copy.84
  618.0 11.9 %reshape.81 = bf16[96,192,2]{2,1,0:T(8,128)(2,1)} reshape(bf16[96,384]{1,0:T(8,128)(2,1)} %reduce-scatter.19.cloned.1.call-done) | data formatting | bytes 147456
  629.9 5.4 copy.97
  635.3 0.1 convert_bitcast_fusion
  635.4 0.7 copy.89
  636.1 12.1 %reshape.79 = bf16[96,192,2]{2,1,0:T(8,128)(2,1)} reshape(bf16[96,384]{1,0:T(8,128)(2,1)} %reduce-scatter.17.cloned.1.call-done) | data formatting | bytes 147456
  648.2 5.5 copy.95
  653.7 0.8 copy.87
  654.5 0.6 copy.114
  655.1 0.6 copy.115
  (18 shorter events, 0.1 us)
Async XLA Ops:
  8.0 571.5 %reduce-scatter.15.cloned.1.call-start = ((), (), s32[]{:S(2)}) async-start(), calls=%async_computation.5 | async-start | bytes 245760
  106.6 7.3 %copy-start = (bf16[2,384,1536]{2,1,0:T(8,128)(2,1)S(1)}, bf16[2,384,1536]{2,1,0:T(8,128)(2,1)}, u32[]{:S(2)}) copy-start(bf16[2,384,1536]{2,1,0:T(8,128)(2,1)} %get-tuple-element.28) | copy-start | bytes 7077892
  124.5 5.0 copy-start.5
  463.1 133.6 %all-reduce.9.cloned.1.call-start = ((), (), s32[]{:S(2)}) async-start(), calls=%async_computation.8 | async-start | bytes 1572864 | tf_op jit(solution)/shard_map/psum | solution.py:524
  463.7 144.7 %reduce-scatter.13.cloned.1.call-start = ((), (), s32[]{:S(2)}) async-start(), calls=%async_computation.4 | async-start | bytes 368640
  491.8 126.1 %reduce-scatter.19.cloned.1.call-start = ((), (), s32[]{:S(2)}) async-start(), calls=%async_computation.7 | async-start | bytes 368640
  536.6 99.5 %reduce-scatter.17.cloned.1.call-start = ((), (), s32[]{:S(2)}) async-start(), calls=%async_computation.6 | async-start | bytes 368640
  604.5 2.5 copy-start.1
  604.5 3.2 copy-start.4
  648.2 6.3 copy-start.3
  648.2 6.9 %copy-start.2 = (bf16[134,384]{1,0:T(8,128)(2,1)S(1)}, bf16[134,384]{1,0:T(8,128)(2,1)}, u32[]{:S(2)}) copy-start(bf16[134,384]{1,0:T(8,128)(2,1)} %get-tuple-element.22) | copy-start | bytes 308740
Sparse Core Ops, SparseCore 0:
  463.2 22.8 reduce-scatter.14
  492.0 23.0 reduce-scatter.12
  536.7 23.0 reduce-scatter.18
  579.6 23.0 reduce-scatter.16
Sparse Core Ops, SparseCore 1:
  468.9 127.7 all-reduce.8

commit v2 on v1

--- a/solution.py
+++ b/solution.py
@@ -156,22 +156,236 @@
     return jnp.sum(value, axis=0, keepdims=True)
 
 
-def kernel(
-    n_dp,
-    x_ref, ct_ref, qkv_ref, dw_ref, group_ref, proj_ref, inv_ref, ibias_ref, mdw_ref, mbias_ref, point_ref,
-    gain_ref, shift_ref,
-    out_ref, xgrad_ref, gqkv_ref, gproj_ref, ginv_ref, gpoint_ref, sga_ref, sgm_ref,
-    perm, wp, blocks_bd, dwp, rmask, smask, hid, hidf, normed, mixo, rden, tvals, joined, s0, dvals, gmix,
-    pre_u, pre_d, act, act_d, mid, gact, branch, gnow, stats, exbuf, send_sem, recv_sem,
-):
-    me = lax.axis_index("dp")
-    layers = qkv_ref.shape[0]
+def wait_bytes(ref, sem):
+    pltpu.make_async_copy(ref, ref, sem).wait()
+
+
+class Reduction:
+    def __init__(self, place, own, pair, first, second, send_sem, recv_sem, base):
+        self.place, self.own, self.pair, self.first, self.second = place, own, pair, first, second
+        self.send_sem, self.recv_sem, self.base = send_sem, recv_sem, base
+        self.copies = []
+
+    def copy(self, source, target, kind, pipe, dp):
+        made = pltpu.make_async_remote_copy(
+            src_ref=source,
+            dst_ref=target,
+            send_sem=self.send_sem.at[self.base + kind],
+            recv_sem=self.recv_sem.at[self.base + kind],
+            device_id={"pipe": pipe, "dp": dp},
+        )
+        made.start()
+        self.copies.append(made)
+        return made
+
+    def start(self):
+        at = self.place
+        self.arriving = [self.copy(self.own.at[1 - at.core], self.pair, 0, at.pipe, at.dp + 1 - 2 * at.core)]
+
+    def step1(self):
+        at = self.place
+        self.arriving[0].wait_recv()
+
+        def add(q, carry):
+            self.own[at.core, q] = self.own[at.core, q] + self.pair[q]
+            return carry
+
+        lax.fori_loop(0, self.pair.shape[0], add, 0)
+        peer = at.pipe + (1 + at.core) * (1 - 2 * at.bit1)
+        self.arriving = [
+            self.copy(self.own.at[at.core, at.slab(1 - at.bit1, bit)], self.first.at[bit], 1 + bit, peer, at.dp)
+            for bit in range(2)
+        ]
+
+    def step2(self):
+        at = self.place
+        for bit, arrived in enumerate(self.arriving):
+            arrived.wait_recv()
+            slab = at.slab(at.bit1, bit)
+            self.own[at.core, slab] = self.own[at.core, slab] + self.first[bit]
+        peer = at.pipe + (2 - at.core) * (1 - 2 * at.bit2)
+        self.arriving = [
+            self.copy(self.own.at[at.core, at.slab(at.bit1, 1 - at.bit2)], self.second, 3, peer, at.dp)
+        ]
+
+    def part(self):
+        self.arriving[0].wait_recv()
+        return self.own[self.place.core, self.place.pipe].astype(F32) + self.second[...].astype(F32)
+
+    def drain(self):
+        for made in self.copies:
+            made.wait_send()
+
+
+class Place:
+    def __init__(self):
+        self.pipe, self.dp = lax.axis_index("pipe"), lax.axis_index("dp")
+        self.core = lax.rem(self.dp, 2)
+        low, high = lax.rem(self.pipe, 2), self.pipe // 2
+        self.bit1 = low * (1 - self.core) + high * self.core
+        self.bit2 = high * (1 - self.core) + low * self.core
+
+    def slab(self, bit1, bit2):
+        return bit1 * (1 + self.core) + bit2 * (2 - self.core)
+
+
+class Projection(Reduction):
+    def __init__(self, *args):
+        *rest, self.outgoing, self.landed, self.whole, self.result = args
+        super().__init__(*rest)
+
+    def step3(self):
+        at = self.place
+        n_dp, rows, padded = self.outgoing.shape
+        columns = self.own.shape[3]
+        share = columns // n_dp
+        cover = min(padded + LANE, columns)
+        self.whole[:, 0:columns] = self.part()
+
+        def cut(d, carry):
+            offset = d * share
+            base = jnp.minimum(offset // LANE, (columns - cover) // LANE) * LANE
+            piece = self.whole[:, pl.ds(pl.multiple_of(base, LANE), cover)]
+            piece = pltpu.roll(piece, lax.rem(cover - (offset - base), cover), 1)
+            self.outgoing[d] = piece[:, 0:padded].astype(BF)
+            return carry
+
+        lax.fori_loop(0, n_dp, cut, 0)
+
+        def send(k, carry):
+            peer = lax.rem(at.dp + k, n_dp)
+            pltpu.make_async_remote_copy(
+                src_ref=self.outgoing.at[peer],
+                dst_ref=self.landed.at[at.dp],
+                send_sem=self.send_sem.at[self.base + 4],
+                recv_sem=self.recv_sem.at[self.base + 4],
+                device_id={"dp": peer},
+            ).start()
+            return carry
+
+        lax.fori_loop(1, n_dp, send, 0)
+        self.landed[at.dp] = self.outgoing[at.dp]
+
+    def finish(self):
+        n_dp, rows, _ = self.outgoing.shape
+        wait_bytes(self.landed.at[0 : n_dp - 1], self.recv_sem.at[self.base + 4])
+        for core in range(2):
+            total = self.landed[core].astype(F32)
+            for d in range(core + 2, n_dp, 2):
+                total = total + self.landed[d].astype(F32)
+            self.result[core * rows : (core + 1) * rows, :] = total
+        wait_bytes(self.outgoing.at[0 : n_dp - 1], self.send_sem.at[self.base + 4])
+
+
+class Small(Reduction):
+    def __init__(self, *args):
+        *rest, self.along, self.everywhere, self.result = args
+        super().__init__(*rest)
+
+    def step3(self):
+        at = self.place
+        pairs = self.along.shape[0]
+        mine = at.dp // 2
+        self.along[mine] = self.part()
+
+        def send(k, carry):
+            peer = lax.rem(mine + k, pairs)
+            pltpu.make_async_remote_copy(
+                src_ref=self.along.at[mine],
+                dst_ref=self.along.at[mine],
+                send_sem=self.send_sem.at[self.base + 4],
+                recv_sem=self.recv_sem.at[self.base + 4],
+                device_id={"dp": peer * 2 + at.core},
+            ).start()
+            return carry
+
+        lax.fori_loop(1, pairs, send, 0)
+
+    def step4(self):
+        at = self.place
+        pairs = self.along.shape[0]
+        wait_bytes(self.along.at[0 : pairs - 1], self.recv_sem.at[self.base + 4])
+        total = self.along[0]
+        for d in range(1, pairs):
+            total = total + self.along[d]
+        parts = self.everywhere.shape[0]
+        segments = parts // 2
+        mine = at.core * segments + at.pipe
+        self.everywhere[mine] = total
+
+        def send(k, carry):
+            peer = lax.rem(mine + k, parts)
+            pltpu.make_async_remote_copy(
+                src_ref=self.everywhere.at[mine],
+                dst_ref=self.everywhere.at[mine],
+                send_sem=self.send_sem.at[self.base + 5],
+                recv_sem=self.recv_sem.at[self.base + 5],
+                device_id={"pipe": lax.rem(peer, segments), "dp": at.dp - at.core + peer // segments},
+            ).start()
+            return carry
+
+        lax.fori_loop(1, parts, send, 0)
+
+    def finish(self):
+        parts = self.everywhere.shape[0]
+        wait_bytes(self.everywhere.at[0 : parts - 1], self.recv_sem.at[self.base + 5])
+        for q in range(parts):
+            self.result[q * SUB : (q + 1) * SUB, :] = self.everywhere[q]
+
+    def drain(self):
+        super().drain()
+        pairs, parts = self.along.shape[0], self.everywhere.shape[0]
+        wait_bytes(self.along.at[0 : pairs - 1], self.send_sem.at[self.base + 4])
+        wait_bytes(self.everywhere.at[0 : parts - 1], self.send_sem.at[self.base + 5])
+
+
+KINDS = 6
+MATRICES = ("qkv", "proj", "inv", "point")
+SMALLS = ("att", "mb")
+
+
+def kernel(n_dp, n_pipe, count_in, names, *refs):
+    (
+        x_ref, ct_ref, qkv_hbm, dw_ref, group_ref, proj_hbm, inv_hbm, ibias_ref, mdw_ref, mbias_ref, point_hbm,
+        gain_ref, shift_ref,
+    ) = refs[:count_in]
+    at = dict(zip(names, refs[count_in:]))
+    (
+        qkv_own, proj_ref, inv_ref, point_ref, perm, rowperm, wp, blocks_bd, dwp, mdwp, rmask, smask, hid, hid_t,
+        grad_t, normed, mixo, rden, tvals, joined, s0, dvals, gmix, pre_u, pre_d, act, act_d, mid, gact, branch,
+        gnow, stats, exbuf, send_sem, recv_sem, load_sem, red_send, red_recv, whole,
+    ) = (at[name] for name in (
+        "qkv_own", "proj", "inv", "point", "perm", "rowperm", "wp", "blocks_bd", "dwp", "mdwp", "rmask", "smask", "hid",
+        "hid_t", "grad_t", "normed", "mixo", "rden", "tvals", "joined", "s0", "dvals", "gmix", "pre_u", "pre_d",
+        "act", "act_d", "mid", "dvals", "branch", "gnow", "stats", "exbuf", "send_sem", "recv_sem", "load_sem",
+        "red_send", "red_recv", "whole",
+    ))
+    place = Place()
+    me = place.dp
+    layers = proj_ref.shape[0]
     width = x_ref.shape[1]
     expanded = inv_ref.shape[2]
     total_rows = float(x_ref.shape[0] * n_dp)
     wide = width // LANE
     stages = 2 * layers
 
+    loads = {}
+    for i, (source, target) in enumerate(
+        ((proj_hbm, proj_ref), (inv_hbm, inv_ref), (point_hbm, point_ref)), 1
+    ):
+        for l in range(layers):
+            loads[i, l] = pltpu.make_async_copy(source.at[l], target.at[l], load_sem.at[i, l])
+    piece_rows = width // 2 // n_pipe
+    for l in range(layers):
+        for q in range(2 * n_pipe):
+            pltpu.make_async_copy(
+                qkv_hbm.at[l, q * piece_rows : (q + 1) * piece_rows],
+                qkv_own.at[l, q // n_pipe, q % n_pipe],
+                load_sem.at[0, l],
+            ).start()
+        for i in range(1, 4):
+            loads[i, l].start()
+
     barrier = pltpu.get_barrier_semaphore()
 
     def greet(k, carry):
@@ -180,23 +394,65 @@
 
     lax.fori_loop(1, n_dp, greet, 0)
 
+    def greet_segment(k, carry):
+        there = lax.rem(place.pipe + k, n_pipe)
+        for other in (me, me + 1 - 2 * place.core):
+            pl.semaphore_signal(barrier, inc=1, device_id={"pipe": there, "dp": other})
+        return carry
+
+    lax.fori_loop(1, n_pipe, greet_segment, 0)
+
+    jobs = {}
+    for l in range(layers):
+        for i, name in enumerate(MATRICES):
+            jobs[name, l] = Projection(
+                place, *(at[f"{name}_{kind}"].at[l] for kind in ("own", "pair", "first", "second")), red_send, red_recv,
+                KINDS * (6 * l + i), at[f"{name}_outgoing"], at[f"{name}_landed"].at[l], whole,
+                at[f"out_{name}"].at[l],
+            )
+        for i, name in enumerate(SMALLS):
+            jobs[name, l] = Small(
+                place, *(at[f"{name}_{kind}"].at[l] for kind in ("own", "pair", "first", "second")), red_send, red_recv,
+                KINDS * (6 * l + 4 + i), *(at[f"{name}_{kind}"].at[l] for kind in ("along", "everywhere")),
+                at[f"out_{name}"].at[l],
+            )
+
     masks = head_masks()
     perm[...] = split_matrix(width)
+    row, col = iota((width, width), 0), iota((width, width), 1)
+    half = width // 2
+    core_of = (row >= half).astype(jnp.int32)
+    inner = row - half * core_of
+    for q in range(1, n_pipe):
+        inner = jnp.where(row - half * core_of >= q * piece_rows, inner + piece_rows, inner)
+    rowperm[...] = jnp.where(inner + core_of * piece_rows == col, 1.0, 0.0).astype(BF)
     rmask[...] = row_mask()
     smask[...] = crop_mask(48, 192)
 
     block_lane, block_row = iota((LANE, LANE), 1), iota((LANE, LANE), 0)
     on_diag = (block_lane >> 5) == (block_row >> 5)
     tile = jnp.where((iota((32, LANE), 1) & 31) == iota((32, LANE), 0), 1.0, 0.0).astype(BF)
-    for l in range(layers):
+
+    for t in range(dw_ref.shape[0]):
+        taps = dw_ref[t].astype(F32)
+        for l in range(layers):
+            dwp[l, t : t + 1, :] = taps[l : l + 1]
+    for t in range(mdw_ref.shape[0]):
+        taps = mdw_ref[t].astype(F32)
+        for l in range(layers):
+            mdwp[l, t : t + 1, :] = taps[l : l + 1]
+
+    def prepare(l):
+        wait_bytes(qkv_own.at[l], load_sem.at[0, l])
         for c in range(wide):
             cut = slice(c * width, (c + 1) * width)
-            w_split = mm(qkv_ref[l, :, cut], perm[...]).astype(BF)
-            k_split = mm(dw_ref[l, :, cut], perm[...])
+            w_split = mm(qkv_own[l, :, :, :, cut].reshape(width, width), perm[...]).astype(BF)
             for part in range(3):
-                target = lanes(part * wide + c)
-                wp[l, :, target] = w_split[:, lanes(part)]
-                dwp[l, 0:25, target] = k_split[:, lanes(part)]
+                wp[l, :, lanes(part * wide + c)] = w_split[:, lanes(part)]
+        taps = [mm(dwp[l, :, c * width : (c + 1) * width].astype(BF), perm[...]) for c in range(wide)]
+        for c in range(wide):
+            for part in range(3):
+                dwp[l, :, lanes(part * wide + c)] = taps[c][:, lanes(part)]
                 rows = jnp.concatenate([group_ref[l, 3 * (4 * c + i) + part] for i in range(HEADS)], axis=0)
                 full = jnp.where(on_diag, mm(rows, tile), 0.0)
                 blocks_bd[l, part * wide + c] = full.astype(BF)
@@ -204,15 +460,18 @@
     spread = spread_matrix(x_ref.shape[0])
     hid[0] = mm(spread, x_ref[...]).astype(BF)
     gnow[...] = mm(spread, ct_ref[...])
-    pl.semaphore_wait(barrier, n_dp - 1)
-
-    def exchange(e, vectors):
-        count = len(vectors) * wide
-        rows = -(-count // SUB) * SUB
+    prepare(0)
+    pl.semaphore_wait(barrier, n_dp - 1 + 2 * (n_pipe - 1))
+
+    def slot_rows(count):
+        return -(-count * wide // SUB) * SUB
+
+    def exchange_start(e, vectors):
+        rows = slot_rows(len(vectors))
         for i, vector in enumerate(vectors):
             for j in range(wide):
-                at = i * wide + j
-                exbuf[e, me, at : at + 1, :] = vector[:, lanes(j)]
+                row = i * wide + j
+                exbuf[e, me, row : row + 1, :] = vector[:, lanes(j)]
 
         def send(k, carry):
             pltpu.make_async_remote_copy(
@@ -225,15 +484,17 @@
             return carry
 
         lax.fori_loop(1, n_dp, send, 0)
-        whole = exbuf.at[e, 0 : n_dp - 1, 0:rows]
-        pltpu.make_async_copy(whole, whole, recv_sem.at[e]).wait()
+
+    def exchange_finish(e, count):
+        rows = slot_rows(count)
+        wait_bytes(exbuf.at[e, 0 : n_dp - 1, 0:rows], recv_sem.at[e])
         total = exbuf[e, 0, 0:rows]
         for d in range(1, n_dp):
             total = total + exbuf[e, d, 0:rows]
-        pltpu.make_async_copy(whole, whole, send_sem.at[e]).wait()
+        total = total * (1.0 / total_rows)
         return [
             jnp.concatenate([total[i * wide + j : i * wide + j + 1] for j in range(wide)], axis=1)
-            for i in range(len(vectors))
+            for i in range(count)
         ]
 
     def attention_forward(l, s):
@@ -275,28 +536,33 @@
             return carry
 
         lax.fori_loop(0, UNITS, unit, 0)
+        loads[1, l].wait()
         branch[...] = mm(mixo[l].astype(BF), proj_ref[l])
 
     def expand_forward(l, s):
+        loads[2, l].wait()
         pre_u[l] = mm(hid[s], inv_ref[l])
 
         def chunk(j, carry):
             at = lanes(j)
-            pre = pre_u[l, :, at] + ibias_ref[l, :, at].astype(F32)
+            pre = pre_u[l, :, at] + ibias_ref[:, at].astype(F32)[l : l + 1]
             value, slope = silu_parts(pre)
             value = value * rmask[...]
             pre_u[l, :, at] = value
-            pre_d[l, :, at] = slope * rmask[...]
-            taps = mdw_ref[l, :, at].astype(F32)
-            conv = depthwise(value.reshape(20, SUB, LANE), taps, 3).reshape(ROWS, LANE)
-            out, out_slope = silu_parts(conv + mbias_ref[l, :, at].astype(F32))
+            pre_d[l, :, at] = (slope * rmask[...]).astype(BF)
+            conv = depthwise(value.reshape(20, SUB, LANE), mdwp[l, :, at], 3).reshape(ROWS, LANE)
+            out, out_slope = silu_parts(conv + mbias_ref[:, at].astype(F32)[l : l + 1])
             act[l, :, at] = (out * rmask[...]).astype(BF)
-            act_d[l, :, at] = out_slope
+            act_d[l, :, at] = out_slope.astype(BF)
             return carry
 
         lax.fori_loop(0, expanded // LANE, chunk, 0)
+        loads[3, l].wait()
         branch[...] = mm(act[l], point_ref[l])
 
+    gains = gain_ref[...].astype(F32)
+    shifts = shift_ref[...].astype(F32)
+    last = stages - 1
     for s in range(stages):
         l = s // 2
         if s % 2 == 0:
@@ -308,23 +574,47 @@
             branch[:, lanes(j)] = branch[:, lanes(j)] * keep
         value = branch[...]
         vectors = [column_sum(value), column_sum(value * value)]
-        mean, square = exchange(s, vectors)
-        mean = mean * (1.0 / total_rows)
-        square = square * (1.0 / total_rows)
+        if s == last:
+            upstream = gnow[...]
+            vectors += [column_sum(upstream * value), column_sum(upstream)]
+        exchange_start(s, vectors)
+        if s == 0:
+            for l in range(1, layers):
+                prepare(l)
+        hid_t[s] = mm(rowperm[...], hid[s], NT).astype(BF)
+        mean, square, *backward = exchange_finish(s, len(vectors))
         scale = lax.rsqrt(square - mean * mean + EPS)
         stats[s : s + 1, :] = scale
         norm = (branch[...] - mean) * scale
-        gain = gain_ref[s].astype(F32)
-        shift = shift_ref[s].astype(F32)
-        after = hid[s].astype(F32) + gain * norm + shift
+        after = hid[s].astype(F32) + gains[s : s + 1] * norm + shifts[s : s + 1]
         for j in range(wide):
             normed[s, :, lanes(j)] = norm[:, lanes(j)] * keep
             hid[s + 1, :, lanes(j)] = (after[:, lanes(j)] * keep).astype(BF)
-
-    out_ref[...] = mm(spread, hid[stages], TN).astype(BF)
-
-    def attention_backward(l, s, grad_branch):
+        if s == last:
+            first_cross = scale * (backward[0] - mean * backward[1])
+            first_total = backward[1]
+            local_cross = scale * (vectors[2] - mean * vectors[3])
+            local_sum = vectors[3]
+
+    def small_row(name, l, row, value, at):
+        jobs[name, l].own[row // 32, row // SUB % 4, row % SUB : row % SUB + 1, at] = value
+
+    def expand_row(l, j, tap, value):
+        block = j // wide
+        jobs["mb", l].own[block // 2, block % 2 * 2 + tap // SUB, tap % SUB : tap % SUB + 1, lanes(j % wide)] = value
+
+    def matrix(name, l, left, right, columns):
+        own = jobs[name, l].own
+        step = width
+        for c in range(columns // step):
+            cut = slice(c * step, (c + 1) * step)
+            own[:, :, :, cut] = mm(left, right(cut)).astype(BF).reshape(2, n_pipe, piece_rows, step)
+        jobs[name, l].start()
+
+    def attention_backward(l, s, grad_branch, pause):
         gmix[...] = mm(grad_branch, proj_ref[l], NT).astype(BF).astype(F32)
+        matrix("proj", l, grad_t[...], lambda cut: mixo[l, :, cut].astype(BF), mixo.shape[2])
+        pause(0)
 
         def unit(u, carry):
             for start, size in BLOCKS:
@@ -365,6 +655,7 @@
             return carry
 
         lax.fori_loop(0, UNITS, unit, 0)
+        pause(1)
 
         def chunk(j, carry):
             at = lanes(j)
@@ -372,175 +663,312 @@
             slot = part * UNITS + j % wide
             grad_spread = dvals[:, lanes(slot + wide)].astype(BF)
             block = jnp.where(on_diag, mm(s0[l, :, at], grad_spread, TN), 0.0)
-            sga_ref[l, 32:64, at] = block[0:32] + block[32:64] + block[64:96] + block[96:128]
+            block = block[0:32] + block[32:64] + block[64:96] + block[96:128]
+            jobs["att", l].own[1, :, :, at] = block.reshape(4, SUB, LANE)
             grad_conv = mm(grad_spread, blocks_bd[l, j], NT).reshape(20, SUB, LANE)
             cells = joined[l, :, at].reshape(20, SUB, LANE)
             for tap, row in enumerate(depthwise_taps(cells, grad_conv, 5)):
-                sga_ref[l, tap : tap + 1, at] = row
+                small_row("att", l, tap, row, at)
             back = depthwise(grad_conv, dwp[l, :, at], 5, flip=True).reshape(ROWS, LANE)
             mid[:, at] = (dvals[:, lanes(slot)] + back * rmask[...]).astype(BF)
             return carry
 
         lax.fori_loop(0, 3 * wide, chunk, 0)
+        jobs["att", l].start()
         grad_hidden = mm(mid[:, : 3 * width], wp[l], NT)
-        for c in range(wide):
-            piece = jnp.concatenate([mid[:, lanes(part * wide + c)] for part in range(3)], axis=1)
-            natural = mm(piece, perm[...], NT).astype(BF)
-            gqkv_ref[l, :, c * width : (c + 1) * width] = mm(hid[s], natural, TN).astype(BF)
-        gproj_ref[l] = mm(grad_branch, mixo[l].astype(BF), TN).astype(BF)
-        return grad_hidden
-
-    def expand_backward(l, s, grad_branch):
-        gact[...] = mm(grad_branch, point_ref[l], NT).astype(BF).astype(F32)
+
+        def gradients():
+            def natural(cut):
+                c = cut.start // width
+                piece = jnp.concatenate([mid[:, lanes(part * wide + c)] for part in range(3)], axis=1)
+                return mm(piece, perm[...], NT).astype(BF)
+
+            matrix("qkv", l, hid_t[s], natural, 3 * width)
+
+        return grad_hidden, gradients
+
+    def expand_backward(l, s, grad_branch, pause):
+        gact[:, 0:expanded] = mm(grad_branch, point_ref[l], NT).astype(BF).astype(F32)
+        matrix("point", l, grad_t[...], lambda cut: act[l, :, cut], expanded)
+        pause(0)
 
         def chunk(j, carry):
             at = lanes(j)
-            grad_conv = gact[:, at] * act_d[l, :, at]
-            sgm_ref[l, 9:10, at] = column_sum(grad_conv)
+            grad_conv = gact[:, at] * act_d[l, :, at].astype(F32)
+            expand_row(l, j, 9, column_sum(grad_conv))
             cells = pre_u[l, :, at].reshape(20, SUB, LANE)
             grad_conv = grad_conv.reshape(20, SUB, LANE)
             for tap, row in enumerate(depthwise_taps(cells, grad_conv, 3)):
-                sgm_ref[l, tap : tap + 1, at] = row
-            taps = mdw_ref[l, :, at].astype(F32)
-            back = depthwise(grad_conv, taps, 3, flip=True).reshape(ROWS, LANE)
-            grad_pre = (back * pre_d[l, :, at]).astype(BF)
+                expand_row(l, j, tap, row)
+            back = depthwise(grad_conv, mdwp[l, :, at], 3, flip=True).reshape(ROWS, LANE)
+            grad_pre = (back * pre_d[l, :, at].astype(F32)).astype(BF)
             mid[:, at] = grad_pre
-            sgm_ref[l, 10:11, at] = column_sum(grad_pre.astype(F32))
+            expand_row(l, j, 10, column_sum(grad_pre.astype(F32)))
             return carry
 
         lax.fori_loop(0, expanded // LANE, chunk, 0)
+        jobs["mb", l].start()
+        pause(1)
         grad_hidden = mm(mid[...], inv_ref[l], NT)
-        ginv_ref[l] = mm(hid[s], mid[...], TN).astype(BF)
-        gpoint_ref[l] = mm(grad_branch, act[l], TN).astype(BF)
-        return grad_hidden
+
+        def gradients():
+            matrix("inv", l, hid_t[s], lambda cut: mid[:, cut], expanded)
+
+        return grad_hidden, gradients
+
+    queue = []
+
+    def advance():
+        for entry in queue:
+            if entry[1]:
+                entry[1].pop(0)()
+
+    def enter(job):
+        steps = [job.step1, job.step2, job.step3]
+        if isinstance(job, Small):
+            steps.append(job.step4)
+        queue.append((job, steps + [job.finish]))
+
+    def pause(k):
+        advance()
 
     for s in range(stages - 1, -1, -1):
         l = s // 2
         keep = rmask[...]
-        upstream = gnow[...]
-        norm = normed[s]
-        local_cross, local_sum = column_sum(upstream * norm), column_sum(upstream)
+        if s == last:
+            cross, total = first_cross, first_total
+        else:
+            cross, total = exchange_finish(stages + s, 2)
         if s % 2 == 0:
-            sga_ref[l, 25:26, 0:width] = local_cross
-            sga_ref[l, 25:26, width : 2 * width] = local_sum
+            small_row("att", l, 25, local_cross, slice(0, width))
+            small_row("att", l, 25, local_sum, slice(width, 2 * width))
         else:
-            sgm_ref[l, 11:12, 0:width] = local_cross
-            sgm_ref[l, 11:12, width : 2 * width] = local_sum
-        cross, total = exchange(stages + s, [local_cross, local_sum])
-        gain = gain_ref[s].astype(F32)
-        scale = stats[s : s + 1, :]
-        cross = cross * (1.0 / total_rows)
-        total = total * (1.0 / total_rows)
-        grad_branch = (scale * gain) * (gnow[...] - total - normed[s] * cross)
+            small_row("mb", l, 11, local_cross, slice(0, width))
+            small_row("mb", l, 16 + 11, local_sum, slice(0, width))
+        grad_branch = (stats[s : s + 1, :] * gains[s : s + 1]) * (gnow[...] - total - normed[s] * cross)
         grad_branch = jnp.concatenate(
             [grad_branch[:, lanes(j)] * keep for j in range(wide)], axis=1
         ).astype(BF)
+        grad_t[...] = mm(rowperm[...], grad_branch, NT).astype(BF)
         back = attention_backward if s % 2 == 0 else expand_backward
-        grad_hidden = back(l, s, grad_branch)
-        gnow[...] = (gnow[...] + grad_hidden).astype(BF).astype(F32)
-
-    xgrad_ref[...] = mm(spread, gnow[...].astype(BF), TN).astype(BF)
+        grad_hidden, gradients = back(l, s, grad_branch, pause)
+        after = (gnow[...] + grad_hidden).astype(BF).astype(F32)
+        gnow[...] = after
+        if s > 0:
+            local_cross, local_sum = column_sum(after * normed[s - 1]), column_sum(after)
+            exchange_start(stages + s - 1, [local_cross, local_sum])
+        gradients()
+        advance()
+        for name in ("att", "proj", "qkv") if s % 2 == 0 else ("mb", "point", "inv"):
+            enter(jobs[name, l])
+        if s == last:
+            at["out_x"][...] = mm(spread, hid[stages], TN).astype(BF)
+
+    at["out_g"][...] = mm(spread, gnow[...].astype(BF), TN).astype(BF)
+    while any(steps for _, steps in queue):
+        advance()
+    for job, _ in queue:
+        job.drain()
+    for e in range(2 * stages - 1):
+        rows = slot_rows(4 if e == last else 2)
+        wait_bytes(exbuf.at[e, 0 : n_dp - 1, 0:rows], send_sem.at[e])
+
+
+def unsplit(value, wide):
+    lane = iota((1, LANE), 1) >> 5
+    columns = []
+    for c in range(wide):
+        parts = [value[:, lanes(part * wide + c)] for part in range(3)]
+        for k in range(3):
+            column = None
+            for slot in range(4):
+                index = 4 * k + slot
+                moved = pltpu.roll(parts[index % 3], (slot - index // 3) % 4 * 32, 1)
+                column = moved if column is None else jnp.where(lane == slot, moved, column)
+            columns.append(column)
+    return columns
+
+
+def arrange(layers, wide, shares, x_in, g_in, qkv_in, proj_in, inv_in, point_in, att_in, mb_in,
+            x_out, g_out, qkv_out, proj_out, inv_out, point_out, dw_out, group_out, ibias_out, mdw_out, mbias_out,
+            gain_out, shift_out):
+    width = wide * LANE
+    share_qkv, share_proj, share_inv, share_point = shares
+    x_out[...] = x_in[...]
+    g_out[...] = g_in[...]
+    taps, mtaps = dw_out.shape[0], mdw_out.shape[0]
+    for l in range(layers):
+        qkv_out[l] = jnp.transpose(jnp.concatenate([qkv_in[l], jnp.zeros((32, qkv_in.shape[2]), F32)], axis=0))[
+            0:share_qkv, 0 : qkv_in.shape[1]
+        ]
+        proj_out[l] = jnp.transpose(jnp.concatenate([proj_in[l], jnp.zeros((32, proj_in.shape[2]), F32)], axis=0))[
+            0:share_proj, 0 : proj_in.shape[1]
+        ]
+        inv_out[l] = inv_in[l, :, 0:share_inv]
+        point_out[l] = jnp.transpose(jnp.concatenate([point_in[l], jnp.zeros((32, point_in.shape[2]), F32)], axis=0))[
+            0:share_point, 0 : point_in.shape[1]
+        ]
+        natural = unsplit(att_in[l], wide)
+        for j, column in enumerate(natural):
+            for t in range(taps):
+                dw_out[t, l : l + 1, lanes(j)] = column[t : t + 1]
+            group_out[l, :, lanes(j)] = column[32:64]
+        for block in range(4):
+            cut = slice(block * width, (block + 1) * width)
+            rows = mb_in[l, 16 * block : 16 * block + 16]
+            for t in range(mtaps):
+                mdw_out[t, l : l + 1, cut] = rows[t : t + 1]
+            mbias_out[l : l + 1, cut] = rows[9:10]
+            ibias_out[l : l + 1, cut] = rows[10:11]
+        gain_out[2 * l : 2 * l + 1, :] = att_in[l, 25:26, 0:width]
+        shift_out[2 * l : 2 * l + 1, :] = att_in[l, 25:26, width : 2 * width]
+        gain_out[2 * l + 1 : 2 * l + 2, :] = mb_in[l, 11:12, :]
+        shift_out[2 * l + 1 : 2 * l + 2, :] = mb_in[l, 27:28, :]
+
+
+def padded(columns):
+    return -(-columns // LANE) * LANE
 
 
 def body(
     activations, cotangent, att_qkv, att_dw, att_group, att_proj, mb_inv, mb_inv_bias, mb_dw, mb_dw_bias, mb_point,
     bn_gain, bn_bias,
 ):
-    n_dp = lax.axis_size("dp")
+    n_dp, n_pipe = lax.axis_size("dp"), lax.axis_size("pipe")
     layers, width, joined_width = att_qkv.shape
     mixed_width = att_proj.shape[1]
     expanded = mb_inv.shape[2]
     tokens = activations.shape[2]
     stages = 2 * layers
+    rows = width // 2 // n_pipe
     vmem = pl.BlockSpec(memory_space=pltpu.VMEM)
+    hbm = pl.BlockSpec(memory_space=pl.ANY)
+    columns = {"qkv": joined_width, "proj": mixed_width, "inv": expanded, "point": expanded}
+    small_columns = {"att": joined_width, "mb": width}
+    outs = {
+        "out_x": jax.ShapeDtypeStruct((tokens, width), BF),
+        "out_g": jax.ShapeDtypeStruct((tokens, width), BF),
+    }
+    scratch = {
+        "proj": pltpu.VMEM(att_proj.shape, BF),
+        "inv": pltpu.VMEM(mb_inv.shape, BF),
+        "point": pltpu.VMEM(mb_point.shape, BF),
+        "perm": pltpu.VMEM((width, width), BF),
+        "rowperm": pltpu.VMEM((width, width), BF),
+        "wp": pltpu.VMEM((layers, width, joined_width), BF),
+        "blocks_bd": pltpu.VMEM((layers, joined_width // LANE, LANE, LANE), BF),
+        "dwp": pltpu.VMEM((layers, 32, joined_width), F32),
+        "mdwp": pltpu.VMEM((layers, 16, expanded), F32),
+        "rmask": pltpu.VMEM((ROWS, LANE), F32),
+        "smask": pltpu.VMEM((48, 192), F32),
+        "hid": pltpu.VMEM((stages + 1, ROWS, width), BF),
+        "hid_t": pltpu.VMEM((stages, width, ROWS), BF),
+        "grad_t": pltpu.VMEM((width, ROWS), BF),
+        "normed": pltpu.VMEM((stages, ROWS, width), F32),
+        "mixo": pltpu.VMEM((layers, ROWS, mixed_width), F32),
+        "rden": pltpu.VMEM((layers, ROWS, mixed_width), F32),
+        "tvals": pltpu.VMEM((layers, ROWS, 3 * mixed_width), F32),
+        "joined": pltpu.VMEM((layers, ROWS, joined_width), F32),
+        "s0": pltpu.VMEM((layers, ROWS, joined_width), BF),
+        "dvals": pltpu.VMEM((ROWS, 3 * mixed_width), F32),
+        "gmix": pltpu.VMEM((ROWS, mixed_width), F32),
+        "pre_u": pltpu.VMEM((layers, ROWS, expanded), F32),
+        "pre_d": pltpu.VMEM((layers, ROWS, expanded), BF),
+        "act": pltpu.VMEM((layers, ROWS, expanded), BF),
+        "act_d": pltpu.VMEM((layers, ROWS, expanded), BF),
+        "mid": pltpu.VMEM((ROWS, expanded), BF),
+        "branch": pltpu.VMEM((ROWS, width), F32),
+        "gnow": pltpu.VMEM((ROWS, width), F32),
+        "stats": pltpu.VMEM((8, width), F32),
+        "exbuf": pltpu.VMEM((2 * stages - 1, n_dp, 2 * SUB, LANE), F32),
+        "whole": pltpu.VMEM((rows, expanded), F32),
+        "send_sem": pltpu.SemaphoreType.DMA((2 * stages - 1,)),
+        "recv_sem": pltpu.SemaphoreType.DMA((2 * stages - 1,)),
+        "load_sem": pltpu.SemaphoreType.DMA((4, layers)),
+        "red_send": pltpu.SemaphoreType.DMA((KINDS * 6 * layers,)),
+        "red_recv": pltpu.SemaphoreType.DMA((KINDS * 6 * layers,)),
+    }
+    for name in MATRICES:
+        n = columns[name]
+        share = padded(n // n_dp)
+        outs[f"out_{name}"] = jax.ShapeDtypeStruct((layers, 2 * rows, share), F32)
+        scratch[f"{name}_own"] = pltpu.VMEM((layers, 2, n_pipe, rows, n), BF)
+        scratch[f"{name}_pair"] = pltpu.VMEM((layers, n_pipe, rows, n), BF)
+        scratch[f"{name}_first"] = pltpu.VMEM((layers, 2, rows, n), BF)
+        scratch[f"{name}_second"] = pltpu.VMEM((layers, rows, n), BF)
+        scratch[f"{name}_outgoing"] = pltpu.VMEM((n_dp, rows, share), BF)
+        scratch[f"{name}_landed"] = pltpu.VMEM((layers, n_dp, rows, share), BF)
+    for name in SMALLS:
+        n = small_columns[name]
+        outs[f"out_{name}"] = jax.ShapeDtypeStruct((layers, 8 * SUB, n), F32)
+        scratch[f"{name}_own"] = pltpu.VMEM((layers, 2, n_pipe, SUB, n), F32)
+        scratch[f"{name}_pair"] = pltpu.VMEM((layers, n_pipe, SUB, n), F32)
+        scratch[f"{name}_first"] = pltpu.VMEM((layers, 2, SUB, n), F32)
+        scratch[f"{name}_second"] = pltpu.VMEM((layers, SUB, n), F32)
+        scratch[f"{name}_along"] = pltpu.VMEM((layers, n_dp // 2, SUB, n), F32)
+        scratch[f"{name}_everywhere"] = pltpu.VMEM((layers, 2 * n_pipe, SUB, n), F32)
     results = pl.pallas_call(
-        functools.partial(kernel, n_dp),
-        out_shape=(
-            jax.ShapeDtypeStruct((tokens, width), BF),
-            jax.ShapeDtypeStruct((tokens, width), BF),
-            jax.ShapeDtypeStruct((layers, width, joined_width), BF),
-            jax.ShapeDtypeStruct((layers, width, mixed_width), BF),
-            jax.ShapeDtypeStruct((layers, width, expanded), BF),
-            jax.ShapeDtypeStruct((layers, width, expanded), BF),
-            jax.ShapeDtypeStruct((layers, 64, joined_width), F32),
-            jax.ShapeDtypeStruct((layers, 16, expanded), F32),
-        ),
-        in_specs=[vmem] * 13,
-        out_specs=(vmem,) * 8,
-        scratch_shapes=[
-            pltpu.VMEM((width, width), BF),
-            pltpu.VMEM((layers, width, joined_width), BF),
-            pltpu.VMEM((layers, joined_width // LANE, LANE, LANE), BF),
-            pltpu.VMEM((layers, 32, joined_width), F32),
-            pltpu.VMEM((ROWS, LANE), F32),
-            pltpu.VMEM((48, 192), F32),
-            pltpu.VMEM((stages + 1, ROWS, width), BF),
-            pltpu.VMEM((8, LANE), F32),
-            pltpu.VMEM((stages, ROWS, width), F32),
-            pltpu.VMEM((layers, ROWS, mixed_width), F32),
-            pltpu.VMEM((layers, ROWS, mixed_width), F32),
-            pltpu.VMEM((layers, ROWS, 3 * mixed_width), F32),
-            pltpu.VMEM((layers, ROWS, joined_width), F32),
-            pltpu.VMEM((layers, ROWS, joined_width), BF),
-            pltpu.VMEM((ROWS, 3 * mixed_width), F32),
-            pltpu.VMEM((ROWS, mixed_width), F32),
-            pltpu.VMEM((layers, ROWS, expanded), F32),
-            pltpu.VMEM((layers, ROWS, expanded), F32),
-            pltpu.VMEM((layers, ROWS, expanded), BF),
-            pltpu.VMEM((layers, ROWS, expanded), F32),
-            pltpu.VMEM((ROWS, expanded), BF),
-            pltpu.VMEM((ROWS, expanded), F32),
-            pltpu.VMEM((ROWS, width), F32),
-            pltpu.VMEM((ROWS, width), F32),
-            pltpu.VMEM((8, width), F32),
-            pltpu.VMEM((2 * stages, n_dp, SUB, LANE), F32),
-            pltpu.SemaphoreType.DMA((2 * stages,)),
-            pltpu.SemaphoreType.DMA((2 * stages,)),
-        ],
+        functools.partial(kernel, n_dp, n_pipe, 13, tuple(outs) + tuple(scratch)),
+        out_shape=tuple(outs.values()),
+        in_specs=[vmem, vmem, hbm, vmem, vmem, hbm, hbm, vmem, vmem, vmem, hbm, vmem, vmem],
+        out_specs=(vmem,) * len(outs),
+        scratch_shapes=list(scratch.values()),
         compiler_params=pltpu.CompilerParams(
-            collective_id=0, has_side_effects=True, vmem_limit_bytes=60 * 1024 * 1024
+            collective_id=0, has_side_effects=True, vmem_limit_bytes=63 * 1024 * 1024
         ),
     )(
         activations.reshape(tokens, width),
         cotangent.reshape(tokens, width),
         att_qkv,
-        att_dw,
+        att_dw.transpose(1, 0, 2),
         att_group,
         att_proj,
         mb_inv,
-        mb_inv_bias.reshape(layers, 1, expanded),
-        mb_dw,
-        mb_dw_bias.reshape(layers, 1, expanded),
+        mb_inv_bias,
+        mb_dw.transpose(1, 0, 2),
+        mb_dw_bias,
         mb_point,
-        bn_gain.reshape(stages, 1, width),
-        bn_bias.reshape(stages, 1, width),
+        bn_gain,
+        bn_bias,
     )
-    out, xgrad, gqkv, gproj, ginv, gpoint, sga, sgm = results
-
-    def owned(grad):
-        summed = lax.psum_scatter(grad.astype(F32), "dp", scatter_dimension=2, tiled=True)
-        return lax.psum_scatter(summed.astype(BF), "pipe", scatter_dimension=1, tiled=True).astype(F32)
-
-    sga, sgm = lax.psum((sga, sgm), ("pipe", "dp"))
-    heads = width // 32
-    natural = sga.reshape(layers, 64, 3, heads, 32).transpose(0, 1, 3, 2, 4)
-    grad_dw = natural[:, :25].reshape(layers, 25, joined_width)
-    grad_group = natural[:, 32:].transpose(0, 2, 3, 1, 4).reshape(layers, 3 * heads, 32, 32)
-    gains = jnp.stack([sga[:, 25, : 2 * width], sgm[:, 11, : 2 * width]], axis=1).reshape(stages, 2 * width)
+    shares = tuple(columns[name] // n_dp for name in MATRICES)
+    taps, mtaps = att_dw.shape[1], mb_dw.shape[1]
+    arranged = pl.pallas_call(
+        functools.partial(arrange, layers, width // LANE, shares),
+        out_shape=(
+            jax.ShapeDtypeStruct((tokens, width), BF),
+            jax.ShapeDtypeStruct((tokens, width), BF),
+            jax.ShapeDtypeStruct((layers, shares[0], 2 * rows), F32),
+            jax.ShapeDtypeStruct((layers, shares[1], 2 * rows), F32),
+            jax.ShapeDtypeStruct((layers, 2 * rows, shares[2]), F32),
+            jax.ShapeDtypeStruct((layers, shares[3], 2 * rows), F32),
+            jax.ShapeDtypeStruct((taps, layers, joined_width), F32),
+            jax.ShapeDtypeStruct((layers, 32, joined_width), F32),
+            jax.ShapeDtypeStruct((layers, expanded), F32),
+            jax.ShapeDtypeStruct((mtaps, layers, expanded), F32),
+            jax.ShapeDtypeStruct((layers, expanded), F32),
+            jax.ShapeDtypeStruct((stages, width), F32),
+            jax.ShapeDtypeStruct((stages, width), F32),
+        ),
+        in_specs=[vmem] * 8,
+        out_specs=(vmem,) * 13,
+    )(*results)
+    x_out, g_out, qkv, proj, inv, point, dw, group, ibias, mdw, mbias, gain, shift = arranged
+    groups, size = att_group.shape[1], att_group.shape[2]
     return (
-        out.reshape(activations.shape),
-        xgrad.reshape(activations.shape),
-        owned(gqkv),
-        grad_dw,
-        grad_group,
-        owned(gproj).transpose(0, 2, 1),
-        owned(ginv),
-        sgm[:, 10],
-        sgm[:, :9],
-        sgm[:, 9],
-        owned(gpoint).transpose(0, 2, 1),
-        gains[:, :width],
-        gains[:, width:],
+        x_out.reshape(activations.shape),
+        g_out.reshape(activations.shape),
+        qkv.transpose(0, 2, 1),
+        dw.transpose(1, 0, 2),
+        group.reshape(layers, size, groups, size).transpose(0, 2, 1, 3),
+        proj,
+        inv,
+        ibias,
+        mdw.transpose(1, 0, 2),
+        mbias,
+        point,
+        gain,
+        shift,
     )
 
 

time: 674 us -> 151 us (0.22); the launches traced: 663 us -> 150 us
  blocking collectives: 301 us -> 0 us
  local copies, waits for them, and re-layouts: 248 us -> 5.8 us
  Pallas kernels: 87.4 us -> 144 us
  between operations: 17.8 us -> 0.66 us
  waiting for transfers between devices: 9.54 us -> 0 us
    unnamed x1 -> x0, blocking collectives: 301 us -> none
    unnamed x41 -> x2, local copies, waits for them, and re-layouts: 208 us -> 4.38 us
    pallas_call x1 -> x2, Pallas kernels: 87.4 us -> 144 us  [the longest x1 141 us: body(): pl.pallas_call(functools.partial(kernel, n_dp, n_pipe, 13, tuple(outs) +...]
    convert_element_type x7 -> x0, local copies, waits for them, and re-layouts: 26.4 us -> none  [the longest x4 22.9 us: owned(): grad.astype(F32)]
    psum x1 -> x0, waiting for transfers between devices: 8.93 us -> none  [body(): sga, sgm = lax.psum((sga, sgm), ('pipe', 'dp'))]
  transfers between devices with their start and end apart: 5 -> 0, of which waited for: 1 -> 0; matrix products, arithmetic and copies ran while one was open for 24% -> 0% of each run, Pallas kernels for 0% -> 0%
where the time goes in v2:
time: 151 us; the launch traced here: 150 us
  Pallas kernels  144 us (95%)
  local copies, waits for them, and re-layouts  5.8 us (4%)
    pallas_call x1, Pallas kernels, body(): pl.pallas_call(functools.partial(kernel, n_dp, n_pipe, 13, tuple(outs) +...  141 us
    unnamed x2, local copies, waits for them, and re-layouts  4.38 us

profile of v2, /device:TPU:0, one launch (start us, length us, event | category | flops | bytes accessed | tf_op | source)
XLA Modules:
  0.0 150.3 jit_solution(693662852761440043)
XLA Ops:
  0.6 2.9 %copy.28.refs_4_ = bf16[2,36,32,32]{3,2,1,0:T(8,128)(2,1)} copy(bf16[2,36,32,32]{1,3,2,0:T(8,128)(2,1)} %param.17) | data formatting | bytes 294912 | tf_op args[4]
  3.5 141.0 %shard_map.228 = (bf16[134,384]{1,0:T(8,128)(2,1)}, bf16[134,384]{1,0:T(8,128)(2,1)}, f32[2,96,256]{2,1,0:T(8,128)}, f32[2,96,128]{2,1,0:T(8,128)}, f32[2,96,256...) custom-call(bf16[134,384]{1,0:T(8,128)(2,1)} %bitcast.12, ...), custom_call_target="tpu_custom_call" | custom-call | tf_op jit(solution)/shard_map/pallas_call | solution.py:910
  144.5 2.9 %shard_map.229 = (bf16[134,384]{1,0:T(8,128)(2,1)}, bf16[134,384]{1,0:T(8,128)(2,1)}, f32[2,144,96]{2,1,0:T(8,128)}, f32[2,96,96]{2,1,0:T(8,128)}, f32[2,96,192]...) custom-call(bf16[134,384]{1,0:T(8,128)(2,1)} %get-tuple-element.34.x, ...), custom_call_target="tpu_custom_call" | custom-call | tf_op jit(solution)/shard_map/pallas_call | solution.py:936
  147.4 1.4 reshape.45
  148.9 1.5 copy.29

commit v3 on v2

--- a/solution.py
+++ b/solution.py
@@ -17,6 +17,8 @@
 BLOCKS = ((0, 56), (56, 56), (112, 48))
 HEADS = 4
 UNITS = 6
+UNIT_STEP = 6
+EXPAND_STEP = 1
 NN = (((1,), (0,)), ((), ()))
 NT = (((1,), (1,)), ((), ()))
 TN = (((0,), (0,)), ((), ()))
@@ -80,8 +82,12 @@
     return [jnp.where((lane >= 32 * h) & (lane < 32 * h + 32), 1.0, 0.0) for h in range(HEADS)]
 
 
-def stacked(value, masks):
-    return jnp.concatenate([value * mask for mask in masks], axis=0).astype(BF)
+def stacked(value):
+    return jnp.concatenate([value * mask for mask in head_masks()], axis=0).astype(BF)
+
+
+def joint(*values):
+    return jnp.concatenate(values, axis=1).astype(BF)
 
 
 def shifted(tokens, step):
@@ -152,6 +158,26 @@
     return value, gate + value * (1.0 - gate)
 
 
+def loop(count, step, body):
+    def several(i, carry):
+        for k in range(step):
+            body(i * step + k)
+        return carry
+
+    if step == count:
+        several(0, 0)
+    else:
+        lax.fori_loop(0, count // step, several, 0)
+
+
+def groups(count, step, body, unroll=False):
+    if step == count or unroll:
+        for first in range(0, count, step):
+            body(first)
+    else:
+        lax.fori_loop(0, count // step, lambda i, carry: (body(i * step), carry)[1], 0)
+
+
 def column_sum(value):
     return jnp.sum(value, axis=0, keepdims=True)
 
@@ -164,56 +190,60 @@
     def __init__(self, place, own, pair, first, second, send_sem, recv_sem, base):
         self.place, self.own, self.pair, self.first, self.second = place, own, pair, first, second
         self.send_sem, self.recv_sem, self.base = send_sem, recv_sem, base
-        self.copies = []
 
     def copy(self, source, target, kind, pipe, dp):
-        made = pltpu.make_async_remote_copy(
+        return pltpu.make_async_remote_copy(
             src_ref=source,
             dst_ref=target,
             send_sem=self.send_sem.at[self.base + kind],
             recv_sem=self.recv_sem.at[self.base + kind],
             device_id={"pipe": pipe, "dp": dp},
         )
-        made.start()
-        self.copies.append(made)
-        return made
+
+    def to_pair(self):
+        at = self.place
+        return self.copy(self.own.at[1 - at.core], self.pair, 0, at.pipe, at.dp + 1 - 2 * at.core)
+
+    def to_first(self, bit):
+        at = self.place
+        peer = at.pipe + (1 + at.core) * (1 - 2 * at.bit1)
+        return self.copy(self.own.at[at.core, at.slab(1 - at.bit1, bit)], self.first.at[bit], 1 + bit, peer, at.dp)
+
+    def to_second(self):
+        at = self.place
+        peer = at.pipe + (2 - at.core) * (1 - 2 * at.bit2)
+        return self.copy(self.own.at[at.core, at.slab(at.bit1, 1 - at.bit2)], self.second, 3, peer, at.dp)
 
     def start(self):
-        at = self.place
-        self.arriving = [self.copy(self.own.at[1 - at.core], self.pair, 0, at.pipe, at.dp + 1 - 2 * at.core)]
+        self.to_pair().start()
 
     def step1(self):
         at = self.place
-        self.arriving[0].wait_recv()
-
-        def add(q, carry):
-            self.own[at.core, q] = self.own[at.core, q] + self.pair[q]
-            return carry
-
-        lax.fori_loop(0, self.pair.shape[0], add, 0)
-        peer = at.pipe + (1 + at.core) * (1 - 2 * at.bit1)
-        self.arriving = [
-            self.copy(self.own.at[at.core, at.slab(1 - at.bit1, bit)], self.first.at[bit], 1 + bit, peer, at.dp)
-            for bit in range(2)
-        ]
+        self.to_pair().wait_recv()
+        for bit in range(2):
+            slab = at.slab(1 - at.bit1, bit)
+            self.own[at.core, slab] = self.own[at.core, slab] + self.pair[slab]
+            self.to_first(bit).start()
 
     def step2(self):
         at = self.place
-        for bit, arrived in enumerate(self.arriving):
-            arrived.wait_recv()
-            slab = at.slab(at.bit1, bit)
-            self.own[at.core, slab] = self.own[at.core, slab] + self.first[bit]
-        peer = at.pipe + (2 - at.core) * (1 - 2 * at.bit2)
-        self.arriving = [
-            self.copy(self.own.at[at.core, at.slab(at.bit1, 1 - at.bit2)], self.second, 3, peer, at.dp)
-        ]
+        for bit in range(2):
+            self.to_first(bit).wait_recv()
+        bit = 1 - at.bit2
+        slab = at.slab(at.bit1, bit)
+        total = self.own[at.core, slab].astype(F32) + self.pair[slab].astype(F32) + self.first[bit].astype(F32)
+        self.own[at.core, slab] = total.astype(self.own.dtype)
+        self.to_second().start()
 
     def part(self):
-        self.arriving[0].wait_recv()
-        return self.own[self.place.core, self.place.pipe].astype(F32) + self.second[...].astype(F32)
+        at = self.place
+        self.to_second().wait_recv()
+        slab = at.pipe
+        total = self.own[at.core, slab].astype(F32) + self.pair[slab].astype(F32)
+        return total + self.first[at.bit2].astype(F32) + self.second[...].astype(F32)
 
     def drain(self):
-        for made in self.copies:
+        for made in (self.to_pair(), self.to_first(0), self.to_first(1), self.to_second()):
             made.wait_send()
 
 
@@ -229,64 +259,88 @@
         return bit1 * (1 + self.core) + bit2 * (2 - self.core)
 
 
-class Projection(Reduction):
-    def __init__(self, *args):
-        *rest, self.outgoing, self.landed, self.whole, self.result = args
-        super().__init__(*rest)
-
-    def step3(self):
+class Columns:
+    def __init__(self, place, matrices, shares, send_sem, recv_sem, base, outgoing, landed, whole, result):
+        self.place, self.matrices, self.shares = place, matrices, shares
+        self.send_sem, self.recv_sem = send_sem.at[base], recv_sem.at[base]
+        self.outgoing, self.landed, self.whole, self.result = outgoing, landed, whole, result
+
+    def send(self):
         at = self.place
-        n_dp, rows, padded = self.outgoing.shape
-        columns = self.own.shape[3]
-        share = columns // n_dp
-        cover = min(padded + LANE, columns)
-        self.whole[:, 0:columns] = self.part()
+        n_dp, rows, width = self.outgoing.shape
+        spans, start = [], 0
+        for pieces in self.matrices:
+            first = start
+            for piece in pieces:
+                size = piece.own.shape[3]
+                self.whole[:, start : start + size] = piece.part()
+                start += size
+            spans.append((first, start - first))
+        lane = iota((1, width), 1)
 
         def cut(d, carry):
-            offset = d * share
-            base = jnp.minimum(offset // LANE, (columns - cover) // LANE) * LANE
-            piece = self.whole[:, pl.ds(pl.multiple_of(base, LANE), cover)]
-            piece = pltpu.roll(piece, lax.rem(cover - (offset - base), cover), 1)
-            self.outgoing[d] = piece[:, 0:padded].astype(BF)
+            result, target = None, 0
+            for (first, columns), share in zip(spans, self.shares):
+                cover = min(max(padded(share) + LANE, width), columns)
+                offset = d * share
+                base = jnp.minimum(offset // LANE, (columns - cover) // LANE) * LANE
+                piece = self.whole[:, pl.ds(pl.multiple_of(first + base, LANE), cover)]
+                piece = pltpu.roll(piece, lax.rem(cover + target - (offset - base), cover), 1)[:, 0:width]
+                result = piece if result is None else jnp.where(lane < target, result, piece)
+                target += share
+            self.outgoing[d] = result.astype(BF)
             return carry
 
         lax.fori_loop(0, n_dp, cut, 0)
 
-        def send(k, carry):
+        def push(k, carry):
             peer = lax.rem(at.dp + k, n_dp)
             pltpu.make_async_remote_copy(
                 src_ref=self.outgoing.at[peer],
                 dst_ref=self.landed.at[at.dp],
-                send_sem=self.send_sem.at[self.base + 4],
-                recv_sem=self.recv_sem.at[self.base + 4],
+                send_sem=self.send_sem,
+                recv_sem=self.recv_sem,
                 device_id={"dp": peer},
             ).start()
             return carry
 
-        lax.fori_loop(1, n_dp, send, 0)
+        lax.fori_loop(1, n_dp, push, 0)
         self.landed[at.dp] = self.outgoing[at.dp]
 
     def finish(self):
         n_dp, rows, _ = self.outgoing.shape
-        wait_bytes(self.landed.at[0 : n_dp - 1], self.recv_sem.at[self.base + 4])
+        wait_bytes(self.landed.at[0 : n_dp - 1], self.recv_sem)
         for core in range(2):
             total = self.landed[core].astype(F32)
             for d in range(core + 2, n_dp, 2):
                 total = total + self.landed[d].astype(F32)
             self.result[core * rows : (core + 1) * rows, :] = total
-        wait_bytes(self.outgoing.at[0 : n_dp - 1], self.send_sem.at[self.base + 4])
+        wait_bytes(self.outgoing.at[0 : n_dp - 1], self.send_sem)
 
 
 class Small(Reduction):
     def __init__(self, *args):
-        *rest, self.along, self.everywhere, self.result = args
+        *rest, self.stage, self.along, self.everywhere, self.result = args
         super().__init__(*rest)
+
+    def start(self):
+        slabs, _, columns = self.stage.shape
+        half = self.own.shape[3]
+        for q in range(slabs):
+            if half == columns:
+                self.own[q // self.own.shape[1], q % self.own.shape[1]] = self.stage[q]
+                continue
+            low, high = self.stage[q, :, 0:half], self.stage[q, :, half:columns]
+            if columns < 2 * half:
+                high = jnp.concatenate([high, jnp.zeros((SUB, 2 * half - columns), F32)], axis=1)
+            self.own[q // self.own.shape[1], q % self.own.shape[1]] = jnp.concatenate([low, high], axis=0).astype(BF)
+        super().start()
 
     def step3(self):
         at = self.place
         pairs = self.along.shape[0]
         mine = at.dp // 2
-        self.along[mine] = self.part()
+        self.along[mine] = self.part().astype(self.along.dtype)
 
         def send(k, carry):
             peer = lax.rem(mine + k, pairs)
@@ -305,13 +359,13 @@
         at = self.place
         pairs = self.along.shape[0]
         wait_bytes(self.along.at[0 : pairs - 1], self.recv_sem.at[self.base + 4])
-        total = self.along[0]
+        total = self.along[0].astype(F32)
         for d in range(1, pairs):
-            total = total + self.along[d]
+            total = total + self.along[d].astype(F32)
         parts = self.everywhere.shape[0]
         segments = parts // 2
         mine = at.core * segments + at.pipe
-        self.everywhere[mine] = total
+        self.everywhere[mine] = total.astype(self.everywhere.dtype)
 
         def send(k, carry):
             peer = lax.rem(mine + k, parts)
@@ -330,7 +384,11 @@
         parts = self.everywhere.shape[0]
         wait_bytes(self.everywhere.at[0 : parts - 1], self.recv_sem.at[self.base + 5])
         for q in range(parts):
-            self.result[q * SUB : (q + 1) * SUB, :] = self.everywhere[q]
+            value = self.everywhere[q].astype(F32)
+            half = value.shape[1]
+            self.result[q * SUB : (q + 1) * SUB, 0:half] = value[0:SUB]
+            if half < self.result.shape[1]:
+                self.result[q * SUB : (q + 1) * SUB, half:] = value[SUB:, 0 : self.result.shape[1] - half]
 
     def drain(self):
         super().drain()
@@ -339,9 +397,35 @@
         wait_bytes(self.everywhere.at[0 : parts - 1], self.send_sem.at[self.base + 5])
 
 
+PLAN = {
+    ("m2", 1): ("point.1.step1",),
+    ("done", 3): ("mb.1.step1",),
+    ("begin", 2): ("inv.1.step1",),
+    ("t0", 1): ("point.1.step2", "mb.1.step2",),
+    ("t2", 1): ("proj.1.step1",),
+    ("c0", 1): (),
+    ("c1", 1): (),
+    ("c2", 1): ("inv.1.step2", "qkv0.1.step1",),
+    ("sent", 2): ("mb.1.step3", "qkv1.1.step1",),
+    ("done", 2): ("qkv2.1.step1", "proj.1.step2", "att.1.step1",),
+    ("begin", 1): ("mbcols.1.send", "qkv0.1.step2",),
+    ("m0", 0): ("qkv1.1.step2", "qkv2.1.step2", "att.1.step2",),
+    ("m2", 0): ("point.0.step1", "mb.1.step4",),
+    ("sent", 1): ("att.1.step3", "attcols.1.send",),
+    ("done", 1): ("mb.0.step1", "mb.1.finish",),
+    ("begin", 0): ("inv.0.step1", "mbcols.1.finish",),
+    ("t0", 0): ("point.0.step2", "mb.0.step2", "att.1.step4",),
+    ("t2", 0): ("proj.0.step1",),
+    ("c0", 0): ("mb.0.step3",),
+    ("c1", 0): ("qkv0.0.step1", "inv.0.step2",),
+    ("c2", 0): ("qkv1.0.step1", "attcols.1.finish", "att.1.finish",),
+    ("sent", 0): ("qkv2.0.step1", "att.0.step1", "proj.0.step2", "mb.0.step4", "qkv0.0.step2", "mbcols.0.send",),
+    ("done", 0): ("att.0.step2", "qkv1.0.step2", "qkv2.0.step2", "att.0.step3", "attcols.0.send", "att.0.step4", "mb.0.finish", "mbcols.0.finish", "attcols.0.finish", "att.0.finish",),
+}
 KINDS = 6
-MATRICES = ("qkv", "proj", "inv", "point")
+MATRICES = ("qkv0", "qkv1", "qkv2", "proj", "inv", "point")
 SMALLS = ("att", "mb")
+JOBS = len(MATRICES) + len(SMALLS)
 
 
 def kernel(n_dp, n_pipe, count_in, names, *refs):
@@ -351,11 +435,11 @@
     ) = refs[:count_in]
     at = dict(zip(names, refs[count_in:]))
     (
-        qkv_own, proj_ref, inv_ref, point_ref, perm, rowperm, wp, blocks_bd, dwp, mdwp, rmask, smask, hid, hid_t,
+        inv_own, proj_ref, inv_ref, point_ref, perm, rowperm, wp, blocks_bd, dwp, mdwp, rmask, smask, diag, diag_t, hid, hid_t,
         grad_t, normed, mixo, rden, tvals, joined, s0, dvals, gmix, pre_u, pre_d, act, act_d, mid, gact, branch,
         gnow, stats, exbuf, send_sem, recv_sem, load_sem, red_send, red_recv, whole,
     ) = (at[name] for name in (
-        "qkv_own", "proj", "inv", "point", "perm", "rowperm", "wp", "blocks_bd", "dwp", "mdwp", "rmask", "smask", "hid",
+        "inv_own", "proj", "inv", "point", "perm", "rowperm", "wp", "blocks_bd", "dwp", "mdwp", "rmask", "smask", "diag", "diag_t", "hid",
         "hid_t", "grad_t", "normed", "mixo", "rden", "tvals", "joined", "s0", "dvals", "gmix", "pre_u", "pre_d",
         "act", "act_d", "mid", "dvals", "branch", "gnow", "stats", "exbuf", "send_sem", "recv_sem", "load_sem",
         "red_send", "red_recv", "whole",
@@ -380,7 +464,7 @@
         for q in range(2 * n_pipe):
             pltpu.make_async_copy(
                 qkv_hbm.at[l, q * piece_rows : (q + 1) * piece_rows],
-                qkv_own.at[l, q // n_pipe, q % n_pipe],
+                inv_own.at[l, q // n_pipe, q % n_pipe, :, 0 : 3 * width],
                 load_sem.at[0, l],
             ).start()
         for i in range(1, 4):
@@ -404,20 +488,24 @@
 
     jobs = {}
     for l in range(layers):
-        for i, name in enumerate(MATRICES):
-            jobs[name, l] = Projection(
-                place, *(at[f"{name}_{kind}"].at[l] for kind in ("own", "pair", "first", "second")), red_send, red_recv,
-                KINDS * (6 * l + i), at[f"{name}_outgoing"], at[f"{name}_landed"].at[l], whole,
-                at[f"out_{name}"].at[l],
+        for i, name in enumerate(MATRICES + SMALLS):
+            refs_of = [at[f"{name}_{kind}"].at[l] for kind in ("own", "pair", "first", "second")]
+            base = KINDS * (JOBS * l + i)
+            if name in SMALLS:
+                rest = [at[f"{name}_stage"]] + [at[f"{name}_{kind}"].at[l] for kind in ("along", "everywhere")]
+                jobs[name, l] = Small(place, *refs_of, red_send, red_recv, base, *rest, at[f"out_{name}"].at[l])
+            else:
+                jobs[name, l] = Reduction(place, *refs_of, red_send, red_recv, base)
+        for i, (name, members, sizes) in enumerate((
+            ("attcols", (("qkv0", "qkv1", "qkv2"), ("proj",)), (3 * width, proj_ref.shape[1])),
+            ("mbcols", (("inv",), ("point",)), (expanded, expanded)),
+        )):
+            jobs[name, l] = Columns(
+                place, [[jobs[piece, l] for piece in pieces] for pieces in members], [n // n_dp for n in sizes],
+                red_send, red_recv, KINDS * JOBS * layers + 2 * l + i, at[f"{name}_outgoing"], at[f"{name}_landed"].at[l],
+                whole, at[f"out_{name}"].at[l],
             )
-        for i, name in enumerate(SMALLS):
-            jobs[name, l] = Small(
-                place, *(at[f"{name}_{kind}"].at[l] for kind in ("own", "pair", "first", "second")), red_send, red_recv,
-                KINDS * (6 * l + 4 + i), *(at[f"{name}_{kind}"].at[l] for kind in ("along", "everywhere")),
-                at[f"out_{name}"].at[l],
-            )
-
-    masks = head_masks()
+
     perm[...] = split_matrix(width)
     row, col = iota((width, width), 0), iota((width, width), 1)
     half = width // 2
@@ -431,6 +519,9 @@
 
     block_lane, block_row = iota((LANE, LANE), 1), iota((LANE, LANE), 0)
     on_diag = (block_lane >> 5) == (block_row >> 5)
+    ones_on_diag = jnp.where(on_diag, 1.0, 0.0)
+    diag[...] = jnp.concatenate([ones_on_diag, ones_on_diag], axis=1)
+    diag_t[...] = jnp.concatenate([ones_on_diag, ones_on_diag], axis=0)
     tile = jnp.where((iota((32, LANE), 1) & 31) == iota((32, LANE), 0), 1.0, 0.0).astype(BF)
 
     for t in range(dw_ref.shape[0]):
@@ -443,10 +534,10 @@
             mdwp[l, t : t + 1, :] = taps[l : l + 1]
 
     def prepare(l):
-        wait_bytes(qkv_own.at[l], load_sem.at[0, l])
+        wait_bytes(inv_own.at[l, :, :, :, 0 : 3 * width], load_sem.at[0, l])
         for c in range(wide):
             cut = slice(c * width, (c + 1) * width)
-            w_split = mm(qkv_own[l, :, :, :, cut].reshape(width, width), perm[...]).astype(BF)
+            w_split = mm(inv_own[l, :, :, :, cut].reshape(width, width), perm[...]).astype(BF)
             for part in range(3):
                 wp[l, :, lanes(part * wide + c)] = w_split[:, lanes(part)]
         taps = [mm(dwp[l, :, c * width : (c + 1) * width].astype(BF), perm[...]) for c in range(wide)]
@@ -500,42 +591,50 @@
     def attention_forward(l, s):
         joined[l] = mm(hid[s], wp[l]).astype(BF).astype(F32)
 
-        def chunk(j, carry):
-            at = lanes(j)
-            cells = joined[l, :, at]
-            conv = depthwise(cells.reshape(20, SUB, LANE), dwp[l, :, at], 5).reshape(ROWS, LANE)
-            conv = (conv * rmask[...]).astype(BF)
-            s0[l, :, at] = conv
-            linear = mm(conv, blocks_bd[l, j])
-            part = j // wide
+        def chunks(c):
             keep = rmask[...]
-            for source, value in ((0, cells), (1, linear)):
-                soft = softplus(value)
-                soft = jnp.where(part == 1, soft * keep, soft)
-                tvals[l, :, lanes(part * UNITS + source * wide + j % wide)] = jnp.where(part == 2, value, soft)
-            return carry
-
-        lax.fori_loop(0, 3 * wide, chunk, 0)
-
-        def unit(u, carry):
-            for start, size in BLOCKS:
-                rows = slice(start, start + size)
-                query = tvals[l, rows, lanes(u)]
-                key = tvals[l, rows, lanes(u + UNITS)]
-                value = tvals[l, rows, lanes(u + 2 * UNITS)]
-                scores = mm(query.astype(BF), stacked(key, masks), NT)
+            columns = [lanes(part * wide + c) for part in range(3)]
+            cells = [joined[l, :, at] for at in columns]
+            convs = []
+            for at, value in zip(columns, cells):
+                conv = depthwise(value.reshape(20, SUB, LANE), dwp[l, :, at], 5)
+                convs.append((conv.reshape(ROWS, LANE) * keep).astype(BF))
+            linears = [mm(conv, blocks_bd[l, part * wide + c]) for part, conv in enumerate(convs)]
+            results = []
+            for query, key, value in (cells, linears):
+                results.append((softplus(query), softplus(key) * keep, value))
+            for part in range(3):
+                s0[l, :, columns[part]] = convs[part]
+                for source in range(2):
+                    tvals[l, :, lanes(part * UNITS + source * wide + c)] = results[source][part]
+
+        groups(wide, 1, chunks, True)
+
+        def units(first):
+            places = [(first + k, start, size) for k in range(UNIT_STEP) for start, size in BLOCKS]
+            inputs = [
+                [tvals[l, start : start + size, lanes(u + part * UNITS)] for part in range(3)]
+                for u, start, size in places
+            ]
+            weights = []
+            for (_, start, size), (query, key, value) in zip(places, inputs):
+                ones = jnp.ones_like(value)
                 if start == SMALL:
-                    scores = scores * smask[...]
-                both = jnp.concatenate(
-                    [stacked(value, masks), stacked(jnp.ones_like(value), masks)], axis=1
-                )
-                sums = mm(scores.astype(BF), both)
-                inverse = 1.0 / sums[:, LANE:]
-                rden[l, rows, lanes(u)] = inverse
-                mixo[l, rows, lanes(u)] = sums[:, :LANE] * inverse
-            return carry
-
-        lax.fori_loop(0, UNITS, unit, 0)
+                    scores = mm(query.astype(BF), stacked(key), NT) * smask[...]
+                    weights.append((scores, jnp.concatenate([stacked(value), stacked(ones)], axis=1)))
+                else:
+                    state = mm(key.astype(BF), joint(value, ones), TN) * diag[...]
+                    weights.append((query, state.astype(BF)))
+            sums = [mm(left.astype(BF), right) for left, right in weights]
+            results = []
+            for value in sums:
+                inverse = 1.0 / value[:, LANE:]
+                results.append((inverse, value[:, :LANE] * inverse))
+            for (u, start, size), (inverse, mixed) in zip(places, results):
+                rden[l, start : start + size, lanes(u)] = inverse
+                mixo[l, start : start + size, lanes(u)] = mixed
+
+        groups(UNITS, UNIT_STEP, units)
         loads[1, l].wait()
         branch[...] = mm(mixo[l].astype(BF), proj_ref[l])
 
@@ -543,7 +642,7 @@
         loads[2, l].wait()
         pre_u[l] = mm(hid[s], inv_ref[l])
 
-        def chunk(j, carry):
+        def chunk(j):
             at = lanes(j)
             pre = pre_u[l, :, at] + ibias_ref[:, at].astype(F32)[l : l + 1]
             value, slope = silu_parts(pre)
@@ -554,9 +653,8 @@
             out, out_slope = silu_parts(conv + mbias_ref[:, at].astype(F32)[l : l + 1])
             act[l, :, at] = (out * rmask[...]).astype(BF)
             act_d[l, :, at] = out_slope.astype(BF)
-            return carry
-
-        lax.fori_loop(0, expanded // LANE, chunk, 0)
+
+        loop(expanded // LANE, EXPAND_STEP, chunk)
         loads[3, l].wait()
         branch[...] = mm(act[l], point_ref[l])
 
@@ -597,11 +695,10 @@
             local_sum = vectors[3]
 
     def small_row(name, l, row, value, at):
-        jobs[name, l].own[row // 32, row // SUB % 4, row % SUB : row % SUB + 1, at] = value
+        jobs[name, l].stage[row // SUB, row % SUB : row % SUB + 1, at] = value
 
     def expand_row(l, j, tap, value):
-        block = j // wide
-        jobs["mb", l].own[block // 2, block % 2 * 2 + tap // SUB, tap % SUB : tap % SUB + 1, lanes(j % wide)] = value
+        jobs["mb", l].stage[j // wide * 2 + tap // SUB, tap % SUB : tap % SUB + 1, lanes(j % wide)] = value
 
     def matrix(name, l, left, right, columns):
         own = jobs[name, l].own
@@ -614,85 +711,99 @@
     def attention_backward(l, s, grad_branch, pause):
         gmix[...] = mm(grad_branch, proj_ref[l], NT).astype(BF).astype(F32)
         matrix("proj", l, grad_t[...], lambda cut: mixo[l, :, cut].astype(BF), mixo.shape[2])
-        pause(0)
-
-        def unit(u, carry):
-            for start, size in BLOCKS:
+        pause("t0", l)
+
+        def units(first):
+            places = [(first + k, start, size) for k in range(UNIT_STEP) for start, size in BLOCKS]
+            inputs = []
+            for u, start, size in places:
                 rows = slice(start, start + size)
-                query = tvals[l, rows, lanes(u)]
-                key = tvals[l, rows, lanes(u + UNITS)]
-                value = tvals[l, rows, lanes(u + 2 * UNITS)]
                 down = gmix[rows, lanes(u)] * rden[l, rows, lanes(u)]
-                level = -down * mixo[l, rows, lanes(u)]
+                inputs.append(
+                    [tvals[l, rows, lanes(u + part * UNITS)] for part in range(3)]
+                    + [down, -down * mixo[l, rows, lanes(u)]]
+                )
+            products = []
+            for (_, start, size), (query, key, value, down, level) in zip(places, inputs):
                 ones = jnp.ones_like(value)
-                key_stack, query_stack, down_stack = (
-                    stacked(key, masks),
-                    stacked(query, masks),
-                    stacked(down, masks),
-                )
-                grad_scores = mm(
-                    jnp.concatenate([down, level], axis=1).astype(BF),
-                    jnp.concatenate([stacked(value, masks), stacked(ones, masks)], axis=1),
-                    NT,
-                )
-                grad_scores_t = mm(
-                    jnp.concatenate([value, ones], axis=1).astype(BF),
-                    jnp.concatenate([down_stack, stacked(level, masks)], axis=1),
-                    NT,
-                )
-                scores_t = mm(key.astype(BF), query_stack, NT)
                 if start == SMALL:
                     inside = smask[...]
-                    grad_scores = grad_scores * inside
-                    grad_scores_t = grad_scores_t * inside
-                    scores_t = scores_t * inside
-                grad_query = mm(grad_scores.astype(BF), key_stack)
-                grad_key = mm(grad_scores_t.astype(BF), query_stack)
-                grad_value = mm(scores_t.astype(BF), down_stack)
-                dvals[rows, lanes(u)] = grad_query * (1.0 - jnp.exp(-query))
-                dvals[rows, lanes(u + UNITS)] = grad_key * (1.0 - jnp.exp(-key))
-                dvals[rows, lanes(u + 2 * UNITS)] = grad_value
-            return carry
-
-        lax.fori_loop(0, UNITS, unit, 0)
-        pause(1)
-
-        def chunk(j, carry):
-            at = lanes(j)
-            part = j // wide
-            slot = part * UNITS + j % wide
-            grad_spread = dvals[:, lanes(slot + wide)].astype(BF)
-            block = jnp.where(on_diag, mm(s0[l, :, at], grad_spread, TN), 0.0)
-            block = block[0:32] + block[32:64] + block[64:96] + block[96:128]
-            jobs["att", l].own[1, :, :, at] = block.reshape(4, SUB, LANE)
-            grad_conv = mm(grad_spread, blocks_bd[l, j], NT).reshape(20, SUB, LANE)
-            cells = joined[l, :, at].reshape(20, SUB, LANE)
-            for tap, row in enumerate(depthwise_taps(cells, grad_conv, 5)):
-                small_row("att", l, tap, row, at)
-            back = depthwise(grad_conv, dwp[l, :, at], 5, flip=True).reshape(ROWS, LANE)
-            mid[:, at] = (dvals[:, lanes(slot)] + back * rmask[...]).astype(BF)
-            return carry
-
-        lax.fori_loop(0, 3 * wide, chunk, 0)
+                    query_stack, down_stack = stacked(query), stacked(down)
+                    grad_scores = mm(
+                        joint(down, level), jnp.concatenate([stacked(value), stacked(ones)], axis=1), NT
+                    )
+                    grad_scores_t = mm(
+                        joint(value, ones), jnp.concatenate([down_stack, stacked(level)], axis=1), NT
+                    )
+                    scores_t = mm(key.astype(BF), query_stack, NT)
+                    products.append((
+                        (grad_scores * inside, stacked(key)),
+                        (grad_scores_t * inside, query_stack),
+                        (scores_t * inside, down_stack),
+                    ))
+                else:
+                    both, slopes = joint(value, ones), joint(down, level)
+                    state_t = mm(both, key.astype(BF), TN) * diag_t[...]
+                    grad_state_t = mm(slopes, query.astype(BF), TN) * diag_t[...]
+                    grad_state = mm(query.astype(BF), down.astype(BF), TN) * diag[:, 0:LANE]
+                    products.append((
+                        (slopes, state_t.astype(BF)), (both, grad_state_t.astype(BF)), (key, grad_state.astype(BF))
+                    ))
+            results = []
+            for (query, key, *_), pairs in zip(inputs, products):
+                grad_query, grad_key, grad_value = (mm(left.astype(BF), right) for left, right in pairs)
+                results.append(
+                    (grad_query * (1.0 - jnp.exp(-query)), grad_key * (1.0 - jnp.exp(-key)), grad_value)
+                )
+            for (u, start, size), grads in zip(places, results):
+                for part, grad in enumerate(grads):
+                    dvals[start : start + size, lanes(u + part * UNITS)] = grad
+
+        groups(UNITS, UNIT_STEP, units)
+        pause("t2", l)
+
+        def chunks(c):
+            keep = rmask[...]
+            columns = [lanes(part * wide + c) for part in range(3)]
+            slots = [part * UNITS + c for part in range(3)]
+            grads = [dvals[:, lanes(slot + wide)].astype(BF) for slot in slots]
+            direct = [dvals[:, lanes(slot)] for slot in slots]
+            cells = [joined[l, :, at].reshape(20, SUB, LANE) for at in columns]
+            convs = [
+                mm(grad, blocks_bd[l, part * wide + c], NT).reshape(20, SUB, LANE) for part, grad in enumerate(grads)
+            ]
+            blocks = [mm(s0[l, :, at], grad, TN) * diag[:, 0:LANE] for at, grad in zip(columns, grads)]
+            taps_of, grads_of = [], []
+            for part, conv in enumerate(convs):
+                back = depthwise(conv, dwp[l, :, columns[part]], 5, flip=True).reshape(ROWS, LANE)
+                taps_of.append(depthwise_taps(cells[part], conv, 5))
+                grads_of.append((direct[part] + back * keep).astype(BF))
+            for at, block, taps, joined_grad in zip(columns, blocks, taps_of, grads_of):
+                block = block[0:32] + block[32:64] + block[64:96] + block[96:128]
+                jobs["att", l].stage[4:8, :, at] = block.reshape(4, SUB, LANE)
+                for tap, row in enumerate(taps):
+                    small_row("att", l, tap, row, at)
+                mid[:, at] = joined_grad
+            natural = mm(jnp.concatenate(grads_of, axis=1), perm[...], NT).astype(BF)
+            matrix(f"qkv{c}", l, hid_t[s], lambda cut: natural, width)
+            pause(f"c{c}", l)
+
+        groups(wide, 1, chunks, True)
         jobs["att", l].start()
+        pause("t5", l)
         grad_hidden = mm(mid[:, : 3 * width], wp[l], NT)
 
         def gradients():
-            def natural(cut):
-                c = cut.start // width
-                piece = jnp.concatenate([mid[:, lanes(part * wide + c)] for part in range(3)], axis=1)
-                return mm(piece, perm[...], NT).astype(BF)
-
-            matrix("qkv", l, hid_t[s], natural, 3 * width)
+            pass
 
         return grad_hidden, gradients
 
     def expand_backward(l, s, grad_branch, pause):
         gact[:, 0:expanded] = mm(grad_branch, point_ref[l], NT).astype(BF).astype(F32)
         matrix("point", l, grad_t[...], lambda cut: act[l, :, cut], expanded)
-        pause(0)
-
-        def chunk(j, carry):
+        pause("m0", l)
+
+        def chunk(j):
             at = lanes(j)
             grad_conv = gact[:, at] * act_d[l, :, at].astype(F32)
             expand_row(l, j, 9, column_sum(grad_conv))
@@ -704,11 +815,10 @@
             grad_pre = (back * pre_d[l, :, at].astype(F32)).astype(BF)
             mid[:, at] = grad_pre
             expand_row(l, j, 10, column_sum(grad_pre.astype(F32)))
-            return carry
-
-        lax.fori_loop(0, expanded // LANE, chunk, 0)
+
+        loop(expanded // LANE, EXPAND_STEP, chunk)
         jobs["mb", l].start()
-        pause(1)
+        pause("m2", l)
         grad_hidden = mm(mid[...], inv_ref[l], NT)
 
         def gradients():
@@ -716,21 +826,10 @@
 
         return grad_hidden, gradients
 
-    queue = []
-
-    def advance():
-        for entry in queue:
-            if entry[1]:
-                entry[1].pop(0)()
-
-    def enter(job):
-        steps = [job.step1, job.step2, job.step3]
-        if isinstance(job, Small):
-            steps.append(job.step4)
-        queue.append((job, steps + [job.finish]))
-
-    def pause(k):
-        advance()
+    def pause(moment, l):
+        for step in PLAN.get((moment, l), ()):
+            name, number, method = step.split(".")
+            getattr(jobs[name, int(number)], method)()
 
     for s in range(stages - 1, -1, -1):
         l = s // 2
@@ -739,6 +838,7 @@
             cross, total = first_cross, first_total
         else:
             cross, total = exchange_finish(stages + s, 2)
+        pause("begin", s)
         if s % 2 == 0:
             small_row("att", l, 25, local_cross, slice(0, width))
             small_row("att", l, 25, local_sum, slice(width, 2 * width))
@@ -757,18 +857,16 @@
         if s > 0:
             local_cross, local_sum = column_sum(after * normed[s - 1]), column_sum(after)
             exchange_start(stages + s - 1, [local_cross, local_sum])
+        pause("sent", s)
         gradients()
-        advance()
-        for name in ("att", "proj", "qkv") if s % 2 == 0 else ("mb", "point", "inv"):
-            enter(jobs[name, l])
+        pause("done", s)
         if s == last:
             at["out_x"][...] = mm(spread, hid[stages], TN).astype(BF)
 
     at["out_g"][...] = mm(spread, gnow[...].astype(BF), TN).astype(BF)
-    while any(steps for _, steps in queue):
-        advance()
-    for job, _ in queue:
-        job.drain()
+    for job in jobs.values():
+        if isinstance(job, Reduction):
+            job.drain()
     for e in range(2 * stages - 1):
         rows = slot_rows(4 if e == last else 2)
         wait_bytes(exbuf.at[e, 0 : n_dp - 1, 0:rows], send_sem.at[e])
@@ -789,7 +887,7 @@
     return columns
 
 
-def arrange(layers, wide, shares, x_in, g_in, qkv_in, proj_in, inv_in, point_in, att_in, mb_in,
+def arrange(layers, wide, shares, x_in, g_in, attcols_in, mbcols_in, att_in, mb_in,
             x_out, g_out, qkv_out, proj_out, inv_out, point_out, dw_out, group_out, ibias_out, mdw_out, mbias_out,
             gain_out, shift_out):
     width = wide * LANE
@@ -798,16 +896,15 @@
     g_out[...] = g_in[...]
     taps, mtaps = dw_out.shape[0], mdw_out.shape[0]
     for l in range(layers):
-        qkv_out[l] = jnp.transpose(jnp.concatenate([qkv_in[l], jnp.zeros((32, qkv_in.shape[2]), F32)], axis=0))[
-            0:share_qkv, 0 : qkv_in.shape[1]
-        ]
-        proj_out[l] = jnp.transpose(jnp.concatenate([proj_in[l], jnp.zeros((32, proj_in.shape[2]), F32)], axis=0))[
-            0:share_proj, 0 : proj_in.shape[1]
-        ]
-        inv_out[l] = inv_in[l, :, 0:share_inv]
-        point_out[l] = jnp.transpose(jnp.concatenate([point_in[l], jnp.zeros((32, point_in.shape[2]), F32)], axis=0))[
-            0:share_point, 0 : point_in.shape[1]
-        ]
+        rows = attcols_in.shape[1]
+        values = []
+        for value, share in ((attcols_in[l], share_qkv), (mbcols_in[l], share_inv)):
+            value = jnp.concatenate([value, jnp.zeros((padded(rows) - rows, value.shape[1]), F32)], axis=0)
+            values += [value, pltpu.roll(value, value.shape[1] - share, 1)]
+        qkv_out[l] = jnp.transpose(values[0])[0:share_qkv, 0:rows]
+        proj_out[l] = jnp.transpose(values[1])[0:share_proj, 0:rows]
+        inv_out[l] = values[2][0:rows, 0:share_inv]
+        point_out[l] = jnp.transpose(values[3])[0:share_point, 0:rows]
         natural = unsplit(att_in[l], wide)
         for j, column in enumerate(natural):
             for t in range(taps):
@@ -843,7 +940,7 @@
     rows = width // 2 // n_pipe
     vmem = pl.BlockSpec(memory_space=pltpu.VMEM)
     hbm = pl.BlockSpec(memory_space=pl.ANY)
-    columns = {"qkv": joined_width, "proj": mixed_width, "inv": expanded, "point": expanded}
+    columns = {"qkv0": width, "qkv1": width, "qkv2": width, "proj": mixed_width, "inv": expanded, "point": expanded}
     small_columns = {"att": joined_width, "mb": width}
     outs = {
         "out_x": jax.ShapeDtypeStruct((tokens, width), BF),
@@ -861,6 +958,8 @@
         "mdwp": pltpu.VMEM((layers, 16, expanded), F32),
         "rmask": pltpu.VMEM((ROWS, LANE), F32),
         "smask": pltpu.VMEM((48, 192), F32),
+        "diag": pltpu.VMEM((LANE, 2 * LANE), F32),
+        "diag_t": pltpu.VMEM((2 * LANE, LANE), F32),
         "hid": pltpu.VMEM((stages + 1, ROWS, width), BF),
         "hid_t": pltpu.VMEM((stages, width, ROWS), BF),
         "grad_t": pltpu.VMEM((width, ROWS), BF),
@@ -881,32 +980,35 @@
         "gnow": pltpu.VMEM((ROWS, width), F32),
         "stats": pltpu.VMEM((8, width), F32),
         "exbuf": pltpu.VMEM((2 * stages - 1, n_dp, 2 * SUB, LANE), F32),
-        "whole": pltpu.VMEM((rows, expanded), F32),
+        "whole": pltpu.VMEM((rows, 2 * expanded), F32),
         "send_sem": pltpu.SemaphoreType.DMA((2 * stages - 1,)),
         "recv_sem": pltpu.SemaphoreType.DMA((2 * stages - 1,)),
         "load_sem": pltpu.SemaphoreType.DMA((4, layers)),
-        "red_send": pltpu.SemaphoreType.DMA((KINDS * 6 * layers,)),
-        "red_recv": pltpu.SemaphoreType.DMA((KINDS * 6 * layers,)),
+        "red_send": pltpu.SemaphoreType.DMA((KINDS * JOBS * layers + 2 * layers,)),
+        "red_recv": pltpu.SemaphoreType.DMA((KINDS * JOBS * layers + 2 * layers,)),
     }
     for name in MATRICES:
         n = columns[name]
-        share = padded(n // n_dp)
-        outs[f"out_{name}"] = jax.ShapeDtypeStruct((layers, 2 * rows, share), F32)
         scratch[f"{name}_own"] = pltpu.VMEM((layers, 2, n_pipe, rows, n), BF)
         scratch[f"{name}_pair"] = pltpu.VMEM((layers, n_pipe, rows, n), BF)
         scratch[f"{name}_first"] = pltpu.VMEM((layers, 2, rows, n), BF)
         scratch[f"{name}_second"] = pltpu.VMEM((layers, rows, n), BF)
+    shares = tuple(n // n_dp for n in (joined_width, mixed_width, expanded, expanded))
+    for name, share in (("attcols", padded(shares[0] + shares[1])), ("mbcols", padded(shares[2] + shares[3]))):
+        outs[f"out_{name}"] = jax.ShapeDtypeStruct((layers, 2 * rows, share), F32)
         scratch[f"{name}_outgoing"] = pltpu.VMEM((n_dp, rows, share), BF)
         scratch[f"{name}_landed"] = pltpu.VMEM((layers, n_dp, rows, share), BF)
     for name in SMALLS:
         n = small_columns[name]
         outs[f"out_{name}"] = jax.ShapeDtypeStruct((layers, 8 * SUB, n), F32)
-        scratch[f"{name}_own"] = pltpu.VMEM((layers, 2, n_pipe, SUB, n), F32)
-        scratch[f"{name}_pair"] = pltpu.VMEM((layers, n_pipe, SUB, n), F32)
-        scratch[f"{name}_first"] = pltpu.VMEM((layers, 2, SUB, n), F32)
-        scratch[f"{name}_second"] = pltpu.VMEM((layers, SUB, n), F32)
-        scratch[f"{name}_along"] = pltpu.VMEM((layers, n_dp // 2, SUB, n), F32)
-        scratch[f"{name}_everywhere"] = pltpu.VMEM((layers, 2 * n_pipe, SUB, n), F32)
+        half, rows_in, kind = (padded(n // 2), 2 * SUB, BF) if name == "att" else (n, SUB, F32)
+        scratch[f"{name}_stage"] = pltpu.VMEM((8, SUB, n), F32)
+        scratch[f"{name}_own"] = pltpu.VMEM((layers, 2, n_pipe, rows_in, half), kind)
+        scratch[f"{name}_pair"] = pltpu.VMEM((layers, n_pipe, rows_in, half), kind)
+        scratch[f"{name}_first"] = pltpu.VMEM((layers, 2, rows_in, half), kind)
+        scratch[f"{name}_second"] = pltpu.VMEM((layers, rows_in, half), kind)
+        scratch[f"{name}_along"] = pltpu.VMEM((layers, n_dp // 2, rows_in, half), kind)
+        scratch[f"{name}_everywhere"] = pltpu.VMEM((layers, 2 * n_pipe, rows_in, half), kind)
     results = pl.pallas_call(
         functools.partial(kernel, n_dp, n_pipe, 13, tuple(outs) + tuple(scratch)),
         out_shape=tuple(outs.values()),
@@ -931,7 +1033,6 @@
         bn_gain,
         bn_bias,
     )
-    shares = tuple(columns[name] // n_dp for name in MATRICES)
     taps, mtaps = att_dw.shape[1], mb_dw.shape[1]
     arranged = pl.pallas_call(
         functools.partial(arrange, layers, width // LANE, shares),
@@ -950,7 +1051,7 @@
             jax.ShapeDtypeStruct((stages, width), F32),
             jax.ShapeDtypeStruct((stages, width), F32),
         ),
-        in_specs=[vmem] * 8,
+        in_specs=[vmem] * 6,
         out_specs=(vmem,) * 13,
     )(*results)
     x_out, g_out, qkv, proj, inv, point, dw, group, ibias, mdw, mbias, gain, shift = arranged

time: 151 us -> 106 us (0.70)
  Pallas kernels: 144 us -> 98.7 us
    pallas_call x1, Pallas kernels: 141 us -> 95.7 us  [body(): pl.pallas_call(functools.partial(kernel, n_dp, n_pipe, 13, tuple(outs) +...]
where the time goes in v3:
time: 106 us; the launch traced here: 105 us
  Pallas kernels  98.7 us (93%)
  local copies, waits for them, and re-layouts  5.8 us (5%)
    pallas_call x1, Pallas kernels, body(): pl.pallas_call(functools.partial(kernel, n_dp, n_pipe, 13, tuple(outs) +...  95.7 us
    unnamed x2, local copies, waits for them, and re-layouts  4.38 us
    pallas_call x1, Pallas kernels, body(): pl.pallas_call(functools.partial(arrange, layers, width // LANE, shares),...  2.96 us

profile of v3, /device:TPU:0, one launch (start us, length us, event | category | flops | bytes accessed | tf_op | source)
XLA Modules:
  0.0 105.1 jit_solution(4106332816713040980)
XLA Ops:
  0.6 2.9 %copy.28.refs_4_ = bf16[2,36,32,32]{3,2,1,0:T(8,128)(2,1)} copy(bf16[2,36,32,32]{1,3,2,0:T(8,128)(2,1)} %param.17) | data formatting | bytes 294912 | tf_op args[4]
  3.5 95.7 %shard_map.228 = (bf16[134,384]{1,0:T(8,128)(2,1)}, bf16[134,384]{1,0:T(8,128)(2,1)}, f32[2,96,256]{2,1,0:T(8,128)}, f32[2,96,384]{2,1,0:T(8,128)}, f32[2,64,1152]{2,1,0:T(8,128)}, /*index=5*/f32[2,64,384]{2,1,0:T(8,128)}) custom-call(bf16[134,384]{1,0:T(8,128)(2,1)} %bitcast.12, bf16[134,384]{1,0:T(8,128)(2,1)} %bitcast.13, bf16[2,384,1152]{2,1,0:T(8,128)(2,1)} %refs_2_.1, ...), custom_call_target="tpu_custom_call" | custom-call | tf_op jit(solution)/shard_map/pallas_call | solution.py:1012
  99.3 3.0 %shard_map.229 = (bf16[134,384]{1,0:T(8,128)(2,1)}, bf16[134,384]{1,0:T(8,128)(2,1)}, f32[2,144,96]{2,1,0:T(8,128)}, f32[2,96,96]{2,1,0:T(8,128)}, f32[2,96,192]...) custom-call(bf16[134,384]{1,0:T(8,128)(2,1)} %get-tuple-element.32.x, ...), custom_call_target="tpu_custom_call" | custom-call | tf_op jit(solution)/shard_map/pallas_call | solution.py:1037
  102.2 1.4 %reshape.45 = f32[2,32,36,32]{3,2,1,0:T(8,128)S(1)} reshape(f32[2,32,1152]{2,1,0:T(8,128)} %get-tuple-element.42) | data formatting | bytes 589824 | tf_op jit(solution)/shard_map/reshape | solution.py:1064
  103.7 1.5 %copy.29 = f32[2,36,32,32]{1,3,2,0:T(8,128)} copy(f32[2,36,32,32]{3,1,2,0:T(8,128)S(1)} %bitcast.10) | data formatting | bytes 589824

commit v4 on v3

--- a/solution.py
+++ b/solution.py
@@ -1,4 +1,5 @@
 import functools
+from types import SimpleNamespace
 
 import jax
 import jax.numpy as jnp
@@ -187,7 +188,8 @@
 
 
 class Reduction:
-    def __init__(self, place, own, pair, first, second, send_sem, recv_sem, base):
+    def __init__(self, direct, place, own, pair, first, second, send_sem, recv_sem, base):
+        self.direct = direct
         self.place, self.own, self.pair, self.first, self.second = place, own, pair, first, second
         self.send_sem, self.recv_sem, self.base = send_sem, recv_sem, base
 
@@ -214,18 +216,32 @@
         peer = at.pipe + (2 - at.core) * (1 - 2 * at.bit2)
         return self.copy(self.own.at[at.core, at.slab(at.bit1, 1 - at.bit2)], self.second, 3, peer, at.dp)
 
+    def to_segment(self, k):
+        at = self.place
+        peer = lax.rem(at.pipe + k, self.pair.shape[0])
+        target = self.second if k == 3 else self.first.at[k - 1]
+        return self.copy(self.own.at[at.core, peer], target, k, peer, at.dp)
+
     def start(self):
         self.to_pair().start()
 
     def step1(self):
         at = self.place
         self.to_pair().wait_recv()
+        if self.direct:
+            for k in (2, 1, 3):
+                slab = lax.rem(at.pipe + k, self.pair.shape[0])
+                self.own[at.core, slab] = self.own[at.core, slab] + self.pair[slab]
+                self.to_segment(k).start()
+            return
         for bit in range(2):
             slab = at.slab(1 - at.bit1, bit)
             self.own[at.core, slab] = self.own[at.core, slab] + self.pair[slab]
             self.to_first(bit).start()
 
     def step2(self):
+        if self.direct:
+            return
         at = self.place
         for bit in range(2):
             self.to_first(bit).wait_recv()
@@ -237,13 +253,29 @@
 
     def part(self):
         at = self.place
+        slab = at.pipe
+        if self.direct:
+            total = self.own[at.core, slab].astype(F32) + self.pair[slab].astype(F32)
+            for k in (1, 2, 3):
+                self.to_segment(k).wait_recv()
+                total = total + (self.second[...] if k == 3 else self.first[k - 1]).astype(F32)
+            return total
         self.to_second().wait_recv()
-        slab = at.pipe
         total = self.own[at.core, slab].astype(F32) + self.pair[slab].astype(F32)
         return total + self.first[at.bit2].astype(F32) + self.second[...].astype(F32)
 
+    def do(self, step):
+        (None, self.step1, self.step2, self.step3, self.step4, self.finish)[step]()
+
+    step3 = step4 = finish = None
+
     def drain(self):
-        for made in (self.to_pair(), self.to_first(0), self.to_first(1), self.to_second()):
+        self.to_pair().wait_send()
+        if self.direct:
+            rest = [self.to_segment(k) for k in (1, 2, 3)]
+        else:
+            rest = [self.to_first(0), self.to_first(1), self.to_second()]
+        for made in rest:
             made.wait_send()
 
 
@@ -264,6 +296,12 @@
         self.place, self.matrices, self.shares = place, matrices, shares
         self.send_sem, self.recv_sem = send_sem.at[base], recv_sem.at[base]
         self.outgoing, self.landed, self.whole, self.result = outgoing, landed, whole, result
+
+    def do(self, step):
+        if step == SEND:
+            self.send()
+        else:
+            self.finish()
 
     def send(self):
         at = self.place
@@ -397,35 +435,44 @@
         wait_bytes(self.everywhere.at[0 : parts - 1], self.send_sem.at[self.base + 5])
 
 
+QKV, PROJ, INV, POINT, ATT, MB, ATT_COLUMNS, MB_COLUMNS = 0, 3, 4, 5, 6, 7, 8, 9
+MATRICES, SMALLS = 6, 2
+JOBS = MATRICES + SMALLS
+DIRECT = ()
+SEND, FINISH = 0, 5
+BEGIN, M_START, M_CHUNKS, T_START, T_UNITS, T_CHUNKS, SENT, DONE = 0, 1, 2, 3, 4, 5, 8, 9
 PLAN = {
-    ("m2", 1): ("point.1.step1",),
-    ("done", 3): ("mb.1.step1",),
-    ("begin", 2): ("inv.1.step1",),
-    ("t0", 1): ("point.1.step2", "mb.1.step2",),
-    ("t2", 1): ("proj.1.step1",),
-    ("c0", 1): (),
-    ("c1", 1): (),
-    ("c2", 1): ("inv.1.step2", "qkv0.1.step1",),
-    ("sent", 2): ("mb.1.step3", "qkv1.1.step1",),
-    ("done", 2): ("qkv2.1.step1", "proj.1.step2", "att.1.step1",),
-    ("begin", 1): ("mbcols.1.send", "qkv0.1.step2",),
-    ("m0", 0): ("qkv1.1.step2", "qkv2.1.step2", "att.1.step2",),
-    ("m2", 0): ("point.0.step1", "mb.1.step4",),
-    ("sent", 1): ("att.1.step3", "attcols.1.send",),
-    ("done", 1): ("mb.0.step1", "mb.1.finish",),
-    ("begin", 0): ("inv.0.step1", "mbcols.1.finish",),
-    ("t0", 0): ("point.0.step2", "mb.0.step2", "att.1.step4",),
-    ("t2", 0): ("proj.0.step1",),
-    ("c0", 0): ("mb.0.step3",),
-    ("c1", 0): ("qkv0.0.step1", "inv.0.step2",),
-    ("c2", 0): ("qkv1.0.step1", "attcols.1.finish", "att.1.finish",),
-    ("sent", 0): ("qkv2.0.step1", "att.0.step1", "proj.0.step2", "mb.0.step4", "qkv0.0.step2", "mbcols.0.send",),
-    ("done", 0): ("att.0.step2", "qkv1.0.step2", "qkv2.0.step2", "att.0.step3", "attcols.0.send", "att.0.step4", "mb.0.finish", "mbcols.0.finish", "attcols.0.finish", "att.0.finish",),
+    (M_CHUNKS, 3): ((POINT, 1, 1),),
+    (DONE, 3): ((MB, 1, 1), (INV, 1, 1),),
+    (BEGIN, 2): (),
+    (T_START, 2): ((POINT, 1, 2), (MB, 1, 2),),
+    (T_UNITS, 2): ((PROJ, 1, 1),),
+    (T_CHUNKS, 2): (),
+    (T_CHUNKS + 1, 2): (),
+    (T_CHUNKS + 2, 2): ((INV, 1, 2), (QKV, 1, 1),),
+    (SENT, 2): ((MB, 1, 3), (QKV + 1, 1, 1),),
+    (DONE, 2): ((QKV + 2, 1, 1), (PROJ, 1, 2), (ATT, 1, 1),),
+    (BEGIN, 1): ((MB_COLUMNS, 1, SEND), (QKV, 1, 2),),
+    (M_START, 1): ((QKV + 1, 1, 2), (QKV + 2, 1, 2), (ATT, 1, 2),),
+    (M_CHUNKS, 1): ((POINT, 0, 1), (MB, 1, 4),),
+    (SENT, 1): ((ATT, 1, 3), (ATT_COLUMNS, 1, SEND),),
+    (DONE, 1): ((MB, 0, 1), (INV, 0, 1), (MB, 1, FINISH),),
+    (BEGIN, 0): ((MB_COLUMNS, 1, FINISH),),
+    (T_START, 0): ((POINT, 0, 2), (MB, 0, 2), (ATT, 1, 4),),
+    (T_UNITS, 0): ((PROJ, 0, 1),),
+    (T_CHUNKS, 0): ((MB, 0, 3),),
+    (T_CHUNKS + 1, 0): ((INV, 0, 2), (QKV, 0, 1),),
+    (T_CHUNKS + 2, 0): ((QKV + 1, 0, 1), (ATT_COLUMNS, 1, FINISH), (ATT, 1, FINISH),),
+    (SENT, 0): (
+        (QKV + 2, 0, 1), (ATT, 0, 1), (PROJ, 0, 2), (MB, 0, 4), (QKV, 0, 2), (MB_COLUMNS, 0, SEND),
+    ),
+    (DONE, 0): (
+        (ATT, 0, 2), (QKV + 1, 0, 2), (QKV + 2, 0, 2), (ATT, 0, 3), (ATT_COLUMNS, 0, SEND), (ATT, 0, 4),
+        (MB, 0, FINISH), (MB_COLUMNS, 0, FINISH),
+        (ATT_COLUMNS, 0, FINISH), (ATT, 0, FINISH),
+    ),
 }
 KINDS = 6
-MATRICES = ("qkv0", "qkv1", "qkv2", "proj", "inv", "point")
-SMALLS = ("att", "mb")
-JOBS = len(MATRICES) + len(SMALLS)
 
 
 def kernel(n_dp, n_pipe, count_in, names, *refs):
@@ -433,17 +480,18 @@
         x_ref, ct_ref, qkv_hbm, dw_ref, group_ref, proj_hbm, inv_hbm, ibias_ref, mdw_ref, mbias_ref, point_hbm,
         gain_ref, shift_ref,
     ) = refs[:count_in]
-    at = dict(zip(names, refs[count_in:]))
+    refs_of = dict(zip(names, refs[count_in:]))
+    at = SimpleNamespace(**{name: ref for name, ref in refs_of.items() if isinstance(name, str)})
     (
-        inv_own, proj_ref, inv_ref, point_ref, perm, rowperm, wp, blocks_bd, dwp, mdwp, rmask, smask, diag, diag_t, hid, hid_t,
-        grad_t, normed, mixo, rden, tvals, joined, s0, dvals, gmix, pre_u, pre_d, act, act_d, mid, gact, branch,
-        gnow, stats, exbuf, send_sem, recv_sem, load_sem, red_send, red_recv, whole,
-    ) = (at[name] for name in (
-        "inv_own", "proj", "inv", "point", "perm", "rowperm", "wp", "blocks_bd", "dwp", "mdwp", "rmask", "smask", "diag", "diag_t", "hid",
-        "hid_t", "grad_t", "normed", "mixo", "rden", "tvals", "joined", "s0", "dvals", "gmix", "pre_u", "pre_d",
-        "act", "act_d", "mid", "dvals", "branch", "gnow", "stats", "exbuf", "send_sem", "recv_sem", "load_sem",
-        "red_send", "red_recv", "whole",
-    ))
+        inv_own, proj_ref, inv_ref, point_ref, perm, rowperm, wp, blocks_bd, dwp, mdwp, rmask, smask, diag, diag_t,
+        hid, hid_t, grad_t, normed, mixo, rden, tvals, joined, s0, dvals, gmix, pre_u, pre_d, act, act_d, mid,
+        gact, branch, gnow, stats, exbuf, send_sem, recv_sem, load_sem, red_send, red_recv, whole,
+    ) = (
+        refs_of[INV, 0], at.proj, at.inv, at.point, at.perm, at.rowperm, at.wp, at.blocks_bd, at.dwp, at.mdwp, at.rmask,
+        at.smask, at.diag, at.diag_t, at.hid, at.hid_t, at.grad_t, at.normed, at.mixo, at.rden, at.tvals,
+        at.joined, at.s0, at.dvals, at.gmix, at.pre_u, at.pre_d, at.act, at.act_d, at.mid, at.dvals, at.branch,
+        at.gnow, at.stats, at.exbuf, at.send_sem, at.recv_sem, at.load_sem, at.red_send, at.red_recv, at.whole,
+    )
     place = Place()
     me = place.dp
     layers = proj_ref.shape[0]
@@ -488,22 +536,23 @@
 
     jobs = {}
     for l in range(layers):
-        for i, name in enumerate(MATRICES + SMALLS):
-            refs_of = [at[f"{name}_{kind}"].at[l] for kind in ("own", "pair", "first", "second")]
-            base = KINDS * (JOBS * l + i)
-            if name in SMALLS:
-                rest = [at[f"{name}_stage"]] + [at[f"{name}_{kind}"].at[l] for kind in ("along", "everywhere")]
-                jobs[name, l] = Small(place, *refs_of, red_send, red_recv, base, *rest, at[f"out_{name}"].at[l])
+        for job in range(JOBS):
+            base = KINDS * (JOBS * l + job)
+            buffers = [refs_of[job, kind].at[l] for kind in range(4)]
+            given = ((job, l) in DIRECT, place, *buffers, red_send, red_recv, base)
+            if job < MATRICES:
+                jobs[job, l] = Reduction(*given)
             else:
-                jobs[name, l] = Reduction(place, *refs_of, red_send, red_recv, base)
-        for i, (name, members, sizes) in enumerate((
-            ("attcols", (("qkv0", "qkv1", "qkv2"), ("proj",)), (3 * width, proj_ref.shape[1])),
-            ("mbcols", (("inv",), ("point",)), (expanded, expanded)),
-        )):
-            jobs[name, l] = Columns(
+                rest = (refs_of[job, 6], refs_of[job, 4].at[l], refs_of[job, 5].at[l])
+                jobs[job, l] = Small(*given, *rest, (at.out_att, at.out_mb)[job - ATT].at[l])
+        for job, members, sizes, result in (
+            (ATT_COLUMNS, ((QKV, QKV + 1, QKV + 2), (PROJ,)), (3 * width, proj_ref.shape[1]), at.out_attcols),
+            (MB_COLUMNS, ((INV,), (POINT,)), (expanded, expanded), at.out_mbcols),
+        ):
+            jobs[job, l] = Columns(
                 place, [[jobs[piece, l] for piece in pieces] for pieces in members], [n // n_dp for n in sizes],
-                red_send, red_recv, KINDS * JOBS * layers + 2 * l + i, at[f"{name}_outgoing"], at[f"{name}_landed"].at[l],
-                whole, at[f"out_{name}"].at[l],
+                red_send, red_recv, KINDS * JOBS * layers + 2 * l + job - ATT_COLUMNS, refs_of[job, 0],
+                refs_of[job, 1].at[l], whole, result.at[l],
             )
 
     perm[...] = split_matrix(width)
@@ -698,7 +747,7 @@
         jobs[name, l].stage[row // SUB, row % SUB : row % SUB + 1, at] = value
 
     def expand_row(l, j, tap, value):
-        jobs["mb", l].stage[j // wide * 2 + tap // SUB, tap % SUB : tap % SUB + 1, lanes(j % wide)] = value
+        jobs[MB, l].stage[j // wide * 2 + tap // SUB, tap % SUB : tap % SUB + 1, lanes(j % wide)] = value
 
     def matrix(name, l, left, right, columns):
         own = jobs[name, l].own
@@ -710,8 +759,8 @@
 
     def attention_backward(l, s, grad_branch, pause):
         gmix[...] = mm(grad_branch, proj_ref[l], NT).astype(BF).astype(F32)
-        matrix("proj", l, grad_t[...], lambda cut: mixo[l, :, cut].astype(BF), mixo.shape[2])
-        pause("t0", l)
+        matrix(PROJ, l, grad_t[...], lambda cut: mixo[l, :, cut].astype(BF), mixo.shape[2])
+        pause(T_START, s)
 
         def units(first):
             places = [(first + k, start, size) for k in range(UNIT_STEP) for start, size in BLOCKS]
@@ -760,7 +809,7 @@
                     dvals[start : start + size, lanes(u + part * UNITS)] = grad
 
         groups(UNITS, UNIT_STEP, units)
-        pause("t2", l)
+        pause(T_UNITS, s)
 
         def chunks(c):
             keep = rmask[...]
@@ -780,28 +829,24 @@
                 grads_of.append((direct[part] + back * keep).astype(BF))
             for at, block, taps, joined_grad in zip(columns, blocks, taps_of, grads_of):
                 block = block[0:32] + block[32:64] + block[64:96] + block[96:128]
-                jobs["att", l].stage[4:8, :, at] = block.reshape(4, SUB, LANE)
+                jobs[ATT, l].stage[4:8, :, at] = block.reshape(4, SUB, LANE)
                 for tap, row in enumerate(taps):
-                    small_row("att", l, tap, row, at)
+                    small_row(ATT, l, tap, row, at)
                 mid[:, at] = joined_grad
             natural = mm(jnp.concatenate(grads_of, axis=1), perm[...], NT).astype(BF)
-            matrix(f"qkv{c}", l, hid_t[s], lambda cut: natural, width)
-            pause(f"c{c}", l)
+            matrix(QKV + c, l, hid_t[s], lambda cut: natural, width)
+            pause(T_CHUNKS + c, s)
 
         groups(wide, 1, chunks, True)
-        jobs["att", l].start()
-        pause("t5", l)
+        jobs[ATT, l].start()
         grad_hidden = mm(mid[:, : 3 * width], wp[l], NT)
 
-        def gradients():
-            pass
-
-        return grad_hidden, gradients
+        return grad_hidden
 
     def expand_backward(l, s, grad_branch, pause):
         gact[:, 0:expanded] = mm(grad_branch, point_ref[l], NT).astype(BF).astype(F32)
-        matrix("point", l, grad_t[...], lambda cut: act[l, :, cut], expanded)
-        pause("m0", l)
+        matrix(POINT, l, grad_t[...], lambda cut: act[l, :, cut], expanded)
+        pause(M_START, s)
 
         def chunk(j):
             at = lanes(j)
@@ -817,19 +862,14 @@
             expand_row(l, j, 10, column_sum(grad_pre.astype(F32)))
 
         loop(expanded // LANE, EXPAND_STEP, chunk)
-        jobs["mb", l].start()
-        pause("m2", l)
-        grad_hidden = mm(mid[...], inv_ref[l], NT)
-
-        def gradients():
-            matrix("inv", l, hid_t[s], lambda cut: mid[:, cut], expanded)
-
-        return grad_hidden, gradients
-
-    def pause(moment, l):
-        for step in PLAN.get((moment, l), ()):
-            name, number, method = step.split(".")
-            getattr(jobs[name, int(number)], method)()
+        matrix(INV, l, hid_t[s], lambda cut: mid[:, cut], expanded)
+        jobs[MB, l].start()
+        pause(M_CHUNKS, s)
+        return mm(mid[...], inv_ref[l], NT)
+
+    def pause(moment, s):
+        for job, l, step in PLAN.get((moment, s), ()):
+            jobs[job, l].do(step)
 
     for s in range(stages - 1, -1, -1):
         l = s // 2
@@ -838,32 +878,31 @@
             cross, total = first_cross, first_total
         else:
             cross, total = exchange_finish(stages + s, 2)
-        pause("begin", s)
+        pause(BEGIN, s)
         if s % 2 == 0:
-            small_row("att", l, 25, local_cross, slice(0, width))
-            small_row("att", l, 25, local_sum, slice(width, 2 * width))
+            small_row(ATT, l, 25, local_cross, slice(0, width))
+            small_row(ATT, l, 25, local_sum, slice(width, 2 * width))
         else:
-            small_row("mb", l, 11, local_cross, slice(0, width))
-            small_row("mb", l, 16 + 11, local_sum, slice(0, width))
+            small_row(MB, l, 11, local_cross, slice(0, width))
+            small_row(MB, l, 16 + 11, local_sum, slice(0, width))
         grad_branch = (stats[s : s + 1, :] * gains[s : s + 1]) * (gnow[...] - total - normed[s] * cross)
         grad_branch = jnp.concatenate(
             [grad_branch[:, lanes(j)] * keep for j in range(wide)], axis=1
         ).astype(BF)
         grad_t[...] = mm(rowperm[...], grad_branch, NT).astype(BF)
         back = attention_backward if s % 2 == 0 else expand_backward
-        grad_hidden, gradients = back(l, s, grad_branch, pause)
+        grad_hidden = back(l, s, grad_branch, pause)
         after = (gnow[...] + grad_hidden).astype(BF).astype(F32)
         gnow[...] = after
         if s > 0:
             local_cross, local_sum = column_sum(after * normed[s - 1]), column_sum(after)
             exchange_start(stages + s - 1, [local_cross, local_sum])
-        pause("sent", s)
-        gradients()
-        pause("done", s)
+        pause(SENT, s)
+        pause(DONE, s)
         if s == last:
-            at["out_x"][...] = mm(spread, hid[stages], TN).astype(BF)
-
-    at["out_g"][...] = mm(spread, gnow[...].astype(BF), TN).astype(BF)
+            at.out_x[...] = mm(spread, hid[stages], TN).astype(BF)
+
+    at.out_g[...] = mm(spread, gnow[...].astype(BF), TN).astype(BF)
     for job in jobs.values():
         if isinstance(job, Reduction):
             job.drain()
@@ -940,75 +979,73 @@
     rows = width // 2 // n_pipe
     vmem = pl.BlockSpec(memory_space=pltpu.VMEM)
     hbm = pl.BlockSpec(memory_space=pl.ANY)
-    columns = {"qkv0": width, "qkv1": width, "qkv2": width, "proj": mixed_width, "inv": expanded, "point": expanded}
-    small_columns = {"att": joined_width, "mb": width}
-    outs = {
-        "out_x": jax.ShapeDtypeStruct((tokens, width), BF),
-        "out_g": jax.ShapeDtypeStruct((tokens, width), BF),
-    }
-    scratch = {
-        "proj": pltpu.VMEM(att_proj.shape, BF),
-        "inv": pltpu.VMEM(mb_inv.shape, BF),
-        "point": pltpu.VMEM(mb_point.shape, BF),
-        "perm": pltpu.VMEM((width, width), BF),
-        "rowperm": pltpu.VMEM((width, width), BF),
-        "wp": pltpu.VMEM((layers, width, joined_width), BF),
-        "blocks_bd": pltpu.VMEM((layers, joined_width // LANE, LANE, LANE), BF),
-        "dwp": pltpu.VMEM((layers, 32, joined_width), F32),
-        "mdwp": pltpu.VMEM((layers, 16, expanded), F32),
-        "rmask": pltpu.VMEM((ROWS, LANE), F32),
-        "smask": pltpu.VMEM((48, 192), F32),
-        "diag": pltpu.VMEM((LANE, 2 * LANE), F32),
-        "diag_t": pltpu.VMEM((2 * LANE, LANE), F32),
-        "hid": pltpu.VMEM((stages + 1, ROWS, width), BF),
-        "hid_t": pltpu.VMEM((stages, width, ROWS), BF),
-        "grad_t": pltpu.VMEM((width, ROWS), BF),
-        "normed": pltpu.VMEM((stages, ROWS, width), F32),
-        "mixo": pltpu.VMEM((layers, ROWS, mixed_width), F32),
-        "rden": pltpu.VMEM((layers, ROWS, mixed_width), F32),
-        "tvals": pltpu.VMEM((layers, ROWS, 3 * mixed_width), F32),
-        "joined": pltpu.VMEM((layers, ROWS, joined_width), F32),
-        "s0": pltpu.VMEM((layers, ROWS, joined_width), BF),
-        "dvals": pltpu.VMEM((ROWS, 3 * mixed_width), F32),
-        "gmix": pltpu.VMEM((ROWS, mixed_width), F32),
-        "pre_u": pltpu.VMEM((layers, ROWS, expanded), F32),
-        "pre_d": pltpu.VMEM((layers, ROWS, expanded), BF),
-        "act": pltpu.VMEM((layers, ROWS, expanded), BF),
-        "act_d": pltpu.VMEM((layers, ROWS, expanded), BF),
-        "mid": pltpu.VMEM((ROWS, expanded), BF),
-        "branch": pltpu.VMEM((ROWS, width), F32),
-        "gnow": pltpu.VMEM((ROWS, width), F32),
-        "stats": pltpu.VMEM((8, width), F32),
-        "exbuf": pltpu.VMEM((2 * stages - 1, n_dp, 2 * SUB, LANE), F32),
-        "whole": pltpu.VMEM((rows, 2 * expanded), F32),
-        "send_sem": pltpu.SemaphoreType.DMA((2 * stages - 1,)),
-        "recv_sem": pltpu.SemaphoreType.DMA((2 * stages - 1,)),
-        "load_sem": pltpu.SemaphoreType.DMA((4, layers)),
-        "red_send": pltpu.SemaphoreType.DMA((KINDS * JOBS * layers + 2 * layers,)),
-        "red_recv": pltpu.SemaphoreType.DMA((KINDS * JOBS * layers + 2 * layers,)),
-    }
-    for name in MATRICES:
-        n = columns[name]
-        scratch[f"{name}_own"] = pltpu.VMEM((layers, 2, n_pipe, rows, n), BF)
-        scratch[f"{name}_pair"] = pltpu.VMEM((layers, n_pipe, rows, n), BF)
-        scratch[f"{name}_first"] = pltpu.VMEM((layers, 2, rows, n), BF)
-        scratch[f"{name}_second"] = pltpu.VMEM((layers, rows, n), BF)
+    columns = (width, width, width, mixed_width, expanded, expanded, joined_width, width)
     shares = tuple(n // n_dp for n in (joined_width, mixed_width, expanded, expanded))
-    for name, share in (("attcols", padded(shares[0] + shares[1])), ("mbcols", padded(shares[2] + shares[3]))):
-        outs[f"out_{name}"] = jax.ShapeDtypeStruct((layers, 2 * rows, share), F32)
-        scratch[f"{name}_outgoing"] = pltpu.VMEM((n_dp, rows, share), BF)
-        scratch[f"{name}_landed"] = pltpu.VMEM((layers, n_dp, rows, share), BF)
-    for name in SMALLS:
-        n = small_columns[name]
-        outs[f"out_{name}"] = jax.ShapeDtypeStruct((layers, 8 * SUB, n), F32)
-        half, rows_in, kind = (padded(n // 2), 2 * SUB, BF) if name == "att" else (n, SUB, F32)
-        scratch[f"{name}_stage"] = pltpu.VMEM((8, SUB, n), F32)
-        scratch[f"{name}_own"] = pltpu.VMEM((layers, 2, n_pipe, rows_in, half), kind)
-        scratch[f"{name}_pair"] = pltpu.VMEM((layers, n_pipe, rows_in, half), kind)
-        scratch[f"{name}_first"] = pltpu.VMEM((layers, 2, rows_in, half), kind)
-        scratch[f"{name}_second"] = pltpu.VMEM((layers, rows_in, half), kind)
-        scratch[f"{name}_along"] = pltpu.VMEM((layers, n_dp // 2, rows_in, half), kind)
-        scratch[f"{name}_everywhere"] = pltpu.VMEM((layers, 2 * n_pipe, rows_in, half), kind)
+    share_att, share_mb = padded(shares[0] + shares[1]), padded(shares[2] + shares[3])
+    outs = dict(
+        out_x=jax.ShapeDtypeStruct((tokens, width), BF),
+        out_g=jax.ShapeDtypeStruct((tokens, width), BF),
+        out_attcols=jax.ShapeDtypeStruct((layers, 2 * rows, share_att), F32),
+        out_mbcols=jax.ShapeDtypeStruct((layers, 2 * rows, share_mb), F32),
+        out_att=jax.ShapeDtypeStruct((layers, 8 * SUB, joined_width), F32),
+        out_mb=jax.ShapeDtypeStruct((layers, 8 * SUB, width), F32),
+    )
+    scratch = dict(
+        proj=pltpu.VMEM(att_proj.shape, BF),
+        inv=pltpu.VMEM(mb_inv.shape, BF),
+        point=pltpu.VMEM(mb_point.shape, BF),
+        perm=pltpu.VMEM((width, width), BF),
+        rowperm=pltpu.VMEM((width, width), BF),
+        wp=pltpu.VMEM((layers, width, joined_width), BF),
+        blocks_bd=pltpu.VMEM((layers, joined_width // LANE, LANE, LANE), BF),
+        dwp=pltpu.VMEM((layers, 32, joined_width), F32),
+        mdwp=pltpu.VMEM((layers, 16, expanded), F32),
+        rmask=pltpu.VMEM((ROWS, LANE), F32),
+        smask=pltpu.VMEM((48, 192), F32),
+        diag=pltpu.VMEM((LANE, 2 * LANE), F32),
+        diag_t=pltpu.VMEM((2 * LANE, LANE), F32),
+        hid=pltpu.VMEM((stages + 1, ROWS, width), BF),
+        hid_t=pltpu.VMEM((stages, width, ROWS), BF),
+        grad_t=pltpu.VMEM((width, ROWS), BF),
+        normed=pltpu.VMEM((stages, ROWS, width), F32),
+        mixo=pltpu.VMEM((layers, ROWS, mixed_width), F32),
+        rden=pltpu.VMEM((layers, ROWS, mixed_width), F32),
+        tvals=pltpu.VMEM((layers, ROWS, 3 * mixed_width), F32),
+        joined=pltpu.VMEM((layers, ROWS, joined_width), F32),
+        s0=pltpu.VMEM((layers, ROWS, joined_width), BF),
+        dvals=pltpu.VMEM((ROWS, 3 * mixed_width), F32),
+        gmix=pltpu.VMEM((ROWS, mixed_width), F32),
+        pre_u=pltpu.VMEM((layers, ROWS, expanded), F32),
+        pre_d=pltpu.VMEM((layers, ROWS, expanded), BF),
+        act=pltpu.VMEM((layers, ROWS, expanded), BF),
+        act_d=pltpu.VMEM((layers, ROWS, expanded), BF),
+        mid=pltpu.VMEM((ROWS, expanded), BF),
+        branch=pltpu.VMEM((ROWS, width), F32),
+        gnow=pltpu.VMEM((ROWS, width), F32),
+        stats=pltpu.VMEM((8, width), F32),
+        exbuf=pltpu.VMEM((2 * stages - 1, n_dp, 2 * SUB, LANE), F32),
+        whole=pltpu.VMEM((rows, 2 * expanded), F32),
+        send_sem=pltpu.SemaphoreType.DMA((2 * stages - 1,)),
+        recv_sem=pltpu.SemaphoreType.DMA((2 * stages - 1,)),
+        load_sem=pltpu.SemaphoreType.DMA((4, layers)),
+        red_send=pltpu.SemaphoreType.DMA((KINDS * JOBS * layers + 2 * layers,)),
+        red_recv=pltpu.SemaphoreType.DMA((KINDS * JOBS * layers + 2 * layers,)),
+    )
+    for job, n in enumerate(columns):
+        high, kind = rows, BF
+        if job == ATT:
+            n, high = padded(n // 2), 2 * SUB
+        elif job == MB:
+            high, kind = SUB, F32
+        shapes = [(2, n_pipe), (n_pipe,), (2,), ()]
+        if job >= MATRICES:
+            shapes += [(n_dp // 2,), (2 * n_pipe,)]
+            scratch[job, 6] = pltpu.VMEM((8, SUB, columns[job]), F32)
+        for i, shape in enumerate(shapes):
+            scratch[job, i] = pltpu.VMEM((layers, *shape, high, n), kind)
+    for job, share in ((ATT_COLUMNS, share_att), (MB_COLUMNS, share_mb)):
+        scratch[job, 0] = pltpu.VMEM((n_dp, rows, share), BF)
+        scratch[job, 1] = pltpu.VMEM((layers, n_dp, rows, share), BF)
     results = pl.pallas_call(
         functools.partial(kernel, n_dp, n_pipe, 13, tuple(outs) + tuple(scratch)),
         out_shape=tuple(outs.values()),

time: 106 us -> 105 us (level)
  no operation moved by 1% of the time
where the time goes in v4:
time: 105 us; the launch traced here: 104 us
  Pallas kernels  97.7 us (93%)
  local copies, waits for them, and re-layouts  5.8 us (6%)
    pallas_call x1, Pallas kernels, body(): pl.pallas_call(functools.partial(kernel, n_dp, n_pipe, 13, tuple(outs) +...  94.7 us
    unnamed x2, local copies, waits for them, and re-layouts  4.38 us
    pallas_call x1, Pallas kernels, body(): pl.pallas_call(functools.partial(arrange, layers, width // LANE, shares),...  2.96 us

profile of v4, /device:TPU:0, one launch (start us, length us, event | category | flops | bytes accessed | tf_op | source)
XLA Modules:
  0.0 104.1 jit_solution(16739140069852355988)
XLA Ops:
  0.6 2.9 %copy.28.refs_4_ = bf16[2,36,32,32]{3,2,1,0:T(8,128)(2,1)} copy(bf16[2,36,32,32]{1,3,2,0:T(8,128)(2,1)} %param.17) | data formatting | bytes 294912 | tf_op args[4]
  3.5 94.7 %shard_map.228 = (bf16[134,384]{1,0:T(8,128)(2,1)}, bf16[134,384]{1,0:T(8,128)(2,1)}, f32[2,96,256]{2,1,0:T(8,128)}, f32[2,96,384]{2,1,0:T(8,128)}, f32[2,64,1152]{2,1,0:T(8,128)}, /*index=5*/f32[2,64,384]{2,1,0:T(8,128)}) custom-call(bf16[134,384]{1,0:T(8,128)(2,1)} %bitcast.12, bf16[134,384]{1,0:T(8,128)(2,1)} %bitcast.13, bf16[2,384,1152]{2,1,0:T(8,128)(2,1)} %refs_2_.1, ...), custom_call_target="tpu_custom_call" | custom-call | tf_op jit(solution)/shard_map/pallas_call | solution.py:1049
  98.3 3.0 %shard_map.229 = (bf16[134,384]{1,0:T(8,128)(2,1)}, bf16[134,384]{1,0:T(8,128)(2,1)}, f32[2,144,96]{2,1,0:T(8,128)}, f32[2,96,96]{2,1,0:T(8,128)}, f32[2,96,192]...) custom-call(bf16[134,384]{1,0:T(8,128)(2,1)} %get-tuple-element.32.x, ...), custom_call_target="tpu_custom_call" | custom-call | tf_op jit(solution)/shard_map/pallas_call | solution.py:1074
  101.2 1.4 %reshape.45 = f32[2,32,36,32]{3,2,1,0:T(8,128)S(1)} reshape(f32[2,32,1152]{2,1,0:T(8,128)} %get-tuple-element.42) | data formatting | bytes 589824 | tf_op jit(solution)/shard_map/reshape | solution.py:1101
  102.7 1.5 %copy.29 = f32[2,36,32,32]{1,3,2,0:T(8,128)} copy(f32[2,36,32,32]{3,1,2,0:T(8,128)S(1)} %bitcast.10) | data formatting | bytes 589824

commit v5 on v4

--- a/solution.py
+++ b/solution.py
@@ -456,18 +456,18 @@
     (M_START, 1): ((QKV + 1, 1, 2), (QKV + 2, 1, 2), (ATT, 1, 2),),
     (M_CHUNKS, 1): ((POINT, 0, 1), (MB, 1, 4),),
     (SENT, 1): ((ATT, 1, 3), (ATT_COLUMNS, 1, SEND),),
-    (DONE, 1): ((MB, 0, 1), (INV, 0, 1), (MB, 1, FINISH),),
-    (BEGIN, 0): ((MB_COLUMNS, 1, FINISH),),
+    (DONE, 1): ((MB, 0, 1), (INV, 0, 1),),
     (T_START, 0): ((POINT, 0, 2), (MB, 0, 2), (ATT, 1, 4),),
     (T_UNITS, 0): ((PROJ, 0, 1),),
     (T_CHUNKS, 0): ((MB, 0, 3),),
     (T_CHUNKS + 1, 0): ((INV, 0, 2), (QKV, 0, 1),),
-    (T_CHUNKS + 2, 0): ((QKV + 1, 0, 1), (ATT_COLUMNS, 1, FINISH), (ATT, 1, FINISH),),
+    (T_CHUNKS + 2, 0): ((QKV + 1, 0, 1), (MB_COLUMNS, 1, FINISH),),
     (SENT, 0): (
         (QKV + 2, 0, 1), (ATT, 0, 1), (PROJ, 0, 2), (MB, 0, 4), (QKV, 0, 2), (MB_COLUMNS, 0, SEND),
     ),
     (DONE, 0): (
-        (ATT, 0, 2), (QKV + 1, 0, 2), (QKV + 2, 0, 2), (ATT, 0, 3), (ATT_COLUMNS, 0, SEND), (ATT, 0, 4),
+        (ATT, 0, 2), (QKV + 1, 0, 2), (QKV + 2, 0, 2), (ATT_COLUMNS, 1, FINISH), (MB, 1, FINISH), (ATT, 1, FINISH),
+        (ATT, 0, 3), (ATT_COLUMNS, 0, SEND), (ATT, 0, 4),
         (MB, 0, FINISH), (MB_COLUMNS, 0, FINISH),
         (ATT_COLUMNS, 0, FINISH), (ATT, 0, FINISH),
     ),

time: 105 us -> 105 us (level)
  no operation moved by 1% of the time
where the time goes in v5:
time: 105 us; the launch traced here: 104 us
  Pallas kernels  98 us (93%)
  local copies, waits for them, and re-layouts  5.8 us (6%)
    pallas_call x1, Pallas kernels, body(): pl.pallas_call(functools.partial(kernel, n_dp, n_pipe, 13, tuple(outs) +...  95 us
    unnamed x2, local copies, waits for them, and re-layouts  4.38 us
    pallas_call x1, Pallas kernels, body(): pl.pallas_call(functools.partial(arrange, layers, width // LANE, shares),...  2.96 us

profile of v5, /device:TPU:0, one launch (start us, length us, event | category | flops | bytes accessed | tf_op | source)
XLA Modules:
  0.0 104.5 jit_solution(15802592708166777044)
XLA Ops:
  0.6 2.9 %copy.28.refs_4_ = bf16[2,36,32,32]{3,2,1,0:T(8,128)(2,1)} copy(bf16[2,36,32,32]{1,3,2,0:T(8,128)(2,1)} %param.17) | data formatting | bytes 294912 | tf_op args[4]
  3.5 95.0 %shard_map.228 = (bf16[134,384]{1,0:T(8,128)(2,1)}, bf16[134,384]{1,0:T(8,128)(2,1)}, f32[2,96,256]{2,1,0:T(8,128)}, f32[2,96,384]{2,1,0:T(8,128)}, f32[2,64,1152]{2,1,0:T(8,128)}, /*index=5*/f32[2,64,384]{2,1,0:T(8,128)}) custom-call(bf16[134,384]{1,0:T(8,128)(2,1)} %bitcast.12, bf16[134,384]{1,0:T(8,128)(2,1)} %bitcast.13, bf16[2,384,1152]{2,1,0:T(8,128)(2,1)} %refs_2_.1, ...), custom_call_target="tpu_custom_call" | custom-call | tf_op jit(solution)/shard_map/pallas_call | solution.py:1049
  98.6 3.0 %shard_map.229 = (bf16[134,384]{1,0:T(8,128)(2,1)}, bf16[134,384]{1,0:T(8,128)(2,1)}, f32[2,144,96]{2,1,0:T(8,128)}, f32[2,96,96]{2,1,0:T(8,128)}, f32[2,96,192]...) custom-call(bf16[134,384]{1,0:T(8,128)(2,1)} %get-tuple-element.32.x, ...), custom_call_target="tpu_custom_call" | custom-call | tf_op jit(solution)/shard_map/pallas_call | solution.py:1074
  101.5 1.4 %reshape.45 = f32[2,32,36,32]{3,2,1,0:T(8,128)S(1)} reshape(f32[2,32,1152]{2,1,0:T(8,128)} %get-tuple-element.42) | data formatting | bytes 589824 | tf_op jit(solution)/shard_map/reshape | solution.py:1101
  103.0 1.5 %copy.29 = f32[2,36,32,32]{1,3,2,0:T(8,128)} copy(f32[2,36,32,32]{3,1,2,0:T(8,128)S(1)} %bitcast.10) | data formatting | bytes 589824
